TPU v7x, 32 devices: a whole 2x2x4 slice. The times are simulated.
32 devices in a mesh: dp: 2 (over x), ctx: 4 (over y, core), mp: 4 (over z).
Axes of the slice: x: 2, y: 2, z: 4, core: 2. Of those that a mesh axis runs over, the one named last changes fastest.
Arguments:
- hidden_in: bfloat16 [2, 1024, 2560], P('dp', 'ctx'), may hold values from -6 to 6
- cotangent: bfloat16 [2, 1024, 2560], P('dp', 'ctx'), may hold values from -6 to 6
- lengths: int32 [2], P('dp'), may hold values from 1024 to 1024, as said below
- norm_attn: bfloat16 [2560], P(('dp', 'ctx')), may hold values from 0.099609375 to 1.8984375
- w_query: bfloat16 [2560, 2560], P(('dp', 'ctx'), 'mp'), may hold values from -0.15625 to 0.15625
- w_key: bfloat16 [2560, 640], P(('dp', 'ctx'), 'mp'), may hold values from -0.125 to 0.125
- w_value: bfloat16 [2560, 640], P(('dp', 'ctx'), 'mp'), may hold values from -0.125 to 0.125
- w_output: bfloat16 [2560, 2560], P('mp', ('dp', 'ctx')), may hold values from -0.5 to 0.5
- norm_mlp: bfloat16 [2560], P(('dp', 'ctx')), may hold values from 0.099609375 to 1.8984375
- w_gate: bfloat16 [2560, 7168], P(('dp', 'ctx'), 'mp'), may hold values from -0.125 to 0.125
- w_up: bfloat16 [2560, 7168], P(('dp', 'ctx'), 'mp'), may hold values from -0.125 to 0.125
- w_down: bfloat16 [7168, 2560], P('mp', ('dp', 'ctx')), may hold values from -0.0625 to 0.0625
Outputs:
- layer_out: bfloat16 [2, 1024, 2560], P('dp', 'ctx')
- input_grad: bfloat16 [2, 1024, 2560], P('dp', 'ctx')
- grad_norm_attn: float32 [2560], P(('dp', 'ctx'))
- grad_query: float32 [2560, 2560], P(('dp', 'ctx'), 'mp')
- grad_key: float32 [2560, 640], P(('dp', 'ctx'), 'mp')
- grad_value: float32 [2560, 640], P(('dp', 'ctx'), 'mp')
- grad_output: float32 [2560, 2560], P('mp', ('dp', 'ctx'))
- grad_norm_mlp: float32 [2560], P(('dp', 'ctx'))
- grad_gate: float32 [2560, 7168], P(('dp', 'ctx'), 'mp')
- grad_up: float32 [2560, 7168], P(('dp', 'ctx'), 'mp')
- grad_down: float32 [7168, 2560], P('mp', ('dp', 'ctx'))
Inputs may be any that keep to these rules, and one draw needn't show every extreme that they name: `lengths`: among the 1 sequence of each index of dp (sequences s with the same s) one is longer than 768; at least one sequence in all has length 1024.
All inputs are finite; a program needn't handle non-finite values.
Results may differ from a plain program's by a relative error of at most 0.017.
Values may be sent and summed in bfloat16 or wider, within the bound.
A program may use at most 256 MiB of HBM per device.

v0:
```python
import jax
import jax.numpy as jnp
from jax import lax
from jax.sharding import PartitionSpec as P

HEAD = 80


EPS = 1e-05
THETA = 1000000.0
NEG = -1e30


def rope_tables(places, head_size):
    half = head_size // 2
    freq = THETA ** (-(jnp.arange(half, dtype=jnp.float32) * 2.0 / head_size))
    angle = places[:, None] * freq[None, :]
    return (jnp.cos(angle), jnp.sin(angle))


def rotate(tensor, cosine, sine_table):
    half = tensor.shape[-1] // 2
    first_half = tensor[..., :half]
    second_half = tensor[..., half:]
    cos_b = cosine[:, None, :]
    sin_b = sine_table[:, None, :]
    return jnp.concatenate(
        [first_half * cos_b - second_half * sin_b, second_half * cos_b + first_half * sin_b],
        axis=-1,
    )


def rotate_back(tensor, cosine, sine_table):
    half = tensor.shape[-1] // 2
    first_half = tensor[..., :half]
    second_half = tensor[..., half:]
    cos_b = cosine[:, None, :]
    sin_b = sine_table[:, None, :]
    return jnp.concatenate(
        [first_half * cos_b + second_half * sin_b, second_half * cos_b - first_half * sin_b],
        axis=-1,
    )


def normed(tensor, gain_row):
    return tensor * lax.rsqrt(jnp.mean(tensor * tensor, axis=-1, keepdims=True) + EPS) * gain_row


def norm_back(tensor, gain_row, grad_normed):
    scale_row = lax.rsqrt(jnp.mean(tensor * tensor, axis=-1, keepdims=True) + EPS)
    grad_scaled = grad_normed * gain_row
    grad_tensor = scale_row * grad_scaled - tensor * scale_row**3 * jnp.mean(
        grad_scaled * tensor, axis=-1, keepdims=True
    )
    grad_gain = jnp.sum(grad_normed * tensor * scale_row, axis=0)
    return (grad_tensor, grad_gain)


def masked_scores(query_seq, key_seq, length, places, kv_heads, group_size):
    query_grp = query_seq.reshape(query_seq.shape[0], kv_heads, group_size, HEAD)
    key_grp = key_seq.reshape(key_seq.shape[0], kv_heads, HEAD)
    raw_scores = jnp.einsum(
        "bkgh,tkh->kgbt", query_grp, key_grp, preferred_element_type=jnp.float32
    ) * HEAD ** (-0.5)
    key_places = jnp.arange(key_grp.shape[0], dtype=jnp.int32)
    allowed = (key_places[None, :] <= places[:, None]) & (key_places[None, :] < length)
    return jnp.where(allowed[None, None], raw_scores, NEG)


def on_device(
    hidden_in,
    cotangent,
    lengths,
    norm_attn,
    w_query,
    w_key,
    w_value,
    w_output,
    norm_mlp,
    w_gate,
    w_up,
    w_down,
):
    seq_count, slot_count, width_all = hidden_in.shape
    tok_rows = seq_count * slot_count
    attn_set = (
        lax.all_gather(w_query, ("dp", "ctx"), axis=0, tiled=True),
        lax.all_gather(w_key, ("dp", "ctx"), axis=0, tiled=True),
        lax.all_gather(w_value, ("dp", "ctx"), axis=0, tiled=True),
        lax.all_gather(w_output, ("dp", "ctx"), axis=1, tiled=True),
        lax.all_gather(norm_attn, ("dp", "ctx"), axis=0, tiled=True),
    )
    query_w, key_w, value_w, output_w, gain_attn = attn_set
    q_heads = query_w.shape[1] // HEAD
    kv_heads = key_w.shape[1] // HEAD
    group_size = q_heads // kv_heads
    first_slot = lax.axis_index("ctx") * slot_count
    places = first_slot + jnp.arange(slot_count, dtype=jnp.int32)
    valid_mask = (places[None, :] < lengths[:, None]).astype(jnp.float32).reshape(tok_rows, 1)
    cosine, sine_table = rope_tables(places.astype(jnp.float32), HEAD)
    inputs = hidden_in.reshape(tok_rows, width_all).astype(jnp.float32)
    gain_one = gain_attn.astype(jnp.float32)
    normed_one = normed(inputs, gain_one).astype(jnp.bfloat16)
    query_proj = jnp.dot(normed_one, query_w, preferred_element_type=jnp.float32).reshape(
        seq_count, slot_count, q_heads, HEAD
    )
    key_proj = jnp.dot(normed_one, key_w, preferred_element_type=jnp.float32).reshape(
        seq_count, slot_count, kv_heads, HEAD
    )
    value_low = (
        jnp.dot(normed_one, value_w, preferred_element_type=jnp.float32)
        .astype(jnp.bfloat16)
        .reshape(seq_count, slot_count, kv_heads * HEAD)
    )
    query_low = rotate(query_proj, cosine, sine_table).astype(jnp.bfloat16)
    key_low = (
        rotate(key_proj, cosine, sine_table)
        .astype(jnp.bfloat16)
        .reshape(seq_count, slot_count, kv_heads * HEAD)
    )
    key_all, value_all = (
        lax.all_gather(key_low, "ctx", axis=1, tiled=True),
        lax.all_gather(value_low, "ctx", axis=1, tiled=True),
    )

    def attend(members):
        query_seq, key_seq, value_seq, length = members
        scores = masked_scores(query_seq, key_seq, length, places, kv_heads, group_size)
        row_max = jnp.max(scores, axis=-1, keepdims=True)
        exponent = jnp.exp(scores - row_max)
        total = jnp.sum(exponent, axis=-1, keepdims=True)
        attention = (exponent / total).astype(jnp.bfloat16)
        value_grp = value_seq.reshape(value_seq.shape[0], kv_heads, HEAD)
        mixed_heads = jnp.einsum(
            "kgbt,tkh->bkgh", attention, value_grp, preferred_element_type=jnp.float32
        )
        return (mixed_heads.reshape(slot_count, q_heads * HEAD), (row_max + jnp.log(total))[..., 0])

    mixed_all, log_total = lax.map(attend, (query_low, key_all, value_all, lengths))
    attn_low = mixed_all.reshape(tok_rows, q_heads * HEAD).astype(jnp.bfloat16)
    branch = lax.psum(jnp.dot(attn_low, output_w, preferred_element_type=jnp.float32), "mp")
    middle = inputs + branch
    mlp_set = (
        lax.all_gather(w_gate, ("dp", "ctx"), axis=0, tiled=True),
        lax.all_gather(w_up, ("dp", "ctx"), axis=0, tiled=True),
        lax.all_gather(w_down, ("dp", "ctx"), axis=1, tiled=True),
        lax.all_gather(norm_mlp, ("dp", "ctx"), axis=0, tiled=True),
    )
    gate_w, up_w, down_w, gain_mlp = mlp_set
    gain_two = gain_mlp.astype(jnp.float32)
    normed_two = normed(middle, gain_two).astype(jnp.bfloat16)
    gate_proj = jnp.dot(normed_two, gate_w, preferred_element_type=jnp.float32)
    up_proj = jnp.dot(normed_two, up_w, preferred_element_type=jnp.float32)
    hidden = (jax.nn.silu(gate_proj) * up_proj).astype(jnp.bfloat16)
    mlp_out = lax.psum(
        jnp.dot(hidden, down_w, preferred_element_type=jnp.float32).astype(jnp.bfloat16), "mp"
    ).astype(jnp.float32)
    layer_out = (
        (valid_mask * (middle + mlp_out))
        .astype(jnp.bfloat16)
        .reshape(seq_count, slot_count, width_all)
    )
    grad_out = valid_mask * cotangent.reshape(tok_rows, width_all).astype(jnp.float32)
    grad_mlp = grad_out.astype(jnp.bfloat16)
    gate_back, up_back, down_back, gain_mlp_back = (
        lax.all_gather(w_gate, ("dp", "ctx"), axis=0, tiled=True),
        lax.all_gather(w_up, ("dp", "ctx"), axis=0, tiled=True),
        lax.all_gather(w_down, ("dp", "ctx"), axis=1, tiled=True),
        lax.all_gather(norm_mlp, ("dp", "ctx"), axis=0, tiled=True),
    )
    grad_hidden = jnp.einsum("tm,fm->tf", grad_mlp, down_back, preferred_element_type=jnp.float32)
    grad_down = jnp.einsum("tf,tm->fm", hidden, grad_mlp, preferred_element_type=jnp.float32)
    sigmoid_gate = jax.nn.sigmoid(gate_proj)
    grad_gate_low = (
        grad_hidden * up_proj * sigmoid_gate * (1.0 + gate_proj * (1.0 - sigmoid_gate))
    ).astype(jnp.bfloat16)
    grad_up_low = (grad_hidden * gate_proj * sigmoid_gate).astype(jnp.bfloat16)
    grad_gate = jnp.einsum(
        "td,tf->df", normed_two, grad_gate_low, preferred_element_type=jnp.float32
    )
    grad_up = jnp.einsum("td,tf->df", normed_two, grad_up_low, preferred_element_type=jnp.float32)
    partial_two = jnp.einsum(
        "tf,df->td", grad_gate_low, gate_back, preferred_element_type=jnp.float32
    ) + jnp.einsum("tf,df->td", grad_up_low, up_back, preferred_element_type=jnp.float32)
    grad_normed_two = lax.psum(partial_two, "mp")
    grad_middle_norm, grad_gain_two = norm_back(
        middle, gain_mlp_back.astype(jnp.float32), grad_normed_two
    )
    mlp_grads = (
        lax.psum_scatter(grad_gate, ("dp", "ctx"), scatter_dimension=0, tiled=True),
        lax.psum_scatter(grad_up, ("dp", "ctx"), scatter_dimension=0, tiled=True),
        lax.psum_scatter(grad_down, ("dp", "ctx"), scatter_dimension=1, tiled=True),
        lax.psum_scatter(grad_gain_two, ("dp", "ctx"), scatter_dimension=0, tiled=True),
    )
    grad_middle = grad_out + grad_middle_norm
    grad_branch = grad_middle.astype(jnp.bfloat16)
    query_back, key_back, value_back, output_back, gain_attn_back = (
        lax.all_gather(w_query, ("dp", "ctx"), axis=0, tiled=True),
        lax.all_gather(w_key, ("dp", "ctx"), axis=0, tiled=True),
        lax.all_gather(w_value, ("dp", "ctx"), axis=0, tiled=True),
        lax.all_gather(w_output, ("dp", "ctx"), axis=1, tiled=True),
        lax.all_gather(norm_attn, ("dp", "ctx"), axis=0, tiled=True),
    )
    grad_output = jnp.einsum("tq,td->qd", attn_low, grad_branch, preferred_element_type=jnp.float32)
    grad_attn_low = (
        jnp.einsum("td,qd->tq", grad_branch, output_back, preferred_element_type=jnp.float32)
        .astype(jnp.bfloat16)
        .reshape(seq_count, slot_count, q_heads, HEAD)
    )

    def attend_back(members):
        query_seq, key_seq, value_seq, length, log_seq, grad_seq = members
        scores = masked_scores(query_seq, key_seq, length, places, kv_heads, group_size)
        attention = jnp.exp(scores - log_seq[..., None])
        query_grp = query_seq.reshape(slot_count, kv_heads, group_size, HEAD)
        key_grp = key_seq.reshape(key_seq.shape[0], kv_heads, HEAD)
        value_grp = value_seq.reshape(value_seq.shape[0], kv_heads, HEAD)
        grad_grp = grad_seq.reshape(slot_count, kv_heads, group_size, HEAD)
        grad_attention = jnp.einsum(
            "bkgh,tkh->kgbt", grad_grp, value_grp, preferred_element_type=jnp.float32
        )
        inner = jnp.sum(attention * grad_attention, axis=-1, keepdims=True)
        grad_scores = (attention * (grad_attention - inner)).astype(jnp.bfloat16)
        scale_qk = HEAD ** (-0.5)
        grad_query_seq = (
            jnp.einsum("kgbt,tkh->bkgh", grad_scores, key_grp, preferred_element_type=jnp.float32)
            * scale_qk
        )
        grad_key_seq = (
            jnp.einsum("kgbt,bkgh->tkh", grad_scores, query_grp, preferred_element_type=jnp.float32)
            * scale_qk
        )
        grad_value_seq = jnp.einsum(
            "kgbt,bkgh->tkh",
            attention.astype(jnp.bfloat16),
            grad_grp,
            preferred_element_type=jnp.float32,
        )
        key_rows = key_grp.shape[0]
        return (
            grad_query_seq.reshape(slot_count, q_heads, HEAD),
            grad_key_seq.reshape(key_rows, kv_heads * HEAD),
            grad_value_seq.reshape(key_rows, kv_heads * HEAD),
        )

    grad_query_rot, grad_key_all, grad_value_all = lax.map(
        attend_back, (query_low, key_all, value_all, lengths, log_total, grad_attn_low)
    )
    grad_key_rot, grad_value_rot = (
        lax.psum_scatter(grad_key_all, "ctx", scatter_dimension=1, tiled=True),
        lax.psum_scatter(grad_value_all, "ctx", scatter_dimension=1, tiled=True),
    )
    grad_query_low = (
        rotate_back(grad_query_rot, cosine, sine_table)
        .astype(jnp.bfloat16)
        .reshape(tok_rows, q_heads * HEAD)
    )
    grad_key_low = (
        rotate_back(grad_key_rot.reshape(seq_count, slot_count, kv_heads, HEAD), cosine, sine_table)
        .astype(jnp.bfloat16)
        .reshape(tok_rows, kv_heads * HEAD)
    )
    grad_value_low = grad_value_rot.astype(jnp.bfloat16).reshape(tok_rows, kv_heads * HEAD)
    grad_query = jnp.einsum(
        "td,tq->dq", normed_one, grad_query_low, preferred_element_type=jnp.float32
    )
    grad_key = jnp.einsum("td,tq->dq", normed_one, grad_key_low, preferred_element_type=jnp.float32)
    grad_value = jnp.einsum(
        "td,tq->dq", normed_one, grad_value_low, preferred_element_type=jnp.float32
    )
    partial_one = jnp.einsum(
        "tq,dq->td", grad_query_low, query_back, preferred_element_type=jnp.float32
    )
    partial_one = partial_one + jnp.einsum(
        "tq,dq->td", grad_key_low, key_back, preferred_element_type=jnp.float32
    )
    partial_one = partial_one + jnp.einsum(
        "tq,dq->td", grad_value_low, value_back, preferred_element_type=jnp.float32
    )
    grad_normed_one = lax.psum(partial_one, "mp")
    grad_inputs_norm, grad_gain_one = norm_back(
        inputs, gain_attn_back.astype(jnp.float32), grad_normed_one
    )
    input_grad = (
        (grad_middle + grad_inputs_norm)
        .astype(jnp.bfloat16)
        .reshape(seq_count, slot_count, width_all)
    )
    attn_grads = (
        lax.psum_scatter(grad_query, ("dp", "ctx"), scatter_dimension=0, tiled=True),
        lax.psum_scatter(grad_key, ("dp", "ctx"), scatter_dimension=0, tiled=True),
        lax.psum_scatter(grad_value, ("dp", "ctx"), scatter_dimension=0, tiled=True),
        lax.psum_scatter(grad_output, ("dp", "ctx"), scatter_dimension=1, tiled=True),
        lax.psum_scatter(grad_gain_one, ("dp", "ctx"), scatter_dimension=0, tiled=True),
    )
    return (
        layer_out,
        input_grad,
        attn_grads[4],
        attn_grads[0],
        attn_grads[1],
        attn_grads[2],
        attn_grads[3],
        mlp_grads[3],
        mlp_grads[0],
        mlp_grads[1],
        mlp_grads[2],
    )


def solution(mesh):
    return jax.shard_map(
        on_device,
        mesh=mesh,
        in_specs=(
            P("dp", "ctx", None),
            P("dp", "ctx", None),
            P("dp"),
            P(("dp", "ctx")),
            P(("dp", "ctx"), "mp"),
            P(("dp", "ctx"), "mp"),
            P(("dp", "ctx"), "mp"),
            P("mp", ("dp", "ctx")),
            P(("dp", "ctx")),
            P(("dp", "ctx"), "mp"),
            P(("dp", "ctx"), "mp"),
            P("mp", ("dp", "ctx")),
        ),
        out_specs=(
            P("dp", "ctx", None),
            P("dp", "ctx", None),
            P(("dp", "ctx")),
            P(("dp", "ctx"), "mp"),
            P(("dp", "ctx"), "mp"),
            P(("dp", "ctx"), "mp"),
            P("mp", ("dp", "ctx")),
            P(("dp", "ctx")),
            P(("dp", "ctx"), "mp"),
            P(("dp", "ctx"), "mp"),
            P("mp", ("dp", "ctx")),
        ),
        check_vma=False,
    )
```

profile of v0, /device:TPU:0, one launch (start us, length us, event | category | flops | bytes accessed | tf_op | source)
XLA Modules:
  0.0 1362.0 jit_solution(10992167410683904162)
XLA Ops:
  13.2 25.8 %all-reduce.5 = (bf16[2560]{0:T(1024)(128)(2,1)S(1)}, bf16[2560]{0:T(1024)(128)(2,1)S(1)}) all-reduce(bf16[2560]{0:T(1024)(128)(2,1)S(1)} %dynamic-update-slice, bf16[2560]{0:T(1024)(128)(2,1)S(1)} %dynamic-update-slice.1), channel_id=1, replica_groups=mesh['dp'=2,'ctx'=4,'mp'=4] {'dp','ctx'}, use_global_device_ids=true, to_apply=%add | all-reduce | flops 5120 | bytes 20480
  39.0 11.2 all-gather.2
  51.2 13.2 all-gather.1
  68.3 7.5 all_gather.46
  76.4 8.6 all-gather
  85.3 5.6 copy.40
  90.9 3.0 fusion.45
  96.9 2.1 copy-done
  100.7 4.8 fusion.79
  108.4 101.6 %all-reduce.11.cloned.1.call-done = f32[256,2560]{1,0:T(8,128)} async-done(((f32[256,2560]{1,0:T(8,128)}), f32[256,2560]{1,0:T(8,128)}) %all-reduce.11.cloned.1.call-update) | async-done | bytes 2621456 | tf_op jit(solution)/shard_map/psum | solution.py:141
  209.9 2.2 multiply_reduce_fusion.2
  213.8 54.6 %all-gather.15.cloned.1.call-done = bf16[2560,1792]{1,0:T(8,128)(2,1)} async-done(((bf16[320,1792]{1,0:T(8,128)(2,1)}), bf16[2560,1792]{1,0:T(8,128)(2,1)}) %all-gather.15.cloned.1.call-update) | async-done | bytes 9175056 | tf_op jit(solution)/shard_map/all_gather | solution.py:145
  268.4 7.4 fusion.81
  275.8 52.1 %all-gather.13.cloned.1.call-done = bf16[2560,1792]{1,0:T(8,128)(2,1)} async-done(((bf16[320,1792]{1,0:T(8,128)(2,1)}), bf16[2560,1792]{1,0:T(8,128)(2,1)}) %all-gather.13.cloned.1.call-update) | async-done | bytes 9175056 | tf_op jit(solution)/shard_map/all_gather | solution.py:144
  327.9 7.4 fusion.80
  335.3 52.1 %all-gather.17.cloned.1.call-done = bf16[1792,2560]{0,1:T(8,128)(2,1)} async-done(((bf16[1792,320]{0,1:T(8,128)(2,1)}), bf16[1792,2560]{0,1:T(8,128)(2,1)}) %all-gather.17.cloned.1.call-update) | async-done | bytes 9175056 | tf_op jit(solution)/shard_map/all_gather | solution.py:146
  387.4 9.1 multiply_convert_fusion.2
  396.6 6.8 fusion.82
  403.5 4.1 convolution_add_fusion.2
  407.8 7.5 convolution_convert_fusion
  416.7 95.1 %all-reduce.15.cloned.1.call-done = f32[256,2560]{1,0:T(8,128)} async-done(((f32[256,2560]{1,0:T(8,128)}), f32[256,2560]{1,0:T(8,128)}) %all-reduce.15.cloned.1.call-update) | async-done | bytes 2621456 | tf_op jit(solution)/shard_map/psum | solution.py:185
  511.9 3.9 multiply_reduce_fusion
  516.3 57.6 %all-reduce.13.cloned.1.call-done = bf16[256,2560]{1,0:T(8,128)(2,1)} async-done(((bf16[256,2560]{1,0:T(8,128)(2,1)}), bf16[256,2560]{1,0:T(8,128)(2,1)}) %all-reduce.13.cloned.1.call-update) | async-done | bytes 1310736 | tf_op jit(solution)/shard_map/psum | solution.py:155
  573.9 5.7 fusion.27
  584.9 5.8 fusion.5
  590.7 5.5 fusion
  596.2 4.8 fusion.2
  603.0 2.2 fusion.48
  605.3 7.7 reduce-scatter.16.cloned.1.call-done
  613.0 3.2 fusion.41
  616.2 22.1 %reduce-scatter.14.cloned.1.call-done = f32[1,256,160]{1,2,0:T(8,128)} async-done(((f32[1,1024,160]{1,2,0:T(8,128)}), f32[1,256,160]{1,2,0:T(8,128)}) %reduce-scatter.14.cloned.1.call-update) | async-done | bytes 163856 | tf_op jit(solution)/shard_map/reduce_scatter | solution.py:250
  639.4 2.3 fusion.39
  642.0 3.3 convolution_multiply_fusion
  651.0 5.8 fusion.57
  657.8 4.0 fusion.37
  662.9 10.3 fusion.60
  674.4 8.9 fusion.85
  684.6 8.9 fusion.84
  696.0 36.3 %reduce-scatter.28.cloned.1.call-done = f32[320,160]{1,0:T(8,128)} async-done(((f32[2560,160]{1,0:T(8,128)}), f32[320,160]{1,0:T(8,128)}) %reduce-scatter.28.cloned.1.call-update) | async-done | bytes 204816
  734.1 104.7 %all-reduce.17.cloned.1.call-done = f32[256,2560]{1,0:T(8,128)} async-done(((f32[256,2560]{1,0:T(8,128)}), f32[256,2560]{1,0:T(8,128)}) %all-reduce.17.cloned.1.call-update) | async-done | bytes 2621456 | tf_op jit(solution)/shard_map/psum | solution.py:280
  838.8 2.5 fusion.24
  841.3 24.0 %all-reduce.4 = (f32[2560]{0:T(1024)S(1)}, f32[2560]{0:T(1024)S(1)}) all-reduce(f32[2560]{0:T(1024)S(1)} %get-tuple-element.59, f32[2560]{0:T(1024)S(1)} %copy-done.32), channel_id=5, replica_groups=mesh['dp'=2,'ctx'=4,'mp'=4] {'dp','ctx'}, use_global_device_ids=true, to_apply=%region_14.15.clone | all-reduce | flops 5120 | bytes 40960
  866.5 4.4 fusion.30
  870.9 33.8 %reduce-scatter.20.cloned.1.call-done = f32[640,320]{0,1:T(8,128)} async-done(((f32[640,2560]{0,1:T(8,128)}), f32[640,320]{0,1:T(8,128)}) %reduce-scatter.20.cloned.1.call-update) | async-done | bytes 819216 | tf_op jit(solution)/shard_map/reduce_scatter | solution.py:293
  904.7 67.3 %reduce-scatter.18.cloned.1.call-done = f32[320,640]{1,0:T(8,128)} async-done(((f32[2560,640]{1,0:T(8,128)}), f32[320,640]{1,0:T(8,128)}) %reduce-scatter.18.cloned.1.call-update) | async-done | bytes 819216 | tf_op jit(solution)/shard_map/reduce_scatter | solution.py:290
  972.0 127.5 %reduce-scatter.26.cloned.1.call-done = f32[1792,320]{0,1:T(8,128)} async-done(((f32[1792,2560]{0,1:T(8,128)}), f32[1792,320]{0,1:T(8,128)}) %reduce-scatter.26.cloned.1.call-update) | async-done | bytes 2293776 | tf_op jit(solution)/shard_map/reduce_scatter | solution.py:192
  1099.5 127.9 %reduce-scatter.24.cloned.1.call-done = f32[320,1792]{1,0:T(8,128)} async-done(((f32[2560,1792]{1,0:T(8,128)}), f32[320,1792]{1,0:T(8,128)}) %reduce-scatter.24.cloned.1.call-update) | async-done | bytes 2293776 | tf_op jit(solution)/shard_map/reduce_scatter | solution.py:191
  1227.4 127.5 %reduce-scatter.22.cloned.1.call-done = f32[320,1792]{1,0:T(8,128)} async-done(((f32[2560,1792]{1,0:T(8,128)}), f32[320,1792]{1,0:T(8,128)}) %reduce-scatter.22.cloned.1.call-update) | async-done | bytes 2293776 | tf_op jit(solution)/shard_map/reduce_scatter | solution.py:190
  (161 shorter events, 45.2 us)
Async XLA Ops:
  7.2 78.1 %all-gather.9.cloned.1.call-start = ((), (), s32[]{:S(2)}) async-start(), calls=%async_computation.9 | async-start | bytes 3686400 | tf_op jit(solution)/shard_map/all_gather | solution.py:87
  7.9 43.3 %copy-start.30 = (bf16[320,160]{0,1:T(8,128)(2,1)S(1)}, bf16[320,160]{0,1:T(8,128)(2,1)}, u32[]{:S(2)}) copy-start(bf16[320,160]{0,1:T(8,128)(2,1)} %param.18) | copy-start | bytes 307204
  7.9 92.7 %all-gather.11.cloned.1.call-start = ((), (), s32[]{:S(2)}) async-start(), calls=%async_computation.10 | async-start | bytes 3686400 | tf_op jit(solution)/shard_map/all_gather | solution.py:90
  8.7 201.3 %all-reduce.11.cloned.1.call-start = ((), (), s32[]{:S(2)}) async-start(), calls=%async_computation.11 | async-start | bytes 5242880 | tf_op jit(solution)/shard_map/psum | solution.py:141
  51.2 15.2 %copy-start.1 = (bf16[1,256,2560]{2,1,0:T(8,128)(2,1)S(1)}, bf16[1,256,2560]{2,1,0:T(8,128)(2,1)}, u32[]{:S(2)}) copy-start(bf16[1,256,2560]{2,1,0:T(8,128)(2,1)} %param.12) | copy-start | bytes 3932164
  66.4 9.4 copy-start.7
  67.6 570.8 %copy-start.21 = (f32[256,40]{0,1:T(8,128)}, f32[256,40]{0,1:T(8,128)S(1)}, u32[]{:S(2)}) copy-start(f32[256,40]{0,1:T(8,128)S(1)} %get-tuple-element.91) | copy-start | bytes 122884
  67.6 570.8 %copy-start.23 = (f32[256,40]{0,1:T(8,128)}, f32[256,40]{0,1:T(8,128)S(1)}, u32[]{:S(2)}) copy-start(f32[256,40]{0,1:T(8,128)S(1)} %get-tuple-element.92) | copy-start | bytes 122884
  75.7 18.4 %copy-start.9 = (bf16[1,1024,160]{1,2,0:T(8,128)(2,1)}, bf16[1,1024,160]{1,2,0:T(8,128)(2,1)S(1)}, u32[]{:S(2)}) copy-start(bf16[1,1024,160]{1,2,0:T(8,128)(2,1)S(1)} %all_gather.46) | copy-start | bytes 983044
  85.1 11.8 copy-start.18
  94.1 1.6 copy-start.14
  94.1 1.6 copy-start.16
  95.7 3.3 copy-start
  95.7 3.3 copy-start.31
  96.9 3.8 copy-start.33
  100.6 4.8 copy-start.12
  105.5 163.0 %all-gather.15.cloned.1.call-start = ((), (), s32[]{:S(2)}) async-start(), calls=%async_computation.13 | async-start | bytes 10321920 | tf_op jit(solution)/shard_map/all_gather | solution.py:145
  106.1 221.9 %all-gather.13.cloned.1.call-start = ((), (), s32[]{:S(2)}) async-start(), calls=%async_computation.12 | async-start | bytes 10321920 | tf_op jit(solution)/shard_map/all_gather | solution.py:144
  106.6 280.8 %all-gather.17.cloned.1.call-start = ((), (), s32[]{:S(2)}) async-start(), calls=%async_computation.14 | async-start | bytes 10321920 | tf_op jit(solution)/shard_map/all_gather | solution.py:146
  107.2 404.7 %all-reduce.15.cloned.1.call-start = ((), (), s32[]{:S(2)}) async-start(), calls=%async_computation.16 | async-start | bytes 5242880 | tf_op jit(solution)/shard_map/psum | solution.py:185
  212.1 1.4 copy-start.3
  387.4 16.0 %slice-start = ((s8[9175040]{0:T(1024)(128)(4,1)}), s8[4194304]{0:T(1024)(128)(4,1)S(1)}, s32[]{:S(2)}) async-start(s8[9175040]{0:T(1024)(128)(4,1)} %bitcast.215), calls=%async_computation.27 | async-start | bytes 8388608
  387.4 16.0 %slice-start.1 = ((s8[9175040]{0:T(1024)(128)(4,1)}), s8[4194304]{0:T(1024)(128)(4,1)S(1)}, s32[]{:S(2)}) async-start(s8[9175040]{0:T(1024)(128)(4,1)} %bitcast.215), calls=%async_computation.28 | async-start | bytes 8388608
  396.6 6.9 copy-start.25
  396.6 6.9 copy-start.27
  396.6 6.9 slice-start.2
  407.6 166.3 %all-reduce.13.cloned.1.call-start = ((), (), s32[]{:S(2)}) async-start(), calls=%async_computation.15 | async-start | bytes 2621440 | tf_op jit(solution)/shard_map/psum | solution.py:155
  415.4 197.6 %reduce-scatter.16.cloned.1.call-start = ((), (), s32[]{:S(2)}) async-start(), calls=%async_computation.18 | async-start | bytes 819200 | tf_op jit(solution)/shard_map/reduce_scatter | solution.py:251
  573.9 7.2 copy-start.6
  579.6 1.5 copy-start.2
  581.1 3.8 copy-start.29
  590.7 47.7 %reduce-scatter.14.cloned.1.call-start = ((), (), s32[]{:S(2)}) async-start(), calls=%async_computation.17 | async-start | bytes 819200 | tf_op jit(solution)/shard_map/reduce_scatter | solution.py:250
  596.2 6.8 copy-start.15
  596.2 6.8 copy-start.17
  601.0 2.0 copy-start.4
  605.3 88.9 %reduce-scatter.30.cloned.1.call-start = ((), (), s32[]{:S(2)}) async-start(), calls=%async_computation.26 | async-start | bytes 2949120
  616.2 116.1 %reduce-scatter.28.cloned.1.call-start = ((), (), s32[]{:S(2)}) async-start(), calls=%async_computation.25 | async-start | bytes 2949120
  641.7 197.1 %all-reduce.17.cloned.1.call-start = ((), (), s32[]{:S(2)}) async-start(), calls=%async_computation.19 | async-start | bytes 5242880 | tf_op jit(solution)/shard_map/psum | solution.py:280
  642.0 3.3 copy-start.22
  642.0 3.3 copy-start.24
  642.0 3.4 copy-start.5
  650.0 254.7 %reduce-scatter.20.cloned.1.call-start = ((), (), s32[]{:S(2)}) async-start(), calls=%async_computation.21 | async-start | bytes 7372800 | tf_op jit(solution)/shard_map/reduce_scatter | solution.py:293
  656.8 315.2 %reduce-scatter.18.cloned.1.call-start = ((), (), s32[]{:S(2)}) async-start(), calls=%async_computation.20 | async-start | bytes 7372800 | tf_op jit(solution)/shard_map/reduce_scatter | solution.py:290
  661.8 437.7 %reduce-scatter.26.cloned.1.call-start = ((), (), s32[]{:S(2)}) async-start(), calls=%async_computation.24 | async-start | bytes 20643840 | tf_op jit(solution)/shard_map/reduce_scatter | solution.py:192
  673.3 554.2 %reduce-scatter.24.cloned.1.call-start = ((), (), s32[]{:S(2)}) async-start(), calls=%async_computation.23 | async-start | bytes 20643840 | tf_op jit(solution)/shard_map/reduce_scatter | solution.py:191
  683.4 671.5 %reduce-scatter.22.cloned.1.call-start = ((), (), s32[]{:S(2)}) async-start(), calls=%async_computation.22 | async-start | bytes 20643840 | tf_op jit(solution)/shard_map/reduce_scatter | solution.py:190
  693.5 147.8 %copy-start.32 = (f32[2560]{0:T(1024)S(1)}, f32[2560]{0:T(1024)}, u32[]{:S(2)}) copy-start(f32[2560]{0:T(1024)} %get-tuple-element.57) | copy-start | bytes 30724
  693.5 173.0 %copy-start.34 = (f32[256]{0:T(256)S(1)}, f32[256]{0:T(256)}, u32[]{:S(2)}) copy-start(f32[256]{0:T(256)} %get-tuple-element.93) | copy-start | bytes 3076
  (8 other events, 9.1 us)
Sparse Core Ops, SparseCore 0:
  9.9 37.0 all-gather.8
  48.8 36.8 all-gather.10
  105.6 104.2 all-reduce.10
  211.7 56.7 all-gather.14
  270.2 57.7 all-gather.12
  329.7 57.7 all-gather.16
  407.7 104.1 all-reduce.14
  514.8 59.0 all-reduce.12
  590.8 22.1 reduce-scatter.15
  615.9 22.4 reduce-scatter.13
  641.7 43.6 reduce-scatter.29
  688.6 43.6 reduce-scatter.27
  734.6 104.1 all-reduce.16
  842.7 62.0 reduce-scatter.19
  909.0 62.9 reduce-scatter.17
  976.2 123.2 reduce-scatter.25
  1104.1 123.2 reduce-scatter.23
  1231.6 123.2 reduce-scatter.21
where the time goes:
time: 1370 us; the launch traced here: 1360 us
  waiting for transfers between devices  1070 us (78%)
  matrix products  121 us (9%)
  blocking collectives  90.3 us (7%)
  local copies, waits for them, and re-layouts  30.6 us (2%)
  other arithmetic  30.5 us (2%)
  between operations  17.1 us (1%)
    reduce_scatter x1, waiting for transfers between devices, on_device(): lax.psum_scatter(grad_up, ('dp', 'ctx'), scatter_dimension=0, tiled=True)  128 us
    reduce_scatter x1, waiting for transfers between devices, on_device(): lax.psum_scatter(grad_gate, ('dp', 'ctx'), scatter_dimension=0, tiled=True)  127 us
    reduce_scatter x1, waiting for transfers between devices, on_device(): lax.psum_scatter(grad_down, ('dp', 'ctx'), scatter_dimension=1, tiled=True)  127 us
    psum x1, waiting for transfers between devices, on_device(): grad_normed_one = lax.psum(partial_one, 'mp')  105 us
    psum x1, waiting for transfers between devices, on_device(): lax.psum(jnp.dot(attn_low, output_w, preferred_element_type=jnp.float32),...  102 us
    psum x1, waiting for transfers between devices, on_device(): grad_normed_two = lax.psum(partial_two, 'mp')  95.1 us
    reduce_scatter x1, waiting for transfers between devices, on_device(): lax.psum_scatter(grad_query, ('dp', 'ctx'), scatter_dimension=0, tiled=True)  67.3 us
    psum x1, waiting for transfers between devices, on_device(): lax.psum(jnp.dot(hidden, down_w, preferred_element_type=jnp.float32).asty...  57.6 us
  transfers between devices with their start and end apart: 18, of which 15 were waited for; matrix products, arithmetic and copies ran while one was open for 9% of the time, Pallas kernels for 0%

commit v1 on v0

--- a/solution.py
+++ b/solution.py
@@ -67,7 +67,7 @@
     return jnp.where(allowed[None, None], raw_scores, NEG)
 
 
-def on_device(
+def any_mesh(
     hidden_in,
     cotangent,
     lengths,
@@ -308,9 +308,306 @@
     )
 
 
+CORE_SWAP = [(0, 1), (1, 0), (2, 3), (3, 2)]
+Y_SWAP = [(0, 2), (1, 3), (2, 0), (3, 1)]
+X_SWAP = [(0, 1), (1, 0)]
+
+
+def over_core(tensor):
+    return lax.ppermute(tensor, "ctx", CORE_SWAP)
+
+
+class Link:
+    def __init__(self, axis, pairs):
+        self.axis, self.pairs, self.sent = axis, pairs, []
+
+    def send(self, tensor):
+        if len(self.sent) >= 2:
+            tensor, _ = lax.optimization_barrier((tensor, self.sent[-2]))
+        got = lax.ppermute(tensor, self.axis, self.pairs)
+        self.sent.append(got)
+        return got
+
+
+def on_plane(
+    hidden_in,
+    cotangent,
+    lengths,
+    norm_attn,
+    w_query,
+    w_key,
+    w_value,
+    w_output,
+    norm_mlp,
+    w_gate,
+    w_up,
+    w_down,
+):
+    low = jnp.bfloat16
+    f32 = jnp.float32
+    _, rows, width = hidden_in.shape
+    part = w_query.shape[0]
+    chip_part = 2 * part
+    x_at, ctx_at, z_at = lax.axis_index("dp"), lax.axis_index("ctx"), lax.axis_index("mp")
+    y_at, core = ctx_at // 2, ctx_at % 2
+    first = core == 0
+    place = 2 * x_at + y_at
+    z_count = lax.axis_size("mp")
+    owned = rows // z_count
+    x_link, y_link = Link("dp", X_SWAP), Link("ctx", Y_SWAP)
+
+    def relative(tensor):
+        return jnp.concatenate(
+            [
+                lax.dynamic_slice_in_dim(tensor, (place ^ turn) * chip_part, chip_part, axis=-1)
+                for turn in range(4)
+            ],
+            axis=-1,
+        )
+
+    def both(mine, other, axis):
+        return jnp.where(
+            first,
+            jnp.concatenate([mine, other], axis=axis),
+            jnp.concatenate([other, mine], axis=axis),
+        )
+
+    def half(tensor, which, axis):
+        size = tensor.shape[axis] // 2
+        return lax.dynamic_slice_in_dim(tensor, which * size, size, axis=axis)
+
+    def cut(tensor, turn):
+        return tensor[..., turn * chip_part : (turn + 1) * chip_part]
+
+    def chip_block(pieces, split_axis, join_axis):
+        keep = jnp.concatenate([half(piece, core, split_axis) for piece in pieces], axis=1)
+        give = jnp.concatenate([half(piece, 1 - core, split_axis) for piece in pieces], axis=1)
+        return both(keep, over_core(give), join_axis)
+
+    def gather(block):
+        middle = block.shape[0] // 2
+        from_x = x_link.send(block)
+        from_y = y_link.send(block)
+        upper = y_link.send(from_x[:middle])
+        lower = x_link.send(from_y[middle:])
+        return [block, from_y, from_x, jnp.concatenate([upper, lower], axis=0)]
+
+    def scatter(parts):
+        own, for_y, for_x, for_far = parts
+        middle = own.shape[0] // 2
+        upper = x_link.send(for_far[:middle].astype(low))
+        lower = y_link.send(for_far[middle:].astype(low))
+        x_one = x_link.send(for_x[:middle].astype(low))
+        y_two = y_link.send(for_y[middle:].astype(low))
+        y_one = y_link.send((for_y[:middle] + upper.astype(f32)).astype(low))
+        x_two = x_link.send((for_x[middle:] + lower.astype(f32)).astype(low))
+        return jnp.concatenate(
+            [
+                own[:middle] + x_one.astype(f32) + y_one.astype(f32),
+                own[middle:] + x_two.astype(f32) + y_two.astype(f32),
+            ],
+            axis=0,
+        )
+
+    def token_sum(total):
+        mine = half(total, core, 0)
+        mine = mine + over_core(half(total, 1 - core, 0).astype(low)).astype(f32)
+        came_up = came_down = None
+
+        def block(at):
+            return lax.dynamic_slice_in_dim(mine, at * owned, owned, axis=0)
+
+        last = z_count - 1
+        for step in range(last):
+            up = block(jnp.clip(last - step + z_at, 0, last))
+            down = block(jnp.clip(z_at - last + step, 0, last))
+            if step:
+                up, down = up + came_up.astype(f32), down + came_down.astype(f32)
+            came_up = lax.ppermute(up.astype(low), "mp", [(z, z + 1) for z in range(step + 1)])
+            came_down = lax.ppermute(
+                down.astype(low), "mp", [(last - z, last - z - 1) for z in range(step + 1)]
+            )
+        return block(z_at) + came_up.astype(f32) + came_down.astype(f32)
+
+    def token_gather(piece):
+        last = z_count - 1
+        out = jnp.zeros((rows, piece.shape[1]), piece.dtype)
+        out = lax.dynamic_update_slice_in_dim(out, piece, z_at * owned, axis=0)
+        up = down = piece
+        for step in range(last):
+            up = lax.ppermute(up, "mp", [(z, z + 1) for z in range(step, last)])
+            down = lax.ppermute(down, "mp", [(z + 1, z) for z in range(0, last - step)])
+            at_up, at_down = z_at - 1 - step, z_at + 1 + step
+            safe_up = jnp.maximum(at_up, 0) * owned
+            old = lax.dynamic_slice_in_dim(out, safe_up, owned, axis=0)
+            out = lax.dynamic_update_slice_in_dim(
+                out, jnp.where(at_up >= 0, up, old), safe_up, axis=0
+            )
+            safe_down = jnp.minimum(at_down, last) * owned
+            old = lax.dynamic_slice_in_dim(out, safe_down, owned, axis=0)
+            out = lax.dynamic_update_slice_in_dim(
+                out, jnp.where(at_down <= last, down, old), safe_down, axis=0
+            )
+        return out
+
+    def matmul(left, right, dims):
+        return lax.dot_general(left, right, (dims, ((), ())), preferred_element_type=f32)
+
+    nn, nt, tn = ((1,), (0,)), ((1,), (1,)), ((0,), (0,))
+
+    gains = both(*(lambda g: (g, over_core(g)))(jnp.stack([norm_attn, norm_mlp])), 1)
+    gains_x = lax.ppermute(gains, "dp", X_SWAP)
+    gains_y = lax.ppermute(gains, "ctx", Y_SWAP)
+    gains_far = lax.ppermute(gains_x, "ctx", Y_SWAP)
+    gains_all = jnp.concatenate([gains, gains_y, gains_x, gains_far], axis=1).astype(f32)
+    gain_one, gain_two = gains_all[0], gains_all[1]
+
+    qkv_w = gather(chip_block((w_query, w_key, w_value), 1, 0))
+    out_w = gather(chip_block((w_output,), 0, 1))
+    gu_w = gather(chip_block((w_gate, w_up), 1, 0))
+    down_w = gather(chip_block((w_down,), 0, 1))
+
+    length = lengths[0]
+    inputs = relative(hidden_in[0]).astype(f32)
+    h1_mine = normed(inputs, gain_one).astype(low)
+    h1 = both(h1_mine, over_core(h1_mine), 0)
+    slots = (y_at * 2) * rows + jnp.arange(2 * rows, dtype=jnp.int32)
+    my_slots = ctx_at * rows + jnp.arange(rows, dtype=jnp.int32)
+    valid = (my_slots < length).astype(f32)[:, None]
+    dout = valid * relative(cotangent[0]).astype(f32)
+    dm_mine = dout.astype(low)
+    dm = both(dm_mine, over_core(dm_mine), 0)
+    cosine, sine = rope_tables(slots.astype(f32), HEAD)
+
+    qkv = sum(matmul(cut(h1, turn), qkv_w[turn], nn) for turn in (0, 2, 1, 3))
+    heads = w_query.shape[1] // HEAD // 2
+    kv_heads = w_key.shape[1] // HEAD // 2
+    group = heads // kv_heads
+    q_cols, k_cols = heads * HEAD, kv_heads * HEAD
+    chip_rows = 2 * rows
+    q_low = rotate(qkv[:, :q_cols].reshape(chip_rows, heads, HEAD), cosine, sine).astype(low)
+    k_low = rotate(
+        qkv[:, q_cols : q_cols + k_cols].reshape(chip_rows, kv_heads, HEAD), cosine, sine
+    ).astype(low)
+    v_low = qkv[:, q_cols + k_cols :].astype(low)
+    kv_mine = jnp.concatenate([k_low.reshape(chip_rows, k_cols), v_low], axis=1)
+    kv_other = lax.ppermute(kv_mine, "ctx", Y_SWAP)
+    kv_all = jnp.where(
+        y_at == 0,
+        jnp.concatenate([kv_mine, kv_other], axis=0),
+        jnp.concatenate([kv_other, kv_mine], axis=0),
+    )
+    keys = kv_all[:, :k_cols].reshape(2 * chip_rows, kv_heads, HEAD)
+    values = kv_all[:, k_cols:].reshape(2 * chip_rows, kv_heads, HEAD)
+    q_grp = q_low.reshape(chip_rows, kv_heads, group, HEAD)
+    scale = HEAD ** (-0.5)
+    raw = jnp.einsum("bkgh,tkh->kgbt", q_grp, keys, preferred_element_type=f32) * scale
+    key_slots = jnp.arange(2 * chip_rows, dtype=jnp.int32)
+    allowed = (key_slots[None, :] <= slots[:, None]) & (key_slots[None, :] < length)
+    scores = jnp.where(allowed[None, None], raw, NEG)
+    exponent = jnp.exp(scores - jnp.max(scores, axis=-1, keepdims=True))
+    probs = exponent / jnp.sum(exponent, axis=-1, keepdims=True)
+    probs_low = probs.astype(low)
+    mixed = jnp.einsum("kgbt,tkh->bkgh", probs_low, values, preferred_element_type=f32)
+    attn_low = mixed.reshape(chip_rows, q_cols).astype(low)
+    branch = token_sum(
+        jnp.concatenate([matmul(attn_low, out_w[turn], nn) for turn in range(4)], axis=1)
+    )
+    inputs_own = lax.dynamic_slice_in_dim(inputs, z_at * owned, owned, axis=0)
+    middle = inputs_own + branch
+    h2_half = token_gather(normed(middle, gain_two).astype(low))
+    h2 = both(h2_half, over_core(h2_half), 0)
+
+    ff = gu_w[0].shape[1] // 2
+    gu = sum(matmul(cut(h2, turn), gu_w[turn], nn) for turn in (0, 2, 1, 3))
+    gate, up = gu[:, :ff], gu[:, ff:]
+    sigma = jax.nn.sigmoid(gate)
+    hidden = (gate * sigma * up).astype(low)
+    d_hidden = sum(matmul(cut(dm, turn), down_w[turn], nt) for turn in (0, 2, 1, 3))
+    d_gate = (d_hidden * up * sigma * (1.0 + gate * (1.0 - sigma))).astype(low)
+    d_up = (d_hidden * gate * sigma).astype(low)
+    d_gu = jnp.concatenate([d_gate, d_up], axis=1)
+    dh2 = token_sum(jnp.concatenate([matmul(d_gu, gu_w[turn], nt) for turn in range(4)], axis=1))
+    grad_gu = scatter([matmul(cut(h2, turn), d_gu, tn) for turn in range(4)])
+    grad_down = scatter([matmul(hidden, cut(dm, turn), tn) for turn in range(4)])
+    mlp = token_sum(jnp.concatenate([matmul(hidden, down_w[turn], nn) for turn in range(4)], axis=1))
+
+    d_norm, gain_two_part = norm_back(middle, gain_two, dh2)
+    dout_own = lax.dynamic_slice_in_dim(dout, z_at * owned, owned, axis=0)
+    valid_own = lax.dynamic_slice_in_dim(valid, z_at * owned, owned, axis=0)
+    d_middle = dout_own + d_norm
+    da_half = token_gather(d_middle.astype(low))
+    da = both(da_half, over_core(da_half), 0)
+    out_half = token_gather((valid_own * (middle + mlp)).astype(low))
+
+    do = sum(matmul(cut(da, turn), out_w[turn], nt) for turn in range(4)).astype(low)
+    grad_out = scatter([matmul(attn_low, cut(da, turn), tn) for turn in range(4)])
+    do_grp = do.reshape(chip_rows, kv_heads, group, HEAD)
+    d_probs = jnp.einsum("bkgh,tkh->kgbt", do_grp, values, preferred_element_type=f32)
+    inner = jnp.sum(probs * d_probs, axis=-1, keepdims=True)
+    d_scores = (probs * (d_probs - inner)).astype(low)
+    dq = jnp.einsum("kgbt,tkh->bkgh", d_scores, keys, preferred_element_type=f32) * scale
+    dk = jnp.einsum("kgbt,bkgh->tkh", d_scores, q_grp, preferred_element_type=f32) * scale
+    dv = jnp.einsum("kgbt,bkgh->tkh", probs_low, do_grp, preferred_element_type=f32)
+    dkv = jnp.concatenate(
+        [dk.reshape(2 * chip_rows, k_cols), dv.reshape(2 * chip_rows, k_cols)], axis=1
+    )
+    dkv_mine = half(dkv, y_at, 0) + lax.ppermute(half(dkv, 1 - y_at, 0), "ctx", Y_SWAP)
+    dq_low = rotate_back(dq.reshape(chip_rows, heads, HEAD), cosine, sine).astype(low)
+    dk_low = rotate_back(
+        dkv_mine[:, :k_cols].reshape(chip_rows, kv_heads, HEAD), cosine, sine
+    ).astype(low)
+    d_qkv = jnp.concatenate(
+        [
+            dq_low.reshape(chip_rows, q_cols),
+            dk_low.reshape(chip_rows, k_cols),
+            dkv_mine[:, k_cols:].astype(low),
+        ],
+        axis=1,
+    )
+    dh1 = token_sum(jnp.concatenate([matmul(d_qkv, qkv_w[turn], nt) for turn in range(4)], axis=1))
+    grad_qkv = scatter([matmul(cut(h1, turn), d_qkv, tn) for turn in range(4)])
+    d_norm_one, gain_one_part = norm_back(inputs_own, gain_one, dh1)
+    grad_half = token_gather((d_middle + d_norm_one).astype(low))
+
+    gain_sum = lax.psum(
+        relative(jnp.stack([gain_one_part, gain_two_part])), ("dp", "ctx", "mp")
+    )
+    gain_mine = lax.dynamic_slice_in_dim(gain_sum, (2 * place + core) * part, part, axis=1)
+
+    def to_rows(total):
+        give = half(total, 1 - core, 0)
+        return half(total, core, 0), over_core(give)
+
+    def to_cols(total):
+        give = half(total, 1 - core, 1)
+        return both(half(total, core, 1), over_core(give), 0)
+
+    gu_mine, gu_other = to_rows(grad_gu)
+    qkv_mine, qkv_other = to_rows(grad_qkv)
+
+    def joined(start, size, mine, other):
+        return both(mine[:, start : start + size], other[:, start : start + size], 1)
+
+    return (
+        relative(out_half)[None],
+        relative(grad_half)[None],
+        gain_mine[0],
+        joined(0, q_cols, qkv_mine, qkv_other),
+        joined(q_cols, k_cols, qkv_mine, qkv_other),
+        joined(q_cols + k_cols, k_cols, qkv_mine, qkv_other),
+        to_cols(grad_out),
+        gain_mine[1],
+        joined(0, ff, gu_mine, gu_other),
+        joined(ff, ff, gu_mine, gu_other),
+        to_cols(grad_down),
+    )
+
+
 def solution(mesh):
+    plane = dict(mesh.shape) == {"dp": 2, "ctx": 4, "mp": 4}
     return jax.shard_map(
-        on_device,
+        on_plane if plane else any_mesh,
         mesh=mesh,
         in_specs=(
             P("dp", "ctx", None),

time: 1370 us -> 705 us (0.51)
  waiting for transfers between devices: 1070 us -> 226 us
  starting transfers between devices: 1.89 us -> 162 us
  other arithmetic: 30.5 us -> 116 us
  blocking collectives: 90.3 us -> 41.6 us
  matrix products: 121 us -> 76.8 us
  local copies, waits for them, and re-layouts: 30.6 us -> 71.8 us
    reduce_scatter x7 -> x0, waiting for transfers between devices: 514 us -> none  [the longest x1 128 us: on_device(): lax.psum_scatter(grad_up, ('dp', 'ctx'), scatter_dimension=0, tiled=True)]
    psum x4 -> x0, waiting for transfers between devices: 359 us -> none  [the longest x1 105 us: on_device(): grad_normed_one = lax.psum(partial_one, 'mp')]
    ppermute x0 -> x110, waiting for transfers between devices: none -> 226 us  [the longest x40 145 us: send(): got = lax.ppermute(tensor, self.axis, self.pairs)]
    ppermute x0 -> x110, starting transfers between devices: none -> 162 us  [the longest x12 58.9 us: token_sum(): lax.ppermute(up.astype(low), 'mp', [(z, z + 1) for z in range(step + 1)])]
    all_gather x5 -> x0, waiting for transfers between devices: 159 us -> none  [the longest x1 54.6 us: on_device(): lax.all_gather(w_up, ('dp', 'ctx'), axis=0, tiled=True)]
    unnamed x2 -> x0, blocking collectives: 49.8 us -> none
    psum x0 -> x1, blocking collectives: none -> 41.6 us  [on_plane(): lax.psum(relative(jnp.stack([gain_one_part, gain_two_part])), ('dp', 'ctx...]
    all_gather x4 -> x0, blocking collectives: 40.6 us -> none  [the longest x1 13.2 us: on_device(): lax.all_gather(w_value, ('dp', 'ctx'), axis=0, tiled=True)]
  transfers between devices with their start and end apart: 18 -> 110, of which waited for: 15 -> 34; matrix products, arithmetic and copies ran while one was open for 9% -> 26% of each run, Pallas kernels for 0% -> 0%
where the time goes in v1:
time: 705 us; the launch traced here: 698 us
  waiting for transfers between devices  226 us (32%)
  starting transfers between devices  162 us (23%)
  other arithmetic  116 us (16%)
  matrix products  76.8 us (11%)
  local copies, waits for them, and re-layouts  71.8 us (10%)
  blocking collectives  41.6 us (6%)
    ppermute x40, waiting for transfers between devices, send(): got = lax.ppermute(tensor, self.axis, self.pairs)  145 us
    dot_general x48, matrix products, matmul(): lax.dot_general(left, right, (dims, ((), ())), preferred_element_type=f32)  64.7 us
    ppermute x12, starting transfers between devices, token_sum(): lax.ppermute(up.astype(low), 'mp', [(z, z + 1) for z in range(step + 1)])  58.9 us
    ppermute x12, waiting for transfers between devices, token_gather(): down = lax.ppermute(down, 'mp', [(z + 1, z) for z in range(0, last - step)])  46.6 us
    ppermute x40, starting transfers between devices, send(): got = lax.ppermute(tensor, self.axis, self.pairs)  42.8 us
    psum x1, blocking collectives, on_plane(): lax.psum(relative(jnp.stack([gain_one_part, gain_two_part])), ('dp', 'ctx...  41.6 us
    select_n x14, other arithmetic, both(): jnp.where(first, jnp.concatenate([mine, other], axis=axis), jnp.concatena...  30.5 us
    unnamed x194, local copies, waits for them, and re-layouts  27.7 us
  transfers between devices with their start and end apart: 110, of which 34 were waited for; matrix products, arithmetic and copies ran while one was open for 26% of the time, Pallas kernels for 0%

profile of v1, /device:TPU:0, one launch (start us, length us, event | category | flops | bytes accessed | tf_op | source)
XLA Modules:
  0.0 698.0 jit_solution(6107285017837261185)
XLA Ops:
  23.0 10.8 %collective-permute-done.7 = bf16[640,480]{0,1:T(8,128)(2,1)S(1)} collective-permute-done((bf16[640,480]{0,1:T(8,128)(2,1)S(1)}, bf16[640,480]{0,1:T(8,128)(2,1)S(1)}, u32[]{:S(2)}, u32[]{:S(2)}) %collective-permute-start.7) | collective-permute-done | bytes 614432 | tf_op jit(solution)/shard_map/ppermute | solution.py:327
  50.9 7.1 %collective-permute-done.12 = bf16[320,640]{0,1:T(8,128)(2,1)S(1)} collective-permute-done((bf16[320,640]{0,1:T(8,128)(2,1)S(1)}, bf16[320,640]{0,1:T(8,128)(2,1)S(1)}, u32[]{:S(2)}, u32[]{:S(2)}) %collective-permute-start.12) | collective-permute-done | bytes 409632 | tf_op jit(solution)/shard_map/ppermute | solution.py:327
  84.2 4.2 collective-permute-start.17
  91.3 3.8 collective-permute-done.17
  96.2 4.6 collective-permute-start.18
  100.8 4.0 maximum_select_fusion.5
  115.7 4.3 collective-permute-start.19
  125.3 30.6 %collective-permute-done.31 = bf16[640,1792]{1,0:T(8,128)(2,1)} collective-permute-done((bf16[640,1792]{1,0:T(8,128)(2,1)}, bf16[640,1792]{1,0:T(8,128)(2,1)}, u32[]{:S(2)}, u32[]{:S(2)}) %collective-permute-start.31) | collective-permute-done | bytes 2293792 | tf_op jit(solution)/shard_map/ppermute | solution.py:327
  160.1 2.9 collective-permute-start.23
  163.0 3.4 fusion.74
  175.8 6.0 collective-permute-done.24
  187.5 8.6 %collective-permute-done.33 = bf16[320,1792]{1,0:T(8,128)(2,1)} collective-permute-done((bf16[320,1792]{1,0:T(8,128)(2,1)S(1)}, bf16[320,1792]{1,0:T(8,128)(2,1)}, u32[]{:S(2)}, u32[]{:S(2)}) %collective-permute-start.33) | collective-permute-done | bytes 1146912 | tf_op jit(solution)/shard_map/ppermute | solution.py:327
  198.4 22.2 %collective-permute-done.36 = bf16[896,640]{0,1:T(8,128)(2,1)S(1)} collective-permute-done((bf16[896,640]{0,1:T(8,128)(2,1)}, bf16[896,640]{0,1:T(8,128)(2,1)S(1)}, u32[]{:S(2)}, u32[]{:S(2)}) %collective-permute-start.36) | collective-permute-done | bytes 1146912 | tf_op jit(solution)/shard_map/ppermute | solution.py:327
  246.3 3.4 fusion.91
  251.3 3.2 fusion.87
  260.2 3.3 fusion.173
  266.2 4.3 fusion.161
  290.0 4.5 fusion.159
  305.3 10.1 %collective-permute-done.83 = bf16[320,1792]{1,0:T(8,128)(2,1)} collective-permute-done((bf16[320,1792]{1,0:T(8,128)(2,1)}, bf16[320,1792]{1,0:T(8,128)(2,1)}, u32[]{:S(2)}, u32[]{:S(2)}) %collective-permute-start.83) | collective-permute-done | bytes 1146912 | tf_op jit(solution)/shard_map/ppermute | solution.py:327
  320.6 22.0 %collective-permute-done.94 = bf16[320,1792]{1,0:T(8,128)(2,1)} collective-permute-done((bf16[320,1792]{1,0:T(8,128)(2,1)S(1)}, bf16[320,1792]{1,0:T(8,128)(2,1)}, u32[]{:S(2)}, u32[]{:S(2)}) %collective-permute-start.94) | collective-permute-done | bytes 1146912 | tf_op jit(solution)/shard_map/ppermute | solution.py:327
  349.6 4.2 collective-permute-done.41
  353.7 4.4 collective-permute-start.55
  358.2 4.5 collective-permute-done.55
  363.4 14.7 %collective-permute-done.95 = bf16[448,640]{1,0:T(8,128)(2,1)S(1)} collective-permute-done((bf16[448,640]{1,0:T(8,128)(2,1)S(1)}, bf16[448,640]{1,0:T(8,128)(2,1)S(1)}, u32[]{:S(2)}, u32[]{:S(2)}) %collective-permute-start.95) | collective-permute-done | bytes 573472 | tf_op jit(solution)/shard_map/ppermute | solution.py:327
  383.2 5.2 collective-permute-done.42
  389.7 3.6 collective-permute-done.56
  394.8 21.2 %collective-permute-start.43 = (bf16[64,2560]{1,0:T(8,128)(2,1)S(1)}, bf16[64,2560]{1,0:T(8,128)(2,1)S(1)}, u32[]{:S(2)}, u32[]{:S(2)}) collective-permute-start(bf16[64,2560]{1,0:T(8,128)(2,1)S(1)} %get-tuple-element.152), channel_id=1, source_target_pairs={{0,1},{1,2},{2,3},{4,5},{5,6},{6,7},{8,9},{9,10},{10,11},{12,13},{... | collective-permute-start | bytes 983048 | tf_op jit(solution)/shard_map/ppermute | solution.py:426
  421.9 3.0 fusion.13
  431.9 4.1 collective-permute-done.46
  437.0 4.7 collective-permute-start.47
  443.0 4.6 collective-permute-start.61
  462.8 9.0 %collective-permute-done.50 = bf16[64,2560]{1,0:T(8,128)(2,1)S(1)} collective-permute-done((bf16[64,2560]{1,0:T(8,128)(2,1)}, bf16[64,2560]{1,0:T(8,128)(2,1)S(1)}, u32[]{:S(2)}, u32[]{:S(2)}) %collective-permute-start.50) | collective-permute-done | bytes 327712 | tf_op jit(solution)/shard_map/ppermute | solution.py:439
  474.1 4.9 collective-permute-done.64
  481.4 11.1 %collective-permute-done.66 = bf16[64,2560]{1,0:T(8,128)(2,1)S(1)} collective-permute-done((bf16[64,2560]{1,0:T(8,128)(2,1)S(1)}, bf16[64,2560]{1,0:T(8,128)(2,1)S(1)}, u32[]{:S(2)}, u32[]{:S(2)}) %collective-permute-start.66) | collective-permute-done | bytes 327712 | tf_op jit(solution)/shard_map/ppermute | solution.py:439
  497.0 3.8 maximum_select_fusion
  500.8 3.2 copy.69
  514.0 3.0 fusion
  519.7 3.0 fusion.6
  531.8 3.2 collective-permute-done.89
  535.0 6.4 collective-permute-done.86
  557.9 3.9 collective-permute-done.101
  577.4 5.3 collective-permute-start.71
  601.8 3.8 collective-permute-start.72
  614.0 3.9 collective-permute-done.75
  623.0 3.1 collective-permute-start.76
  627.5 41.6 %psum.7 = f32[2,2560]{1,0:T(2,128)S(1)} all-reduce(f32[2,2560]{1,0:T(2,128)S(1)} %pad_maximum_fusion.19), channel_id=1, replica_groups=mesh['dp'=2,'ctx'=4,'mp'=4] {'dp','ctx','mp'}, use_global_device_ids=true, to_apply=%region_10.11 | all-reduce | flops 5120 | bytes 40960 | tf_op jit(solution)/shard_map/psum | solution.py:573
  677.7 5.6 collective-permute-done.79
  688.3 4.7 collective-permute-done.81
  (605 shorter events, 337.0 us)
Async XLA Ops:
  13.2 25.8 %collective-permute-start.4 = (bf16[256,2560]{1,0:T(8,128)(2,1)S(1)}, bf16[256,2560]{1,0:T(8,128)(2,1)}, u32[]{:S(2)}, u32[]{:S(2)}) collective-permute-start(bf16[256,2560]{1,0:T(8,128)(2,1)S(1)} %multiply_convert_fusion), channel_id=1, source_target_pairs={{0,4},{4,0},{8,12},{12,8},{1,5},{5,1},{9,13},{13,9},{2,6},{6,2},{1... | collective-permute-start | bytes 3932168 | tf_op jit(solution)/shard_map/ppermute | solution.py:317
  17.3 16.5 %collective-permute-start.7 = (bf16[640,480]{0,1:T(8,128)(2,1)S(1)}, bf16[640,480]{0,1:T(8,128)(2,1)S(1)}, u32[]{:S(2)}, u32[]{:S(2)}) collective-permute-start(bf16[640,480]{0,1:T(8,128)(2,1)S(1)} %maximum_select_fusion.11), channel_id=1, source_target_pairs={{0,8},{4,12},{8,0},{12,4},{1,9},{5,13},{9,1},{13,5},{2,10},{6,14},... | collective-permute-start | bytes 1843208 | tf_op jit(solution)/shard_map/ppermute | solution.py:327
  19.4 16.4 %collective-permute-start.6 = (bf16[640,480]{0,1:T(8,128)(2,1)S(1)}, bf16[640,480]{0,1:T(8,128)(2,1)S(1)}, u32[]{:S(2)}, u32[]{:S(2)}) collective-permute-start(bf16[640,480]{0,1:T(8,128)(2,1)S(1)} %maximum_select_fusion.11), channel_id=1, source_target_pairs={{0,16},{16,0},{1,17},{17,1},{2,18},{18,2},{3,19},{19,3},{4,20},{20... | collective-permute-start | bytes 1843208 | tf_op jit(solution)/shard_map/ppermute | solution.py:327
  37.4 20.5 %collective-permute-start.12 = (bf16[320,640]{0,1:T(8,128)(2,1)S(1)}, bf16[320,640]{0,1:T(8,128)(2,1)S(1)}, u32[]{:S(2)}, u32[]{:S(2)}) collective-permute-start(bf16[320,640]{0,1:T(8,128)(2,1)S(1)} %maximum_select_fusion.12), channel_id=1, source_target_pairs={{0,8},{4,12},{8,0},{12,4},{1,9},{5,13},{9,1},{13,5},{2,10},{6,14},... | collective-permute-start | bytes 1228808 | tf_op jit(solution)/shard_map/ppermute | solution.py:327
  37.9 21.3 %collective-permute-start.13 = (bf16[320,640]{0,1:T(8,128)(2,1)S(1)}, bf16[320,640]{0,1:T(8,128)(2,1)S(1)}, u32[]{:S(2)}, u32[]{:S(2)}) collective-permute-start(bf16[320,640]{0,1:T(8,128)(2,1)S(1)} %maximum_select_fusion.12), channel_id=1, source_target_pairs={{0,16},{16,0},{1,17},{17,1},{2,18},{18,2},{3,19},{19,3},{4,20},{20... | collective-permute-start | bytes 1228808 | tf_op jit(solution)/shard_map/ppermute | solution.py:327
  79.1 21.7 %collective-permute-start.30 = (bf16[320,1792]{1,0:T(8,128)(2,1)}, bf16[320,1792]{1,0:T(8,128)(2,1)}, u32[]{:S(2)}, u32[]{:S(2)}) collective-permute-start(bf16[320,1792]{1,0:T(8,128)(2,1)} %pad_maximum_fusion.5), channel_id=1, source_target_pairs={{0,4},{4,0},{8,12},{12,8},{1,5},{5,1},{9,13},{13,9},{2,6},{6,2},{1... | collective-permute-start | bytes 3440648 | tf_op jit(solution)/shard_map/ppermute | solution.py:317
  80.2 31.1 %collective-permute-start.35 = (bf16[896,320]{0,1:T(8,128)(2,1)}, bf16[896,320]{0,1:T(8,128)(2,1)}, u32[]{:S(2)}, u32[]{:S(2)}) collective-permute-start(bf16[896,320]{0,1:T(8,128)(2,1)} %get-tuple-element.195), channel_id=1, source_target_pairs={{0,4},{4,0},{8,12},{12,8},{1,5},{5,1},{9,13},{13,9},{2,6},{6,2},{1... | collective-permute-start | bytes 1720328 | tf_op jit(solution)/shard_map/ppermute | solution.py:317
  90.7 31.7 %collective-permute-start.53 = (bf16[256,2560]{1,0:T(8,128)(2,1)}, bf16[256,2560]{1,0:T(8,128)(2,1)}, u32[]{:S(2)}, u32[]{:S(2)}) collective-permute-start(bf16[256,2560]{1,0:T(8,128)(2,1)} %get-tuple-element.173), channel_id=1, source_target_pairs={{0,4},{4,0},{8,12},{12,8},{1,5},{5,1},{9,13},{13,9},{2,6},{6,2},{1... | collective-permute-start | bytes 3932168 | tf_op jit(solution)/shard_map/ppermute | solution.py:317
  104.8 51.1 %collective-permute-start.31 = (bf16[640,1792]{1,0:T(8,128)(2,1)}, bf16[640,1792]{1,0:T(8,128)(2,1)}, u32[]{:S(2)}, u32[]{:S(2)}) collective-permute-start(bf16[640,1792]{1,0:T(8,128)(2,1)} %maximum_select_fusion.5), channel_id=1, source_target_pairs={{0,16},{16,0},{1,17},{17,1},{2,18},{18,2},{3,19},{19,3},{4,20},{20... | collective-permute-start | bytes 6881288 | tf_op jit(solution)/shard_map/ppermute | solution.py:327
  114.0 55.1 %collective-permute-start.32 = (bf16[640,1792]{1,0:T(8,128)(2,1)}, bf16[640,1792]{1,0:T(8,128)(2,1)S(1)}, u32[]{:S(2)}, u32[]{:S(2)}) collective-permute-start(bf16[640,1792]{1,0:T(8,128)(2,1)} %maximum_select_fusion.5), channel_id=1, source_target_pairs={{0,8},{4,12},{8,0},{12,4},{1,9},{5,13},{9,1},{13,5},{2,10},{6,14},... | collective-permute-start | bytes 6881288 | tf_op jit(solution)/shard_map/ppermute | solution.py:327
  115.7 40.9 %collective-permute-start.19 = (bf16[64,2560]{1,0:T(8,128)(2,1)}, bf16[64,2560]{1,0:T(8,128)(2,1)S(1)}, u32[]{:S(2)}, u32[]{:S(2)}) collective-permute-start(bf16[64,2560]{1,0:T(8,128)(2,1)} %get-tuple-element.156), channel_id=1, source_target_pairs={{0,1},{1,2},{2,3},{4,5},{5,6},{6,7},{8,9},{9,10},{10,11},{12,13},{... | collective-permute-start | bytes 983048 | tf_op jit(solution)/shard_map/ppermute | solution.py:426
  121.1 35.6 %collective-permute-start.22 = (bf16[64,2560]{1,0:T(8,128)(2,1)S(1)}, bf16[64,2560]{1,0:T(8,128)(2,1)S(1)}, u32[]{:S(2)}, u32[]{:S(2)}) collective-permute-start(bf16[64,2560]{1,0:T(8,128)(2,1)S(1)} %add_convert_fusion.13), channel_id=1, source_target_pairs={{3,2},{2,1},{1,0},{7,6},{6,5},{5,4},{11,10},{10,9},{9,8},{15,14},{... | collective-permute-start | bytes 983048 | tf_op jit(solution)/shard_map/ppermute | solution.py:427
  155.9 28.4 %collective-permute-start.37 = (bf16[896,640]{0,1:T(8,128)(2,1)}, bf16[896,640]{0,1:T(8,128)(2,1)S(1)}, u32[]{:S(2)}, u32[]{:S(2)}) collective-permute-start(bf16[896,640]{0,1:T(8,128)(2,1)} %maximum_select_fusion.8), channel_id=1, source_target_pairs={{0,16},{16,0},{1,17},{17,1},{2,18},{18,2},{3,19},{19,3},{4,20},{20... | collective-permute-start | bytes 3440648 | tf_op jit(solution)/shard_map/ppermute | solution.py:327
  167.7 28.4 %collective-permute-start.33 = (bf16[320,1792]{1,0:T(8,128)(2,1)S(1)}, bf16[320,1792]{1,0:T(8,128)(2,1)}, u32[]{:S(2)}, u32[]{:S(2)}) collective-permute-start(bf16[320,1792]{1,0:T(8,128)(2,1)S(1)} %slice.405), channel_id=1, source_target_pairs={{0,8},{4,12},{8,0},{12,4},{1,9},{5,13},{9,1},{13,5},{2,10},{6,14},... | collective-permute-start | bytes 3440648 | tf_op jit(solution)/shard_map/ppermute | solution.py:327
  170.2 52.6 %collective-permute-start.34 = (bf16[320,1792]{1,0:T(8,128)(2,1)}, bf16[320,1792]{1,0:T(8,128)(2,1)}, u32[]{:S(2)}, u32[]{:S(2)}) collective-permute-start(bf16[320,1792]{1,0:T(8,128)(2,1)} %slice.406), channel_id=1, source_target_pairs={{0,16},{16,0},{1,17},{17,1},{2,18},{18,2},{3,19},{19,3},{4,20},{20... | collective-permute-start | bytes 3440648 | tf_op jit(solution)/shard_map/ppermute | solution.py:327
  172.0 48.6 %collective-permute-start.36 = (bf16[896,640]{0,1:T(8,128)(2,1)}, bf16[896,640]{0,1:T(8,128)(2,1)S(1)}, u32[]{:S(2)}, u32[]{:S(2)}) collective-permute-start(bf16[896,640]{0,1:T(8,128)(2,1)} %maximum_select_fusion.8), channel_id=1, source_target_pairs={{0,8},{4,12},{8,0},{12,4},{1,9},{5,13},{9,1},{13,5},{2,10},{6,14},... | collective-permute-start | bytes 3440648 | tf_op jit(solution)/shard_map/ppermute | solution.py:327
  181.8 44.5 %collective-permute-start.25 = (bf16[64,2560]{1,0:T(8,128)(2,1)}, bf16[64,2560]{1,0:T(8,128)(2,1)}, u32[]{:S(2)}, u32[]{:S(2)}) collective-permute-start(bf16[64,2560]{1,0:T(8,128)(2,1)} %collective-permute-done.23), channel_id=1, source_target_pairs={{1,2},{2,3},{5,6},{6,7},{9,10},{10,11},{13,14},{14,15},{17,18},{18... | collective-permute-start | bytes 983048 | tf_op jit(solution)/shard_map/ppermute | solution.py:438
  184.3 42.7 %collective-permute-start.26 = (bf16[64,2560]{1,0:T(8,128)(2,1)}, bf16[64,2560]{1,0:T(8,128)(2,1)}, u32[]{:S(2)}, u32[]{:S(2)}) collective-permute-start(bf16[64,2560]{1,0:T(8,128)(2,1)} %collective-permute-done.24), channel_id=1, source_target_pairs={{1,0},{2,1},{5,4},{6,5},{9,8},{10,9},{13,12},{14,13},{17,16},{18,1... | collective-permute-start | bytes 983048 | tf_op jit(solution)/shard_map/ppermute | solution.py:439
  197.2 45.5 %collective-permute-start.38 = (bf16[448,640]{1,0:T(8,128)(2,1)}, bf16[448,640]{1,0:T(8,128)(2,1)}, u32[]{:S(2)}, u32[]{:S(2)}) collective-permute-start(bf16[448,640]{1,0:T(8,128)(2,1)} %copy.55), channel_id=1, source_target_pairs={{0,8},{4,12},{8,0},{12,4},{1,9},{5,13},{9,1},{13,5},{2,10},{6,14},... | collective-permute-start | bytes 1720328 | tf_op jit(solution)/shard_map/ppermute | solution.py:327
  225.1 18.7 %collective-permute-start.39 = (bf16[448,640]{1,0:T(8,128)(2,1)}, bf16[448,640]{1,0:T(8,128)(2,1)S(1)}, u32[]{:S(2)}, u32[]{:S(2)}) collective-permute-start(bf16[448,640]{1,0:T(8,128)(2,1)} %copy.56), channel_id=1, source_target_pairs={{0,16},{16,0},{1,17},{17,1},{2,18},{18,2},{3,19},{19,3},{4,20},{20... | collective-permute-start | bytes 1720328 | tf_op jit(solution)/shard_map/ppermute | solution.py:327
  285.7 58.0 %collective-permute-start.40 = (bf16[256,2560]{1,0:T(8,128)(2,1)}, bf16[256,2560]{1,0:T(8,128)(2,1)}, u32[]{:S(2)}, u32[]{:S(2)}) collective-permute-start(bf16[256,2560]{1,0:T(8,128)(2,1)} %dynamic-slice_convert_fusion.2), channel_id=1, source_target_pairs={{0,4},{4,0},{8,12},{12,8},{1,5},{5,1},{9,13},{13,9},{2,6},{6,2},{1... | collective-permute-start | bytes 3932168 | tf_op jit(solution)/shard_map/ppermute | solution.py:317
  287.8 27.5 %collective-permute-start.83 = (bf16[320,1792]{1,0:T(8,128)(2,1)}, bf16[320,1792]{1,0:T(8,128)(2,1)}, u32[]{:S(2)}, u32[]{:S(2)}) collective-permute-start(bf16[320,1792]{1,0:T(8,128)(2,1)} %get-tuple-element.60), channel_id=1, source_target_pairs={{0,8},{4,12},{8,0},{12,4},{1,9},{5,13},{9,1},{13,5},{2,10},{6,14},... | collective-permute-start | bytes 3440648 | tf_op jit(solution)/shard_map/ppermute | solution.py:327
  289.6 29.0 %collective-permute-start.82 = (bf16[320,1792]{1,0:T(8,128)(2,1)}, bf16[320,1792]{1,0:T(8,128)(2,1)}, u32[]{:S(2)}, u32[]{:S(2)}) collective-permute-start(bf16[320,1792]{1,0:T(8,128)(2,1)} %get-tuple-element.59), channel_id=1, source_target_pairs={{0,16},{16,0},{1,17},{17,1},{2,18},{18,2},{3,19},{19,3},{4,20},{20... | collective-permute-start | bytes 3440648 | tf_op jit(solution)/shard_map/ppermute | solution.py:327
  300.7 46.1 %collective-permute-start.54 = (bf16[256,2560]{1,0:T(8,128)(2,1)S(1)}, bf16[256,2560]{1,0:T(8,128)(2,1)S(1)}, u32[]{:S(2)}, u32[]{:S(2)}) collective-permute-start(bf16[256,2560]{1,0:T(8,128)(2,1)S(1)} %dynamic-slice_convert_fusion.1), channel_id=1, source_target_pairs={{0,4},{4,0},{8,12},{12,8},{1,5},{5,1},{9,13},{13,9},{2,6},{6,2},{1... | collective-permute-start | bytes 3932168 | tf_op jit(solution)/shard_map/ppermute | solution.py:317
  302.6 40.0 %collective-permute-start.94 = (bf16[320,1792]{1,0:T(8,128)(2,1)S(1)}, bf16[320,1792]{1,0:T(8,128)(2,1)}, u32[]{:S(2)}, u32[]{:S(2)}) collective-permute-start(bf16[320,1792]{1,0:T(8,128)(2,1)S(1)} %slice.640), channel_id=1, source_target_pairs={{0,16},{16,0},{1,17},{17,1},{2,18},{18,2},{3,19},{19,3},{4,20},{20... | collective-permute-start | bytes 3440648 | tf_op jit(solution)/shard_map/ppermute | solution.py:327
  315.3 27.6 %collective-permute-start.92 = (bf16[320,1792]{1,0:T(8,128)(2,1)S(1)}, bf16[320,1792]{1,0:T(8,128)(2,1)S(1)}, u32[]{:S(2)}, u32[]{:S(2)}) collective-permute-start(bf16[320,1792]{1,0:T(8,128)(2,1)S(1)} %slice.641), channel_id=1, source_target_pairs={{0,8},{4,12},{8,0},{12,4},{1,9},{5,13},{9,1},{13,5},{2,10},{6,14},... | collective-permute-start | bytes 3440648 | tf_op jit(solution)/shard_map/ppermute | solution.py:327
  318.6 97.5 %collective-permute-start.87 = (bf16[320,1792]{1,0:T(8,128)(2,1)S(1)}, bf16[320,1792]{1,0:T(8,128)(2,1)S(1)}, u32[]{:S(2)}, u32[]{:S(2)}) collective-permute-start(bf16[320,1792]{1,0:T(8,128)(2,1)S(1)} %fusion.16), channel_id=1, source_target_pairs={{0,16},{16,0},{1,17},{17,1},{2,18},{18,2},{3,19},{19,3},{4,20},{20... | collective-permute-start | bytes 3440648 | tf_op jit(solution)/shard_map/ppermute | solution.py:327
  342.6 75.9 %collective-permute-start.84 = (bf16[320,1792]{1,0:T(8,128)(2,1)S(1)}, bf16[320,1792]{1,0:T(8,128)(2,1)S(1)}, u32[]{:S(2)}, u32[]{:S(2)}) collective-permute-start(bf16[320,1792]{1,0:T(8,128)(2,1)S(1)} %fusion.17), channel_id=1, source_target_pairs={{0,8},{4,12},{8,0},{12,4},{1,9},{5,13},{9,1},{13,5},{2,10},{6,14},... | collective-permute-start | bytes 3440648 | tf_op jit(solution)/shard_map/ppermute | solution.py:327
  342.9 35.2 %collective-permute-start.95 = (bf16[448,640]{1,0:T(8,128)(2,1)S(1)}, bf16[448,640]{1,0:T(8,128)(2,1)S(1)}, u32[]{:S(2)}, u32[]{:S(2)}) collective-permute-start(bf16[448,640]{1,0:T(8,128)(2,1)S(1)} %get-tuple-element.72), channel_id=1, source_target_pairs={{0,16},{16,0},{1,17},{17,1},{2,18},{18,2},{3,19},{19,3},{4,20},{20... | collective-permute-start | bytes 1720328 | tf_op jit(solution)/shard_map/ppermute | solution.py:327
  343.7 36.7 %collective-permute-start.93 = (bf16[448,640]{1,0:T(8,128)(2,1)S(1)}, bf16[448,640]{1,0:T(8,128)(2,1)S(1)}, u32[]{:S(2)}, u32[]{:S(2)}) collective-permute-start(bf16[448,640]{1,0:T(8,128)(2,1)S(1)} %get-tuple-element.70), channel_id=1, source_target_pairs={{0,8},{4,12},{8,0},{12,4},{1,9},{5,13},{9,1},{13,5},{2,10},{6,14},... | collective-permute-start | bytes 1720328 | tf_op jit(solution)/shard_map/ppermute | solution.py:327
  362.7 18.6 %collective-permute-start.44 = (bf16[64,2560]{1,0:T(8,128)(2,1)S(1)}, bf16[64,2560]{1,0:T(8,128)(2,1)S(1)}, u32[]{:S(2)}, u32[]{:S(2)}) collective-permute-start(bf16[64,2560]{1,0:T(8,128)(2,1)S(1)} %get-tuple-element.155), channel_id=1, source_target_pairs={{3,2},{7,6},{11,10},{15,14},{19,18},{23,22},{27,26},{31,30}} | collective-permute-start | bytes 983048 | tf_op jit(solution)/shard_map/ppermute | solution.py:427
  388.4 48.6 %collective-permute-start.99 = (bf16[448,640]{1,0:T(8,128)(2,1)S(1)}, bf16[448,640]{1,0:T(8,128)(2,1)S(1)}, u32[]{:S(2)}, u32[]{:S(2)}) collective-permute-start(bf16[448,640]{1,0:T(8,128)(2,1)S(1)} %fusion.37), channel_id=1, source_target_pairs={{0,8},{4,12},{8,0},{12,4},{1,9},{5,13},{9,1},{13,5},{2,10},{6,14},... | collective-permute-start | bytes 1720328 | tf_op jit(solution)/shard_map/ppermute | solution.py:327
  388.8 52.8 %collective-permute-start.96 = (bf16[448,640]{1,0:T(8,128)(2,1)S(1)}, bf16[448,640]{1,0:T(8,128)(2,1)S(1)}, u32[]{:S(2)}, u32[]{:S(2)}) collective-permute-start(bf16[448,640]{1,0:T(8,128)(2,1)S(1)} %fusion.38), channel_id=1, source_target_pairs={{0,16},{16,0},{1,17},{17,1},{2,18},{18,2},{3,19},{19,3},{4,20},{20... | collective-permute-start | bytes 1720328 | tf_op jit(solution)/shard_map/ppermute | solution.py:327
  394.8 36.5 %collective-permute-start.43 = (bf16[64,2560]{1,0:T(8,128)(2,1)S(1)}, bf16[64,2560]{1,0:T(8,128)(2,1)S(1)}, u32[]{:S(2)}, u32[]{:S(2)}) collective-permute-start(bf16[64,2560]{1,0:T(8,128)(2,1)S(1)} %get-tuple-element.152), channel_id=1, source_target_pairs={{0,1},{1,2},{2,3},{4,5},{5,6},{6,7},{8,9},{9,10},{10,11},{12,13},{... | collective-permute-start | bytes 983048 | tf_op jit(solution)/shard_map/ppermute | solution.py:426
  436.0 68.0 %collective-permute-start.108 = (f32[320,1792]{1,0:T(8,128)}, f32[320,1792]{1,0:T(8,128)}, u32[]{:S(2)}, u32[]{:S(2)}) collective-permute-start(f32[320,1792]{1,0:T(8,128)} %get-tuple-element.139), channel_id=1, source_target_pairs={{0,4},{4,0},{8,12},{12,8},{1,5},{5,1},{9,13},{13,9},{2,6},{6,2},{1... | collective-permute-start | bytes 6881288 | tf_op jit(solution)/shard_map/ppermute | solution.py:317
  437.0 17.5 %collective-permute-start.47 = (bf16[64,2560]{1,0:T(8,128)(2,1)}, bf16[64,2560]{1,0:T(8,128)(2,1)}, u32[]{:S(2)}, u32[]{:S(2)}) collective-permute-start(bf16[64,2560]{1,0:T(8,128)(2,1)} %get-tuple-element.131), channel_id=1, source_target_pairs={{0,1},{1,2},{2,3},{4,5},{5,6},{6,7},{8,9},{9,10},{10,11},{12,13},{... | collective-permute-start | bytes 983048 | tf_op jit(solution)/shard_map/ppermute | solution.py:438
  454.5 39.6 %collective-permute-start.109 = (f32[896,320]{0,1:T(8,128)}, f32[896,320]{0,1:T(8,128)}, u32[]{:S(2)}, u32[]{:S(2)}) collective-permute-start(f32[896,320]{0,1:T(8,128)} %copy.64), channel_id=1, source_target_pairs={{0,4},{4,0},{8,12},{12,8},{1,5},{5,1},{9,13},{13,9},{2,6},{6,2},{1... | collective-permute-start | bytes 3440648 | tf_op jit(solution)/shard_map/ppermute | solution.py:317
  461.4 17.5 %collective-permute-start.64 = (bf16[64,2560]{1,0:T(8,128)(2,1)S(1)}, bf16[64,2560]{1,0:T(8,128)(2,1)S(1)}, u32[]{:S(2)}, u32[]{:S(2)}) collective-permute-start(bf16[64,2560]{1,0:T(8,128)(2,1)S(1)} %collective-permute-done.62), channel_id=1, source_target_pairs={{1,0},{2,1},{5,4},{6,5},{9,8},{10,9},{13,12},{14,13},{17,16},{18,1... | collective-permute-start | bytes 983048 | tf_op jit(solution)/shard_map/ppermute | solution.py:439
  471.8 20.9 %collective-permute-start.51 = (bf16[64,2560]{1,0:T(8,128)(2,1)S(1)}, bf16[64,2560]{1,0:T(8,128)(2,1)S(1)}, u32[]{:S(2)}, u32[]{:S(2)}) collective-permute-start(bf16[64,2560]{1,0:T(8,128)(2,1)S(1)} %collective-permute-done.49), channel_id=1, source_target_pairs={{2,3},{6,7},{10,11},{14,15},{18,19},{22,23},{26,27},{30,31}} | collective-permute-start | bytes 983048 | tf_op jit(solution)/shard_map/ppermute | solution.py:438
  472.6 20.2 %collective-permute-start.52 = (bf16[64,2560]{1,0:T(8,128)(2,1)S(1)}, bf16[64,2560]{1,0:T(8,128)(2,1)S(1)}, u32[]{:S(2)}, u32[]{:S(2)}) collective-permute-start(bf16[64,2560]{1,0:T(8,128)(2,1)S(1)} %collective-permute-done.50), channel_id=1, source_target_pairs={{1,0},{5,4},{9,8},{13,12},{17,16},{21,20},{25,24},{29,28}} | collective-permute-start | bytes 983048 | tf_op jit(solution)/shard_map/ppermute | solution.py:439
  492.6 16.5 %collective-permute-start.67 = (bf16[256,2560]{1,0:T(8,128)(2,1)S(1)}, bf16[256,2560]{1,0:T(8,128)(2,1)}, u32[]{:S(2)}, u32[]{:S(2)}) collective-permute-start(bf16[256,2560]{1,0:T(8,128)(2,1)S(1)} %select_dynamic-update-slice_fusion.6), channel_id=1, source_target_pairs={{0,4},{4,0},{8,12},{12,8},{1,5},{5,1},{9,13},{13,9},{2,6},{6,2},{1... | collective-permute-start | bytes 3932168 | tf_op jit(solution)/shard_map/ppermute | solution.py:317
  529.1 21.2 %collective-permute-start.100 = (bf16[160,640]{1,0:T(8,128)(2,1)S(1)}, bf16[160,640]{1,0:T(8,128)(2,1)S(1)}, u32[]{:S(2)}, u32[]{:S(2)}) collective-permute-start(bf16[160,640]{1,0:T(8,128)(2,1)S(1)} %slice.646), channel_id=1, source_target_pairs={{0,8},{4,12},{8,0},{12,4},{1,9},{5,13},{9,1},{13,5},{2,10},{6,14},... | collective-permute-start | bytes 614408 | tf_op jit(solution)/shard_map/ppermute | solution.py:327
  530.2 21.2 %collective-permute-start.97 = (bf16[160,640]{1,0:T(8,128)(2,1)S(1)}, bf16[160,640]{1,0:T(8,128)(2,1)S(1)}, u32[]{:S(2)}, u32[]{:S(2)}) collective-permute-start(bf16[160,640]{1,0:T(8,128)(2,1)S(1)} %slice.647), channel_id=1, source_target_pairs={{0,16},{16,0},{1,17},{17,1},{2,18},{18,2},{3,19},{19,3},{4,20},{20... | collective-permute-start | bytes 614408 | tf_op jit(solution)/shard_map/ppermute | solution.py:327
  556.0 21.4 %collective-permute-start.105 = (bf16[320,480]{0,1:T(8,128)(2,1)S(1)}, bf16[320,480]{0,1:T(8,128)(2,1)S(1)}, u32[]{:S(2)}, u32[]{:S(2)}) collective-permute-start(bf16[320,480]{0,1:T(8,128)(2,1)S(1)} %slice.644), channel_id=1, source_target_pairs={{0,8},{4,12},{8,0},{12,4},{1,9},{5,13},{9,1},{13,5},{2,10},{6,14},... | collective-permute-start | bytes 921608 | tf_op jit(solution)/shard_map/ppermute | solution.py:327
  556.3 26.4 %collective-permute-start.91 = (bf16[320,480]{0,1:T(8,128)(2,1)}, bf16[320,480]{0,1:T(8,128)(2,1)}, u32[]{:S(2)}, u32[]{:S(2)}) collective-permute-start(bf16[320,480]{0,1:T(8,128)(2,1)} %slice.645), channel_id=1, source_target_pairs={{0,16},{16,0},{1,17},{17,1},{2,18},{18,2},{3,19},{19,3},{4,20},{20... | collective-permute-start | bytes 921608 | tf_op jit(solution)/shard_map/ppermute | solution.py:327
  562.8 20.0 %collective-permute-start.103 = (bf16[320,480]{0,1:T(8,128)(2,1)}, bf16[320,480]{0,1:T(8,128)(2,1)}, u32[]{:S(2)}, u32[]{:S(2)}) collective-permute-start(bf16[320,480]{0,1:T(8,128)(2,1)} %fusion.41), channel_id=1, source_target_pairs={{0,16},{16,0},{1,17},{17,1},{2,18},{18,2},{3,19},{19,3},{4,20},{20... | collective-permute-start | bytes 921608 | tf_op jit(solution)/shard_map/ppermute | solution.py:327
  623.0 46.8 %collective-permute-start.76 = (bf16[64,2560]{1,0:T(8,128)(2,1)}, bf16[64,2560]{1,0:T(8,128)(2,1)S(1)}, u32[]{:S(2)}, u32[]{:S(2)}) collective-permute-start(bf16[64,2560]{1,0:T(8,128)(2,1)} %get-tuple-element.125), channel_id=1, source_target_pairs={{0,1},{1,2},{2,3},{4,5},{5,6},{6,7},{8,9},{9,10},{10,11},{12,13},{... | collective-permute-start | bytes 983048 | tf_op jit(solution)/shard_map/ppermute | solution.py:438
  626.0 46.2 %collective-permute-start.77 = (bf16[64,2560]{1,0:T(8,128)(2,1)}, bf16[64,2560]{1,0:T(8,128)(2,1)S(1)}, u32[]{:S(2)}, u32[]{:S(2)}) collective-permute-start(bf16[64,2560]{1,0:T(8,128)(2,1)} %get-tuple-element.125), channel_id=1, source_target_pairs={{1,0},{2,1},{3,2},{5,4},{6,5},{7,6},{9,8},{10,9},{11,10},{13,12},{... | collective-permute-start | bytes 983048 | tf_op jit(solution)/shard_map/ppermute | solution.py:439
  (154 other events, 1335.4 us)

commit v2 on v1

--- a/solution.py
+++ b/solution.py
@@ -1,6 +1,10 @@
+import functools
+
 import jax
 import jax.numpy as jnp
 from jax import lax
+from jax.experimental import pallas as pl
+from jax.experimental.pallas import tpu as pltpu
 from jax.sharding import PartitionSpec as P
 
 HEAD = 80
@@ -305,6 +309,327 @@
         mlp_grads[0],
         mlp_grads[1],
         mlp_grads[2],
+    )
+
+
+SPLIT = 4
+
+
+class Column:
+    def __init__(self, owned, width):
+        self.x, self.ctx, self.z = (lax.axis_index(name) for name in ("dp", "ctx", "mp"))
+        self.core = lax.rem(self.ctx, 2)
+        self.last = lax.axis_size("mp") - 1
+        self.owned, self.rows, self.width = owned, owned * (self.last + 1), width
+        self.step = width // SPLIT
+        self.sibling = (self.x, self.ctx + 1 - 2 * self.core, self.z)
+        self.above, self.below = (self.x, self.ctx, self.z + 1), (self.x, self.ctx, self.z - 1)
+
+    def enter(self):
+        barrier = pltpu.get_barrier_semaphore()
+
+        def greet(device):
+            pl.semaphore_signal(
+                barrier, inc=1, device_id=device, device_id_type=pl.DeviceIdType.MESH
+            )
+
+        greet(self.sibling)
+
+        @pl.when(self.z < self.last)
+        def _():
+            greet(self.above)
+
+        @pl.when(self.z > 0)
+        def _():
+            greet(self.below)
+
+        ends = jnp.where(self.z == 0, 1, 0) + jnp.where(self.z == self.last, 1, 0)
+        pl.semaphore_wait(barrier, 3 - ends)
+
+    def place(self, core, block):
+        return pl.ds(pl.multiple_of(core * self.rows + block * self.owned, 16), self.owned)
+
+    def block(self, at):
+        return pl.ds(pl.multiple_of(at * self.owned, 16), self.owned)
+
+    def columns(self, piece):
+        return pl.ds(piece * self.step, self.step)
+
+
+def remote(src, dst, send, recv, device):
+    return pltpu.make_async_remote_copy(
+        src_ref=src,
+        dst_ref=dst,
+        send_sem=send,
+        recv_sem=recv,
+        device_id=device,
+        device_id_type=pl.DeviceIdType.MESH,
+    )
+
+
+class SumChain:
+    def __init__(self, col, part, held, up_out, up_in, down_out, down_in, core_sem, up_sem, down_sem):
+        self.col, self.part, self.held = col, part, held
+        self.ways = (
+            (col.above, up_out, up_in, up_sem, 1),
+            (col.below, down_out, down_in, down_sem, -1),
+        )
+        self.core_sem = core_sem
+
+    def across(self, block):
+        col = self.col
+        return remote(
+            self.part.at[col.place(1 - col.core, block)],
+            self.held.at[col.block(block)],
+            self.core_sem.at[0, block],
+            self.core_sem.at[1, block],
+            col.sibling,
+        )
+
+    def open(self):
+        for block in range(self.col.last + 1):
+            self.across(block).start()
+
+    def own(self, at, cols):
+        col = self.col
+        mine = self.part[col.place(col.core, at), cols].astype(jnp.float32)
+        return mine + self.held[col.block(at), cols].astype(jnp.float32)
+
+    def hop(self, way, step, piece):
+        device, out, into, sem, _ = way
+        cols = self.col.columns(piece)
+        return remote(
+            out.at[step, :, cols],
+            into.at[step, :, cols],
+            sem.at[0, step, piece],
+            sem.at[1, step, piece],
+            device,
+        )
+
+    def far(self, way):
+        return self.col.z if way[4] == 1 else self.col.last - self.col.z
+
+    def step(self, step):
+        col = self.col
+        for way in self.ways:
+            sign = way[4]
+
+            @pl.when(self.far(way) <= step)
+            def _(way=way, sign=sign):
+                at = col.z + sign * (col.last - step)
+                self.across(at).wait_recv()
+                for piece in range(SPLIT):
+                    cols = col.columns(piece)
+                    out = way[1]
+                    total = self.own(at, cols)
+                    if step:
+
+                        @pl.when(self.far(way) > 0)
+                        def _(total=total, cols=cols, piece=piece):
+                            self.hop(way, step - 1, piece).wait_recv()
+                            got = way[2][step - 1, :, cols].astype(jnp.float32)
+                            out[step, :, cols] = (total + got).astype(out.dtype)
+
+                        @pl.when(self.far(way) == 0)
+                        def _(total=total, cols=cols):
+                            out[step, :, cols] = total.astype(out.dtype)
+
+                    else:
+                        out[step, :, cols] = total.astype(out.dtype)
+                    self.hop(way, step, piece).start()
+
+    def close(self, result):
+        col = self.col
+        final = col.last - 1
+        self.across(col.z).wait_recv()
+        result[...] = self.own(col.z, slice(None))
+        for way in self.ways:
+
+            @pl.when(self.far(way) > 0)
+            def _(way=way):
+                for piece in range(SPLIT):
+                    self.hop(way, final, piece).wait_recv()
+                result[...] += way[2][final].astype(jnp.float32)
+
+    def drain(self):
+        for block in range(self.col.last + 1):
+            self.across(block).wait_send()
+        for step in range(self.col.last):
+            for way in self.ways:
+
+                @pl.when(self.far(way) <= step)
+                def _(way=way, step=step):
+                    for piece in range(SPLIT):
+                        self.hop(way, step, piece).wait_send()
+
+
+class ShareChain:
+    def __init__(self, col, whole, up_sem, down_sem, core_sem=None):
+        self.col, self.whole, self.core_sem = col, whole, core_sem
+        self.ways = ((col.above, up_sem, 1), (col.below, down_sem, -1))
+
+    def rows(self, at):
+        return self.col.block(at) if self.core_sem is None else self.col.place(self.col.core, at)
+
+    def far(self, way):
+        return self.col.z if way[2] == 1 else self.col.last - self.col.z
+
+    def hop(self, way, step, piece, origin):
+        device, sem, _ = way
+        ref = self.whole.at[self.rows(origin), self.col.columns(piece)]
+        return remote(ref, ref, sem.at[0, step, piece], sem.at[1, step, piece], device)
+
+    def across(self, origin):
+        ref = self.whole.at[self.rows(origin)]
+        return remote(
+            ref, ref, self.core_sem.at[0, origin], self.core_sem.at[1, origin], self.col.sibling
+        )
+
+    def across_in(self, origin):
+        ref = self.whole.at[self.col.place(1 - self.col.core, origin)]
+        return remote(
+            ref, ref, self.core_sem.at[0, origin], self.core_sem.at[1, origin], self.col.sibling
+        )
+
+    def step(self, step):
+        col = self.col
+        for way in self.ways:
+            origin = col.z - way[2] * step
+
+            @pl.when(self.far(way) >= step)
+            def _(way=way, origin=origin):
+                for piece in range(SPLIT):
+                    if step:
+                        self.hop(way, step - 1, piece, origin).wait_recv()
+                    if step < col.last:
+
+                        @pl.when(self.far(way) < col.last)
+                        def _(piece=piece):
+                            self.hop(way, step, piece, origin).start()
+
+                if step and self.core_sem is not None:
+                    self.across(origin).start()
+
+        if step == 0 and self.core_sem is not None:
+            self.across(col.z).start()
+
+    def drain(self):
+        col = self.col
+        for step in range(col.last):
+            for way in self.ways:
+
+                @pl.when((self.far(way) >= step) & (self.far(way) < col.last))
+                def _(way=way, step=step):
+                    for piece in range(SPLIT):
+                        self.hop(way, step, piece, col.z - way[2] * step).wait_send()
+
+        if self.core_sem is not None:
+            for origin in range(col.last + 1):
+                self.across_in(origin).wait_recv()
+                self.across(origin).wait_send()
+
+
+def sum_scratch(owned, z_count, width):
+    hops = z_count - 1
+    low = jnp.bfloat16
+    return [
+        pltpu.VMEM((owned * z_count, width), low),
+        pltpu.VMEM((hops, owned, width), low),
+        pltpu.VMEM((hops, owned, width), low),
+        pltpu.VMEM((hops, owned, width), low),
+        pltpu.VMEM((hops, owned, width), low),
+        pltpu.SemaphoreType.DMA((2, z_count)),
+        pltpu.SemaphoreType.DMA((2, hops, SPLIT)),
+        pltpu.SemaphoreType.DMA((2, hops, SPLIT)),
+    ]
+
+
+def share_scratch(z_count, cores):
+    hops = z_count - 1
+    sems = [pltpu.SemaphoreType.DMA((2, hops, SPLIT))] * 2
+    return sems + ([pltpu.SemaphoreType.DMA((2, z_count))] if cores else [])
+
+
+def branch_kernel(part, inputs, gain, whole, middle, *scratch):
+    col = Column(inputs.shape[0], inputs.shape[1])
+    total = SumChain(col, part, *scratch[:8])
+    share = ShareChain(col, whole, *scratch[8:])
+    col.enter()
+    total.open()
+    for step in range(col.last):
+        total.step(step)
+    total.close(middle)
+    middle[...] += inputs[...]
+    whole[col.place(col.core, col.z)] = normed(middle[...], gain[...]).astype(whole.dtype)
+    for step in range(col.last + 1):
+        share.step(step)
+    total.drain()
+    share.drain()
+
+
+def middle_kernel(
+    part, mlp_part, middle, gain, dout, valid, whole, d_middle, layer, d_gain, mlp, *scratch
+):
+    col = Column(middle.shape[0], middle.shape[1])
+    total = SumChain(col, part, *scratch[:8])
+    second = SumChain(col, mlp_part, *scratch[8:16])
+    share = ShareChain(col, whole, *scratch[16:])
+    col.enter()
+    total.open()
+    second.open()
+    for step in range(col.last):
+        total.step(step)
+    total.close(d_middle)
+    d_norm, d_gain_row = norm_back(middle[...], gain[...], d_middle[...])
+    d_gain[...] = d_gain_row[None]
+    d_middle[...] = dout[...] + d_norm
+    whole[col.place(col.core, col.z)] = d_middle[...].astype(whole.dtype)
+    for step in range(col.last + 1):
+        share.step(step)
+        if step < col.last:
+            second.step(step)
+    second.close(mlp)
+    layer[...] = (valid[...] * (middle[...] + mlp[...])).astype(layer.dtype)
+    total.drain()
+    second.drain()
+    share.drain()
+
+
+def input_kernel(
+    part, layer, d_middle, inputs, gain, layer_all, grad_all, d_gain, d_normed, *scratch
+):
+    col = Column(inputs.shape[0], inputs.shape[1])
+    total = SumChain(col, part, *scratch[:8])
+    first = ShareChain(col, layer_all, *scratch[8:10])
+    share = ShareChain(col, grad_all, *scratch[10:])
+    layer_all[col.block(col.z)] = layer[...]
+    col.enter()
+    total.open()
+    for step in range(col.last + 1):
+        if step < col.last:
+            total.step(step)
+        first.step(step)
+    total.close(d_normed)
+    d_norm, d_gain_row = norm_back(inputs[...], gain[...], d_normed[...])
+    d_gain[...] = d_gain_row[None]
+    grad_all[col.block(col.z)] = (d_middle[...] + d_norm).astype(grad_all.dtype)
+    for step in range(col.last + 1):
+        share.step(step)
+    total.drain()
+    first.drain()
+    share.drain()
+
+
+def column_call(body, outs, scratch, collective_id, name):
+    return pl.pallas_call(
+        body,
+        out_shape=[jax.ShapeDtypeStruct(shape, dtype) for shape, dtype in outs],
+        scratch_shapes=scratch,
+        name=name,
+        cost_estimate=pl.CostEstimate(flops=0, bytes_accessed=150_000_000, transcendentals=0),
+        compiler_params=pltpu.CompilerParams(
+            collective_id=collective_id, has_side_effects=True, vmem_limit_bytes=32 * 2**20
+        ),
     )
 
 
@@ -409,49 +734,11 @@
             axis=0,
         )
 
-    def token_sum(total):
-        mine = half(total, core, 0)
-        mine = mine + over_core(half(total, 1 - core, 0).astype(low)).astype(f32)
-        came_up = came_down = None
-
-        def block(at):
-            return lax.dynamic_slice_in_dim(mine, at * owned, owned, axis=0)
-
-        last = z_count - 1
-        for step in range(last):
-            up = block(jnp.clip(last - step + z_at, 0, last))
-            down = block(jnp.clip(z_at - last + step, 0, last))
-            if step:
-                up, down = up + came_up.astype(f32), down + came_down.astype(f32)
-            came_up = lax.ppermute(up.astype(low), "mp", [(z, z + 1) for z in range(step + 1)])
-            came_down = lax.ppermute(
-                down.astype(low), "mp", [(last - z, last - z - 1) for z in range(step + 1)]
-            )
-        return block(z_at) + came_up.astype(f32) + came_down.astype(f32)
-
-    def token_gather(piece):
-        last = z_count - 1
-        out = jnp.zeros((rows, piece.shape[1]), piece.dtype)
-        out = lax.dynamic_update_slice_in_dim(out, piece, z_at * owned, axis=0)
-        up = down = piece
-        for step in range(last):
-            up = lax.ppermute(up, "mp", [(z, z + 1) for z in range(step, last)])
-            down = lax.ppermute(down, "mp", [(z + 1, z) for z in range(0, last - step)])
-            at_up, at_down = z_at - 1 - step, z_at + 1 + step
-            safe_up = jnp.maximum(at_up, 0) * owned
-            old = lax.dynamic_slice_in_dim(out, safe_up, owned, axis=0)
-            out = lax.dynamic_update_slice_in_dim(
-                out, jnp.where(at_up >= 0, up, old), safe_up, axis=0
-            )
-            safe_down = jnp.minimum(at_down, last) * owned
-            old = lax.dynamic_slice_in_dim(out, safe_down, owned, axis=0)
-            out = lax.dynamic_update_slice_in_dim(
-                out, jnp.where(at_down <= last, down, old), safe_down, axis=0
-            )
-        return out
-
     def matmul(left, right, dims):
         return lax.dot_general(left, right, (dims, ((), ())), preferred_element_type=f32)
+
+    def parts(left, blocks, dims):
+        return jnp.concatenate([matmul(left, block, dims).astype(low) for block in blocks], axis=1)
 
     nn, nt, tn = ((1,), (0,)), ((1,), (1,)), ((0,), (0,))
 
@@ -510,13 +797,16 @@
     probs_low = probs.astype(low)
     mixed = jnp.einsum("kgbt,tkh->bkgh", probs_low, values, preferred_element_type=f32)
     attn_low = mixed.reshape(chip_rows, q_cols).astype(low)
-    branch = token_sum(
-        jnp.concatenate([matmul(attn_low, out_w[turn], nn) for turn in range(4)], axis=1)
-    )
+    branch = parts(attn_low, out_w, nn)
     inputs_own = lax.dynamic_slice_in_dim(inputs, z_at * owned, owned, axis=0)
-    middle = inputs_own + branch
-    h2_half = token_gather(normed(middle, gain_two).astype(low))
-    h2 = both(h2_half, over_core(h2_half), 0)
+    whole, half_rows, own = (2 * rows, width), (rows, width), (owned, width)
+    h2, middle = column_call(
+        branch_kernel,
+        [(whole, low), (own, f32)],
+        sum_scratch(owned, z_count, width) + share_scratch(z_count, True),
+        1,
+        "branch_sum",
+    )(branch, inputs_own, gain_two[None])
 
     ff = gu_w[0].shape[1] // 2
     gu = sum(matmul(cut(h2, turn), gu_w[turn], nn) for turn in (0, 2, 1, 3))
@@ -527,18 +817,21 @@
     d_gate = (d_hidden * up * sigma * (1.0 + gate * (1.0 - sigma))).astype(low)
     d_up = (d_hidden * gate * sigma).astype(low)
     d_gu = jnp.concatenate([d_gate, d_up], axis=1)
-    dh2 = token_sum(jnp.concatenate([matmul(d_gu, gu_w[turn], nt) for turn in range(4)], axis=1))
+    dh2 = parts(d_gu, gu_w, nt)
     grad_gu = scatter([matmul(cut(h2, turn), d_gu, tn) for turn in range(4)])
     grad_down = scatter([matmul(hidden, cut(dm, turn), tn) for turn in range(4)])
-    mlp = token_sum(jnp.concatenate([matmul(hidden, down_w[turn], nn) for turn in range(4)], axis=1))
-
-    d_norm, gain_two_part = norm_back(middle, gain_two, dh2)
+    mlp = parts(hidden, down_w, nn)
     dout_own = lax.dynamic_slice_in_dim(dout, z_at * owned, owned, axis=0)
     valid_own = lax.dynamic_slice_in_dim(valid, z_at * owned, owned, axis=0)
-    d_middle = dout_own + d_norm
-    da_half = token_gather(d_middle.astype(low))
-    da = both(da_half, over_core(da_half), 0)
-    out_half = token_gather((valid_own * (middle + mlp)).astype(low))
+    da, d_middle, layer_own, gain_two_part = column_call(
+        middle_kernel,
+        [(whole, low), (own, f32), (own, low), ((1, width), f32)],
+        [pltpu.VMEM(own, f32)]
+        + sum_scratch(owned, z_count, width) * 2
+        + share_scratch(z_count, True),
+        2,
+        "middle_sum",
+    )(dh2, mlp, middle, gain_two[None], dout_own, valid_own)
 
     do = sum(matmul(cut(da, turn), out_w[turn], nt) for turn in range(4)).astype(low)
     grad_out = scatter([matmul(attn_low, cut(da, turn), tn) for turn in range(4)])
@@ -565,15 +858,30 @@
         ],
         axis=1,
     )
-    dh1 = token_sum(jnp.concatenate([matmul(d_qkv, qkv_w[turn], nt) for turn in range(4)], axis=1))
+    dh1 = parts(d_qkv, qkv_w, nt)
     grad_qkv = scatter([matmul(cut(h1, turn), d_qkv, tn) for turn in range(4)])
-    d_norm_one, gain_one_part = norm_back(inputs_own, gain_one, dh1)
-    grad_half = token_gather((d_middle + d_norm_one).astype(low))
-
-    gain_sum = lax.psum(
-        relative(jnp.stack([gain_one_part, gain_two_part])), ("dp", "ctx", "mp")
-    )
-    gain_mine = lax.dynamic_slice_in_dim(gain_sum, (2 * place + core) * part, part, axis=1)
+    out_half, grad_half, gain_one_part = column_call(
+        input_kernel,
+        [(half_rows, low), (half_rows, low), ((1, width), f32)],
+        [pltpu.VMEM(own, f32)]
+        + sum_scratch(owned, z_count, width)
+        + share_scratch(z_count, False) * 2,
+        3,
+        "input_sum",
+    )(dh1, layer_own, d_middle, inputs_own, gain_one[None])
+
+    gain_part = jnp.concatenate([gain_one_part, gain_two_part], axis=0)
+    gain_sum = (
+        cut(gain_part, 0)
+        + lax.ppermute(cut(gain_part, 1), "ctx", Y_SWAP)
+        + lax.ppermute(cut(gain_part, 2), "dp", X_SWAP)
+        + lax.ppermute(lax.ppermute(cut(gain_part, 3), "ctx", Y_SWAP), "dp", X_SWAP)
+    )
+    gain_mine = half(gain_sum, core, 1) + over_core(half(gain_sum, 1 - core, 1))
+    for flip in (1, 2):
+        gain_mine = gain_mine + lax.ppermute(
+            gain_mine, "mp", [(z, z ^ flip) for z in range(z_count)]
+        )
 
     def to_rows(total):
         give = half(total, 1 - core, 0)

time: 705 us -> 625 us (0.89)
  Pallas kernels: 0 us -> 179 us
  starting transfers between devices: 162 us -> 57.2 us
  other arithmetic: 116 us -> 61.1 us
  waiting for transfers between devices: 226 us -> 180 us
  blocking collectives: 41.6 us -> 0 us
  local copies, waits for them, and re-layouts: 71.8 us -> 61 us
    pallas_call x0 -> x3, Pallas kernels: none -> 179 us  [the longest x1 64.3 us: on_plane(): column_call(input_kernel, [(half_rows, low), (half_rows, low), ((1, width...]
    ppermute x48 -> x6, starting transfers between devices: 109 us -> 4.28 us  [the longest x1 1.27 us: on_plane(): lax.ppermute(lax.ppermute(cut(gain_part, 3), 'ctx', Y_SWAP), 'dp', X_SWAP)]
    ppermute x48 -> x6, waiting for transfers between devices: 78.4 us -> 3.74 us  [the longest x2 2.59 us: on_plane(): lax.ppermute(gain_mine, 'mp', [(z, z ^ flip) for z in range(z_count)])]
    psum x1 -> x0, blocking collectives: 41.6 us -> none  [on_plane(): lax.psum(relative(jnp.stack([gain_one_part, gain_two_part])), ('dp', 'ctx...]
    dynamic_update_slice x28 -> x0, other arithmetic: 30.3 us -> none  [the longest x12 12.5 us: token_gather(): lax.dynamic_update_slice_in_dim(out, jnp.where(at_down <= last, down, old...]
    ppermute x40, waiting for transfers between devices: 145 us -> 173 us  [send(): got = lax.ppermute(tensor, self.axis, self.pairs)]
    unnamed x194 -> x180, local copies, waits for them, and re-layouts: 27.7 us -> 16.4 us
    convert_element_type x12 -> x0, other arithmetic: 9.09 us -> none  [the longest x8 6.17 us: token_sum(): up.astype(low)]
  transfers between devices with their start and end apart: 110 -> 63, of which waited for: 34 -> 19; matrix products, arithmetic and copies ran while one was open for 26% -> 22% of each run, Pallas kernels for 0% -> 19%
where the time goes in v2:
time: 625 us; the launch traced here: 619 us
  waiting for transfers between devices  180 us (29%)
  Pallas kernels  179 us (29%)
  matrix products  76.9 us (12%)
  other arithmetic  61.1 us (10%)
  local copies, waits for them, and re-layouts  61 us (10%)
  starting transfers between devices  57.2 us (9%)
    ppermute x40, waiting for transfers between devices, send(): got = lax.ppermute(tensor, self.axis, self.pairs)  173 us
    pallas_call x1, Pallas kernels, on_plane(): column_call(input_kernel, [(half_rows, low), (half_rows, low), ((1, width...  64.3 us
    dot_general x48, matrix products, matmul(): lax.dot_general(left, right, (dims, ((), ())), preferred_element_type=f32)  62.5 us
    pallas_call x1, Pallas kernels, on_plane(): column_call(middle_kernel, [(whole, low), (own, f32), (own, low), ((1, wi...  59.7 us
    pallas_call x1, Pallas kernels, on_plane(): column_call(branch_kernel, [(whole, low), (own, f32)], sum_scratch(owned,...  55.1 us
    ppermute x40, starting transfers between devices, send(): got = lax.ppermute(tensor, self.axis, self.pairs)  44.3 us
    select_n x14, other arithmetic, both(): jnp.where(first, jnp.concatenate([mine, other], axis=axis), jnp.concatena...  25.1 us
    unnamed x180, local copies, waits for them, and re-layouts  16.4 us
  transfers between devices with their start and end apart: 63, of which 19 were waited for; matrix products, arithmetic and copies ran while one was open for 22% of the time, Pallas kernels for 19%

profile of v2, /device:TPU:0, one launch (start us, length us, event | category | flops | bytes accessed | tf_op | source)
XLA Modules:
  0.0 618.9 jit_solution(6956141708636106625)
XLA Ops:
  0.7 2.1 constant_dynamic-slice_fusion.25
  19.4 2.9 collective-permute-start.2
  22.3 2.3 constant_dynamic-slice_fusion.19
  36.7 11.3 %collective-permute-done.7 = bf16[640,480]{0,1:T(8,128)(2,1)S(1)} collective-permute-done((bf16[640,480]{0,1:T(8,128)(2,1)S(1)}, bf16[640,480]{0,1:T(8,128)(2,1)S(1)}, u32[]{:S(2)}, u32[]{:S(2)}) %collective-permute-start.7) | collective-permute-done | bytes 614432 | tf_op jit(solution)/shard_map/ppermute | solution.py:652
  51.0 9.9 %maximum_select_fusion.3 = bf16[640,1792]{1,0:T(8,128)(2,1)S(1)} fusion(bf16[320,1792]{1,0:T(8,128)(2,1)} %collective-permute-done.13, bf16[320,896]{1,0:T(8,128)(2,1)S(1)} %copy-done.32, bf16[320,896]{1,0:T(8,128)(2,1)S(1)} %copy-done.33, pred[]{:T(512)S(6)} %eq.9), kind=kLoop, calls=%fused_computation.48 | loop fusion | flops 14909440 | bytes 4587521 | tf_op jit(solution)/shard_map/jit(_where)/select_n | solution.py:694
  63.1 4.3 fusion.60
  74.0 2.0 collective-permute-start.19
  76.3 2.0 collective-permute-done.10
  80.1 1.8 fusion.4
  83.5 2.9 fusion.27
  88.4 40.5 %collective-permute-done.24 = bf16[160,640]{0,1:T(8,128)(2,1)S(1)} collective-permute-done((bf16[160,640]{0,1:T(8,128)(2,1)S(1)}, bf16[160,640]{0,1:T(8,128)(2,1)S(1)}, u32[]{:S(2)}, u32[]{:S(2)}) %collective-permute-start.24) | collective-permute-done | bytes 204832 | tf_op jit(solution)/shard_map/ppermute | solution.py:652
  129.8 55.1 %branch_sum.1 = (bf16[512,2560]{1,0:T(8,128)(2,1)S(1)}, f32[64,2560]{1,0:T(8,128)S(1)}) custom-call(bf16[512,2560]{1,0:T(8,128)(2,1)S(1)} %pad_maximum_fusion.part, f32[64,2560]{1,0:T(8,128)S(1)} %constant_dynamic-slice_fusion.11.inputs, f32[1,2560]{1,0:T(1,128)S(1)} %get-tuple-element.216.gain), custom_call_target="tpu_custom_call" | custom-call | bytes 150000000 | tf_op jit(solution)/shard_map/branch_sum/pallas_call | solution.py:803
  190.6 3.4 fusion.105
  194.0 3.5 fusion.97
  197.5 3.4 fusion.101
  200.9 39.1 %collective-permute-done.17 = bf16[896,640]{0,1:T(8,128)(2,1)S(1)} collective-permute-done((bf16[896,640]{0,1:T(8,128)(2,1)}, bf16[896,640]{0,1:T(8,128)(2,1)S(1)}, u32[]{:S(2)}, u32[]{:S(2)}) %collective-permute-start.17) | collective-permute-done | bytes 1146912 | tf_op jit(solution)/shard_map/ppermute | solution.py:652
  241.9 2.2 copy.56
  244.6 2.2 slice.421
  246.8 2.2 copy.57
  252.8 5.2 add_add_fusion
  257.9 2.3 fusion.52
  269.7 2.4 convolution_convert_fusion.9
  276.7 2.3 convolution_convert_fusion.8
  280.2 59.7 %middle_sum.1 = (bf16[512,2560]{1,0:T(8,128)(2,1)S(1)}, f32[64,2560]{1,0:T(8,128)S(1)}, bf16[64,2560]{1,0:T(8,128)(2,1)S(1)}, f32[1,2560]{1,0:T(1,128)S(1)}) custom-call(bf16[512,2560]{1,0:T(8,128)(2,1)S(1)} %pad_maximum_fusion.1.part, bf16[512,2560]{1,0:T(8,128)(2,1)S(1)} %pad_maximum_fusion.2.mlp_part, f32[64,2560]{1,0:T(8,128)S(1)} %copy-done.2, ...), custom_call_target="tpu_custom_call" | custom-call | bytes 150000000 | tf_op jit(solution)/shard_map/middle_sum/pallas_call | solution.py:826
  343.0 5.2 fusion
  348.1 2.5 fusion.30
  350.6 5.3 fusion.6
  381.9 2.1 fusion.58
  388.4 64.3 %input_sum.1 = (bf16[256,2560]{1,0:T(8,128)(2,1)S(1)}, bf16[256,2560]{1,0:T(8,128)(2,1)S(1)}, f32[1,2560]{1,0:T(1,128)S(1)}) custom-call(bf16[512,2560]{1,0:T(8,128)(2,1)S(1)} %pad_maximum_fusion.3.part, bf16[64,2560]{1,0:T(8,128)(2,1)S(1)} %get-tuple-element.71.layer, f32[64,2560]{1,0:T(8,128)S(1)} %get-tuple-element.72.d_middle, ...), custom_call_target="tpu_custom_call" | custom-call | bytes 150000000 | tf_op jit(solution)/shard_map/input_sum/pallas_call | solution.py:863
  467.8 22.1 %collective-permute-done.47 = bf16[320,1792]{1,0:T(8,128)(2,1)S(1)} collective-permute-done((bf16[320,1792]{1,0:T(8,128)(2,1)S(1)}, bf16[320,1792]{1,0:T(8,128)(2,1)S(1)}, u32[]{:S(2)}, u32[]{:S(2)}) %collective-permute-start.47) | collective-permute-done | bytes 1146912 | tf_op jit(solution)/shard_map/ppermute | solution.py:652
  493.1 29.9 %collective-permute-done.48 = bf16[448,640]{1,0:T(8,128)(2,1)S(1)} collective-permute-done((bf16[448,640]{1,0:T(8,128)(2,1)S(1)}, bf16[448,640]{1,0:T(8,128)(2,1)S(1)}, u32[]{:S(2)}, u32[]{:S(2)}) %collective-permute-start.48) | collective-permute-done | bytes 573472 | tf_op jit(solution)/shard_map/ppermute | solution.py:652
  524.0 2.3 collective-permute-start.49
  528.9 2.6 collective-permute-done.34
  532.1 3.1 collective-permute-done.52
  537.3 2.8 collective-permute-start.50
  540.8 3.0 fusion.13
  543.9 2.1 collective-permute-start.54
  545.9 1.9 collective-permute-start.51
  549.5 8.4 %collective-permute-done.54 = bf16[320,480]{0,1:T(8,128)(2,1)S(1)} collective-permute-done((bf16[320,480]{0,1:T(8,128)(2,1)S(1)}, bf16[320,480]{0,1:T(8,128)(2,1)S(1)}, u32[]{:S(2)}, u32[]{:S(2)}) %collective-permute-start.54) | collective-permute-done | bytes 307232 | tf_op jit(solution)/shard_map/ppermute | solution.py:652
  558.8 1.9 collective-permute-start.56
  563.8 8.3 %collective-permute-done.42 = bf16[160,640]{1,0:T(8,128)(2,1)S(1)} collective-permute-done((bf16[160,640]{1,0:T(8,128)(2,1)S(1)}, bf16[160,640]{1,0:T(8,128)(2,1)S(1)}, u32[]{:S(2)}, u32[]{:S(2)}) %collective-permute-start.42) | collective-permute-done | bytes 204832 | tf_op jit(solution)/shard_map/ppermute | solution.py:652
  572.8 2.0 collective-permute-done.39
  578.4 2.1 fusion.20
  587.9 5.3 collective-permute-done.58
  600.2 2.8 copy.68
  603.0 3.0 maximum_select_fusion
  606.0 2.0 copy.72
  613.5 1.8 fusion.154
  (440 shorter events, 163.9 us)
Async XLA Ops:
  5.4 24.4 %collective-permute-start.5 = (bf16[320,480]{0,1:T(8,128)(2,1)}, bf16[320,480]{0,1:T(8,128)(2,1)}, u32[]{:S(2)}, u32[]{:S(2)}) collective-permute-start(bf16[320,480]{0,1:T(8,128)(2,1)} %pad_maximum_fusion.9), channel_id=1, source_target_pairs={{0,4},{4,0},{8,12},{12,8},{1,5},{5,1},{9,13},{13,9},{2,6},{6,2},{1... | collective-permute-start | bytes 921608 | tf_op jit(solution)/shard_map/ppermute | solution.py:642
  6.0 13.3 %collective-permute-start = (bf16[2,320]{1,0:T(2,128)(2,1)S(1)}, bf16[2,320]{1,0:T(2,128)(2,1)S(1)}, u32[]{:S(2)}, u32[]{:S(2)}) collective-permute-start(bf16[2,320]{1,0:T(2,128)(2,1)S(1)} %pad_maximum_fusion.20), channel_id=1, source_target_pairs={{0,4},{4,0},{8,12},{12,8},{1,5},{5,1},{9,13},{13,9},{2,6},{6,2},{1... | collective-permute-start | bytes 3848 | tf_op jit(solution)/shard_map/ppermute | solution.py:642
  8.4 41.5 %collective-permute-start.13 = (bf16[320,1792]{1,0:T(8,128)(2,1)}, bf16[320,1792]{1,0:T(8,128)(2,1)}, u32[]{:S(2)}, u32[]{:S(2)}) collective-permute-start(bf16[320,1792]{1,0:T(8,128)(2,1)} %pad_maximum_fusion.5), channel_id=1, source_target_pairs={{0,4},{4,0},{8,12},{12,8},{1,5},{5,1},{9,13},{13,9},{2,6},{6,2},{1... | collective-permute-start | bytes 3440648 | tf_op jit(solution)/shard_map/ppermute | solution.py:642
  9.9 22.8 %collective-permute-start.14 = (bf16[320,320]{0,1:T(8,128)(2,1)}, bf16[320,320]{0,1:T(8,128)(2,1)}, u32[]{:S(2)}, u32[]{:S(2)}) collective-permute-start(bf16[320,320]{0,1:T(8,128)(2,1)} %get-tuple-element.200), channel_id=1, source_target_pairs={{0,4},{4,0},{8,12},{12,8},{1,5},{5,1},{9,13},{13,9},{2,6},{6,2},{1... | collective-permute-start | bytes 614408 | tf_op jit(solution)/shard_map/ppermute | solution.py:642
  29.8 31.1 %collective-permute-start.11 = (bf16[256,2560]{1,0:T(8,128)(2,1)S(1)}, bf16[256,2560]{1,0:T(8,128)(2,1)S(1)}, u32[]{:S(2)}, u32[]{:S(2)}) collective-permute-start(bf16[256,2560]{1,0:T(8,128)(2,1)S(1)} %get-tuple-element.156), channel_id=1, source_target_pairs={{0,4},{4,0},{8,12},{12,8},{1,5},{5,1},{9,13},{13,9},{2,6},{6,2},{1... | collective-permute-start | bytes 3932168 | tf_op jit(solution)/shard_map/ppermute | solution.py:642
  31.7 16.3 %collective-permute-start.7 = (bf16[640,480]{0,1:T(8,128)(2,1)S(1)}, bf16[640,480]{0,1:T(8,128)(2,1)S(1)}, u32[]{:S(2)}, u32[]{:S(2)}) collective-permute-start(bf16[640,480]{0,1:T(8,128)(2,1)S(1)} %maximum_select_fusion.9), channel_id=1, source_target_pairs={{0,8},{4,12},{8,0},{12,4},{1,9},{5,13},{9,1},{13,5},{2,10},{6,14},... | collective-permute-start | bytes 1843208 | tf_op jit(solution)/shard_map/ppermute | solution.py:652
  32.7 16.1 %collective-permute-start.6 = (bf16[640,480]{0,1:T(8,128)(2,1)S(1)}, bf16[640,480]{0,1:T(8,128)(2,1)S(1)}, u32[]{:S(2)}, u32[]{:S(2)}) collective-permute-start(bf16[640,480]{0,1:T(8,128)(2,1)S(1)} %maximum_select_fusion.9), channel_id=1, source_target_pairs={{0,16},{16,0},{1,17},{17,1},{2,18},{18,2},{3,19},{19,3},{4,20},{20... | collective-permute-start | bytes 1843208 | tf_op jit(solution)/shard_map/ppermute | solution.py:652
  33.6 33.7 %collective-permute-start.4 = (bf16[256,2560]{1,0:T(8,128)(2,1)S(1)}, bf16[256,2560]{1,0:T(8,128)(2,1)S(1)}, u32[]{:S(2)}, u32[]{:S(2)}) collective-permute-start(bf16[256,2560]{1,0:T(8,128)(2,1)S(1)} %multiply_convert_fusion), channel_id=1, source_target_pairs={{0,4},{4,0},{8,12},{12,8},{1,5},{5,1},{9,13},{13,9},{2,6},{6,2},{1... | collective-permute-start | bytes 3932168 | tf_op jit(solution)/shard_map/ppermute | solution.py:642
  48.2 21.1 %collective-permute-start.9 = (bf16[320,480]{0,1:T(8,128)(2,1)S(1)}, bf16[320,480]{0,1:T(8,128)(2,1)S(1)}, u32[]{:S(2)}, u32[]{:S(2)}) collective-permute-start(bf16[320,480]{0,1:T(8,128)(2,1)S(1)} %slice.404), channel_id=1, source_target_pairs={{0,16},{16,0},{1,17},{17,1},{2,18},{18,2},{3,19},{19,3},{4,20},{20... | collective-permute-start | bytes 921608 | tf_op jit(solution)/shard_map/ppermute | solution.py:652
  48.8 20.5 %collective-permute-start.8 = (bf16[320,480]{0,1:T(8,128)(2,1)S(1)}, bf16[320,480]{0,1:T(8,128)(2,1)S(1)}, u32[]{:S(2)}, u32[]{:S(2)}) collective-permute-start(bf16[320,480]{0,1:T(8,128)(2,1)S(1)} %slice.403), channel_id=1, source_target_pairs={{0,8},{4,12},{8,0},{12,4},{1,9},{5,13},{9,1},{13,5},{2,10},{6,14},... | collective-permute-start | bytes 921608 | tf_op jit(solution)/shard_map/ppermute | solution.py:652
  49.9 22.0 %collective-permute-start.15 = (bf16[320,640]{0,1:T(8,128)(2,1)S(1)}, bf16[320,640]{0,1:T(8,128)(2,1)S(1)}, u32[]{:S(2)}, u32[]{:S(2)}) collective-permute-start(bf16[320,640]{0,1:T(8,128)(2,1)S(1)} %maximum_select_fusion.10), channel_id=1, source_target_pairs={{0,16},{16,0},{1,17},{17,1},{2,18},{18,2},{3,19},{19,3},{4,20},{20... | collective-permute-start | bytes 1228808 | tf_op jit(solution)/shard_map/ppermute | solution.py:652
  60.9 13.2 %collective-permute-start.18 = (bf16[320,640]{0,1:T(8,128)(2,1)S(1)}, bf16[320,640]{0,1:T(8,128)(2,1)S(1)}, u32[]{:S(2)}, u32[]{:S(2)}) collective-permute-start(bf16[320,640]{0,1:T(8,128)(2,1)S(1)} %maximum_select_fusion.10), channel_id=1, source_target_pairs={{0,8},{4,12},{8,0},{12,4},{1,9},{5,13},{9,1},{13,5},{2,10},{6,14},... | collective-permute-start | bytes 1228808 | tf_op jit(solution)/shard_map/ppermute | solution.py:652
  71.9 113.0 %collective-permute-start.16 = (bf16[640,1792]{1,0:T(8,128)(2,1)S(1)}, bf16[640,1792]{1,0:T(8,128)(2,1)S(1)}, u32[]{:S(2)}, u32[]{:S(2)}) collective-permute-start(bf16[640,1792]{1,0:T(8,128)(2,1)S(1)} %maximum_select_fusion.3), channel_id=1, source_target_pairs={{0,16},{16,0},{1,17},{17,1},{2,18},{18,2},{3,19},{19,3},{4,20},{20... | collective-permute-start | bytes 6881288 | tf_op jit(solution)/shard_map/ppermute | solution.py:652
  72.9 15.4 %collective-permute-start.21 = (bf16[160,640]{0,1:T(8,128)(2,1)S(1)}, bf16[160,640]{0,1:T(8,128)(2,1)S(1)}, u32[]{:S(2)}, u32[]{:S(2)}) collective-permute-start(bf16[160,640]{0,1:T(8,128)(2,1)S(1)} %slice.420), channel_id=1, source_target_pairs={{0,8},{4,12},{8,0},{12,4},{1,9},{5,13},{9,1},{13,5},{2,10},{6,14},... | collective-permute-start | bytes 614408 | tf_op jit(solution)/shard_map/ppermute | solution.py:652
  74.0 112.8 %collective-permute-start.19 = (bf16[640,1792]{1,0:T(8,128)(2,1)S(1)}, bf16[640,1792]{1,0:T(8,128)(2,1)S(1)}, u32[]{:S(2)}, u32[]{:S(2)}) collective-permute-start(bf16[640,1792]{1,0:T(8,128)(2,1)S(1)} %maximum_select_fusion.3), channel_id=1, source_target_pairs={{0,8},{4,12},{8,0},{12,4},{1,9},{5,13},{9,1},{13,5},{2,10},{6,14},... | collective-permute-start | bytes 6881288 | tf_op jit(solution)/shard_map/ppermute | solution.py:652
  76.2 52.6 %collective-permute-start.24 = (bf16[160,640]{0,1:T(8,128)(2,1)S(1)}, bf16[160,640]{0,1:T(8,128)(2,1)S(1)}, u32[]{:S(2)}, u32[]{:S(2)}) collective-permute-start(bf16[160,640]{0,1:T(8,128)(2,1)S(1)} %slice.423), channel_id=1, source_target_pairs={{0,16},{16,0},{1,17},{17,1},{2,18},{18,2},{3,19},{19,3},{4,20},{20... | collective-permute-start | bytes 614408 | tf_op jit(solution)/shard_map/ppermute | solution.py:652
  185.0 56.9 %collective-permute-start.22 = (bf16[320,1792]{1,0:T(8,128)(2,1)S(1)}, bf16[320,1792]{1,0:T(8,128)(2,1)}, u32[]{:S(2)}, u32[]{:S(2)}) collective-permute-start(bf16[320,1792]{1,0:T(8,128)(2,1)S(1)} %slice.419), channel_id=1, source_target_pairs={{0,8},{4,12},{8,0},{12,4},{1,9},{5,13},{9,1},{13,5},{2,10},{6,14},... | collective-permute-start | bytes 3440648 | tf_op jit(solution)/shard_map/ppermute | solution.py:652
  188.0 58.8 %collective-permute-start.25 = (bf16[320,1792]{1,0:T(8,128)(2,1)}, bf16[320,1792]{1,0:T(8,128)(2,1)}, u32[]{:S(2)}, u32[]{:S(2)}) collective-permute-start(bf16[320,1792]{1,0:T(8,128)(2,1)} %slice.422), channel_id=1, source_target_pairs={{0,16},{16,0},{1,17},{17,1},{2,18},{18,2},{3,19},{19,3},{4,20},{20... | collective-permute-start | bytes 3440648 | tf_op jit(solution)/shard_map/ppermute | solution.py:652
  188.5 51.5 %collective-permute-start.17 = (bf16[896,640]{0,1:T(8,128)(2,1)}, bf16[896,640]{0,1:T(8,128)(2,1)S(1)}, u32[]{:S(2)}, u32[]{:S(2)}) collective-permute-start(bf16[896,640]{0,1:T(8,128)(2,1)} %maximum_select_fusion.6), channel_id=1, source_target_pairs={{0,16},{16,0},{1,17},{17,1},{2,18},{18,2},{3,19},{19,3},{4,20},{20... | collective-permute-start | bytes 3440648 | tf_op jit(solution)/shard_map/ppermute | solution.py:652
  190.0 54.6 %collective-permute-start.20 = (bf16[896,640]{0,1:T(8,128)(2,1)}, bf16[896,640]{0,1:T(8,128)(2,1)}, u32[]{:S(2)}, u32[]{:S(2)}) collective-permute-start(bf16[896,640]{0,1:T(8,128)(2,1)} %maximum_select_fusion.6), channel_id=1, source_target_pairs={{0,8},{4,12},{8,0},{12,4},{1,9},{5,13},{9,1},{13,5},{2,10},{6,14},... | collective-permute-start | bytes 3440648 | tf_op jit(solution)/shard_map/ppermute | solution.py:652
  244.1 17.1 %collective-permute-start.23 = (bf16[448,640]{1,0:T(8,128)(2,1)}, bf16[448,640]{1,0:T(8,128)(2,1)}, u32[]{:S(2)}, u32[]{:S(2)}) collective-permute-start(bf16[448,640]{1,0:T(8,128)(2,1)} %copy.56), channel_id=1, source_target_pairs={{0,8},{4,12},{8,0},{12,4},{1,9},{5,13},{9,1},{13,5},{2,10},{6,14},... | collective-permute-start | bytes 1720328 | tf_op jit(solution)/shard_map/ppermute | solution.py:652
  249.0 13.9 %collective-permute-start.26 = (bf16[448,640]{1,0:T(8,128)(2,1)}, bf16[448,640]{1,0:T(8,128)(2,1)S(1)}, u32[]{:S(2)}, u32[]{:S(2)}) collective-permute-start(bf16[448,640]{1,0:T(8,128)(2,1)} %copy.57), channel_id=1, source_target_pairs={{0,16},{16,0},{1,17},{17,1},{2,18},{18,2},{3,19},{19,3},{4,20},{20... | collective-permute-start | bytes 1720328 | tf_op jit(solution)/shard_map/ppermute | solution.py:652
  369.9 14.1 %collective-permute-start.27 = (f32[512,160]{0,1:T(8,128)S(1)}, f32[512,160]{0,1:T(8,128)S(1)}, u32[]{:S(2)}, u32[]{:S(2)}) collective-permute-start(f32[512,160]{0,1:T(8,128)S(1)} %fusion.113), channel_id=1, source_target_pairs={{0,8},{4,12},{8,0},{12,4},{1,9},{5,13},{9,1},{13,5},{2,10},{6,14},... | collective-permute-start | bytes 983048 | tf_op jit(solution)/shard_map/ppermute | solution.py:848
  374.6 90.9 %collective-permute-start.36 = (bf16[320,1792]{1,0:T(8,128)(2,1)}, bf16[320,1792]{1,0:T(8,128)(2,1)}, u32[]{:S(2)}, u32[]{:S(2)}) collective-permute-start(bf16[320,1792]{1,0:T(8,128)(2,1)} %get-tuple-element.78), channel_id=1, source_target_pairs={{0,8},{4,12},{8,0},{12,4},{1,9},{5,13},{9,1},{13,5},{2,10},{6,14},... | collective-permute-start | bytes 3440648 | tf_op jit(solution)/shard_map/ppermute | solution.py:652
  375.0 92.2 %collective-permute-start.35 = (bf16[320,1792]{1,0:T(8,128)(2,1)S(1)}, bf16[320,1792]{1,0:T(8,128)(2,1)S(1)}, u32[]{:S(2)}, u32[]{:S(2)}) collective-permute-start(bf16[320,1792]{1,0:T(8,128)(2,1)S(1)} %get-tuple-element.77), channel_id=1, source_target_pairs={{0,16},{16,0},{1,17},{17,1},{2,18},{18,2},{3,19},{19,3},{4,20},{20... | collective-permute-start | bytes 3440648 | tf_op jit(solution)/shard_map/ppermute | solution.py:652
  461.7 28.2 %collective-permute-start.47 = (bf16[320,1792]{1,0:T(8,128)(2,1)S(1)}, bf16[320,1792]{1,0:T(8,128)(2,1)S(1)}, u32[]{:S(2)}, u32[]{:S(2)}) collective-permute-start(bf16[320,1792]{1,0:T(8,128)(2,1)S(1)} %copy-done.47), channel_id=1, source_target_pairs={{0,16},{16,0},{1,17},{17,1},{2,18},{18,2},{3,19},{19,3},{4,20},{20... | collective-permute-start | bytes 3440648 | tf_op jit(solution)/shard_map/ppermute | solution.py:652
  462.5 28.2 %collective-permute-start.45 = (bf16[320,1792]{1,0:T(8,128)(2,1)S(1)}, bf16[320,1792]{1,0:T(8,128)(2,1)S(1)}, u32[]{:S(2)}, u32[]{:S(2)}) collective-permute-start(bf16[320,1792]{1,0:T(8,128)(2,1)S(1)} %copy-done.46), channel_id=1, source_target_pairs={{0,8},{4,12},{8,0},{12,4},{1,9},{5,13},{9,1},{13,5},{2,10},{6,14},... | collective-permute-start | bytes 3440648 | tf_op jit(solution)/shard_map/ppermute | solution.py:652
  465.5 61.4 %collective-permute-start.33 = (f32[2,320]{1,0:T(2,128)S(1)}, f32[2,320]{1,0:T(2,128)S(1)}, u32[]{:S(2)}, u32[]{:S(2)}) collective-permute-start(f32[2,320]{1,0:T(2,128)S(1)} %fusion.142), channel_id=1, source_target_pairs={{0,1},{1,0},{2,3},{3,2},{4,5},{5,4},{6,7},{7,6},{8,9},{9,8},{10,11... | collective-permute-start | bytes 7688 | tf_op jit(solution)/shard_map/ppermute | solution.py:882
  467.2 72.9 %collective-permute-start.40 = (bf16[320,1792]{1,0:T(8,128)(2,1)S(1)}, bf16[320,1792]{1,0:T(8,128)(2,1)S(1)}, u32[]{:S(2)}, u32[]{:S(2)}) collective-permute-start(bf16[320,1792]{1,0:T(8,128)(2,1)S(1)} %fusion.16), channel_id=1, source_target_pairs={{0,16},{16,0},{1,17},{17,1},{2,18},{18,2},{3,19},{19,3},{4,20},{20... | collective-permute-start | bytes 3440648 | tf_op jit(solution)/shard_map/ppermute | solution.py:652
  489.9 33.0 %collective-permute-start.48 = (bf16[448,640]{1,0:T(8,128)(2,1)S(1)}, bf16[448,640]{1,0:T(8,128)(2,1)S(1)}, u32[]{:S(2)}, u32[]{:S(2)}) collective-permute-start(bf16[448,640]{1,0:T(8,128)(2,1)S(1)} %copy-done.60), channel_id=1, source_target_pairs={{0,16},{16,0},{1,17},{17,1},{2,18},{18,2},{3,19},{19,3},{4,20},{20... | collective-permute-start | bytes 1720328 | tf_op jit(solution)/shard_map/ppermute | solution.py:652
  490.7 32.4 %collective-permute-start.46 = (bf16[448,640]{1,0:T(8,128)(2,1)S(1)}, bf16[448,640]{1,0:T(8,128)(2,1)S(1)}, u32[]{:S(2)}, u32[]{:S(2)}) collective-permute-start(bf16[448,640]{1,0:T(8,128)(2,1)S(1)} %copy-done.59), channel_id=1, source_target_pairs={{0,8},{4,12},{8,0},{12,4},{1,9},{5,13},{9,1},{13,5},{2,10},{6,14},... | collective-permute-start | bytes 1720328 | tf_op jit(solution)/shard_map/ppermute | solution.py:652
  492.7 47.5 %collective-permute-start.37 = (bf16[320,1792]{1,0:T(8,128)(2,1)S(1)}, bf16[320,1792]{1,0:T(8,128)(2,1)S(1)}, u32[]{:S(2)}, u32[]{:S(2)}) collective-permute-start(bf16[320,1792]{1,0:T(8,128)(2,1)S(1)} %fusion.17), channel_id=1, source_target_pairs={{0,8},{4,12},{8,0},{12,4},{1,9},{5,13},{9,1},{13,5},{2,10},{6,14},... | collective-permute-start | bytes 3440648 | tf_op jit(solution)/shard_map/ppermute | solution.py:652
  523.1 12.1 %collective-permute-start.52 = (bf16[448,640]{1,0:T(8,128)(2,1)S(1)}, bf16[448,640]{1,0:T(8,128)(2,1)S(1)}, u32[]{:S(2)}, u32[]{:S(2)}) collective-permute-start(bf16[448,640]{1,0:T(8,128)(2,1)S(1)} %fusion.37), channel_id=1, source_target_pairs={{0,8},{4,12},{8,0},{12,4},{1,9},{5,13},{9,1},{13,5},{2,10},{6,14},... | collective-permute-start | bytes 1720328 | tf_op jit(solution)/shard_map/ppermute | solution.py:652
  524.0 13.3 %collective-permute-start.49 = (bf16[448,640]{1,0:T(8,128)(2,1)S(1)}, bf16[448,640]{1,0:T(8,128)(2,1)S(1)}, u32[]{:S(2)}, u32[]{:S(2)}) collective-permute-start(bf16[448,640]{1,0:T(8,128)(2,1)S(1)} %fusion.38), channel_id=1, source_target_pairs={{0,16},{16,0},{1,17},{17,1},{2,18},{18,2},{3,19},{19,3},{4,20},{20... | collective-permute-start | bytes 1720328 | tf_op jit(solution)/shard_map/ppermute | solution.py:652
  540.1 20.7 %collective-permute-start.41 = (bf16[448,640]{1,0:T(8,128)(2,1)S(1)}, bf16[448,640]{1,0:T(8,128)(2,1)S(1)}, u32[]{:S(2)}, u32[]{:S(2)}) collective-permute-start(bf16[448,640]{1,0:T(8,128)(2,1)S(1)} %copy-done.65), channel_id=1, source_target_pairs={{0,16},{16,0},{1,17},{17,1},{2,18},{18,2},{3,19},{19,3},{4,20},{20... | collective-permute-start | bytes 1720328 | tf_op jit(solution)/shard_map/ppermute | solution.py:652
  540.2 22.8 %collective-permute-start.38 = (bf16[448,640]{1,0:T(8,128)(2,1)S(1)}, bf16[448,640]{1,0:T(8,128)(2,1)S(1)}, u32[]{:S(2)}, u32[]{:S(2)}) collective-permute-start(bf16[448,640]{1,0:T(8,128)(2,1)S(1)} %copy-done.66), channel_id=1, source_target_pairs={{0,8},{4,12},{8,0},{12,4},{1,9},{5,13},{9,1},{13,5},{2,10},{6,14},... | collective-permute-start | bytes 1720328 | tf_op jit(solution)/shard_map/ppermute | solution.py:652
  543.9 69.7 %collective-permute-start.61 = (f32[320,1792]{1,0:T(8,128)}, f32[320,1792]{1,0:T(8,128)}, u32[]{:S(2)}, u32[]{:S(2)}) collective-permute-start(f32[320,1792]{1,0:T(8,128)} %get-tuple-element.139), channel_id=1, source_target_pairs={{0,4},{4,0},{8,12},{12,8},{1,5},{5,1},{9,13},{13,9},{2,6},{6,2},{1... | collective-permute-start | bytes 6881288 | tf_op jit(solution)/shard_map/ppermute | solution.py:642
  543.9 14.0 %collective-permute-start.54 = (bf16[320,480]{0,1:T(8,128)(2,1)S(1)}, bf16[320,480]{0,1:T(8,128)(2,1)S(1)}, u32[]{:S(2)}, u32[]{:S(2)}) collective-permute-start(bf16[320,480]{0,1:T(8,128)(2,1)S(1)} %get-tuple-element.96), channel_id=1, source_target_pairs={{0,8},{4,12},{8,0},{12,4},{1,9},{5,13},{9,1},{13,5},{2,10},{6,14},... | collective-permute-start | bytes 921608 | tf_op jit(solution)/shard_map/ppermute | solution.py:652
  545.9 12.9 %collective-permute-start.51 = (bf16[320,480]{0,1:T(8,128)(2,1)S(1)}, bf16[320,480]{0,1:T(8,128)(2,1)S(1)}, u32[]{:S(2)}, u32[]{:S(2)}) collective-permute-start(bf16[320,480]{0,1:T(8,128)(2,1)S(1)} %get-tuple-element.93), channel_id=1, source_target_pairs={{0,16},{16,0},{1,17},{17,1},{2,18},{18,2},{3,19},{19,3},{4,20},{20... | collective-permute-start | bytes 921608 | tf_op jit(solution)/shard_map/ppermute | solution.py:652
  558.8 24.7 %collective-permute-start.56 = (bf16[320,480]{0,1:T(8,128)(2,1)}, bf16[320,480]{0,1:T(8,128)(2,1)}, u32[]{:S(2)}, u32[]{:S(2)}) collective-permute-start(bf16[320,480]{0,1:T(8,128)(2,1)} %fusion.41), channel_id=1, source_target_pairs={{0,16},{16,0},{1,17},{17,1},{2,18},{18,2},{3,19},{19,3},{4,20},{20... | collective-permute-start | bytes 921608 | tf_op jit(solution)/shard_map/ppermute | solution.py:652
  560.8 11.3 %collective-permute-start.42 = (bf16[160,640]{1,0:T(8,128)(2,1)S(1)}, bf16[160,640]{1,0:T(8,128)(2,1)S(1)}, u32[]{:S(2)}, u32[]{:S(2)}) collective-permute-start(bf16[160,640]{1,0:T(8,128)(2,1)S(1)} %copy-done.76), channel_id=1, source_target_pairs={{0,16},{16,0},{1,17},{17,1},{2,18},{18,2},{3,19},{19,3},{4,20},{20... | collective-permute-start | bytes 614408 | tf_op jit(solution)/shard_map/ppermute | solution.py:652
  561.7 26.1 %collective-permute-start.55 = (bf16[320,480]{0,1:T(8,128)(2,1)}, bf16[320,480]{0,1:T(8,128)(2,1)}, u32[]{:S(2)}, u32[]{:S(2)}) collective-permute-start(bf16[320,480]{0,1:T(8,128)(2,1)} %fusion.43), channel_id=1, source_target_pairs={{0,8},{4,12},{8,0},{12,4},{1,9},{5,13},{9,1},{13,5},{2,10},{6,14},... | collective-permute-start | bytes 921608 | tf_op jit(solution)/shard_map/ppermute | solution.py:652
  563.1 11.7 %collective-permute-start.39 = (bf16[160,640]{1,0:T(8,128)(2,1)S(1)}, bf16[160,640]{1,0:T(8,128)(2,1)S(1)}, u32[]{:S(2)}, u32[]{:S(2)}) collective-permute-start(bf16[160,640]{1,0:T(8,128)(2,1)S(1)} %copy-done.75), channel_id=1, source_target_pairs={{0,8},{4,12},{8,0},{12,4},{1,9},{5,13},{9,1},{13,5},{2,10},{6,14},... | collective-permute-start | bytes 614408 | tf_op jit(solution)/shard_map/ppermute | solution.py:652
  581.9 18.3 %collective-permute-start.62 = (f32[896,320]{0,1:T(8,128)}, f32[896,320]{0,1:T(8,128)}, u32[]{:S(2)}, u32[]{:S(2)}) collective-permute-start(f32[896,320]{0,1:T(8,128)} %copy.67), channel_id=1, source_target_pairs={{0,4},{4,0},{8,12},{12,8},{1,5},{5,1},{9,13},{13,9},{2,6},{6,2},{1... | collective-permute-start | bytes 3440648 | tf_op jit(solution)/shard_map/ppermute | solution.py:642
  582.9 10.3 %collective-permute-start.58 = (bf16[320,480]{0,1:T(8,128)(2,1)}, bf16[320,480]{0,1:T(8,128)(2,1)S(1)}, u32[]{:S(2)}, u32[]{:S(2)}) collective-permute-start(bf16[320,480]{0,1:T(8,128)(2,1)} %slice.687), channel_id=1, source_target_pairs={{0,8},{4,12},{8,0},{12,4},{1,9},{5,13},{9,1},{13,5},{2,10},{6,14},... | collective-permute-start | bytes 921608 | tf_op jit(solution)/shard_map/ppermute | solution.py:652
  583.6 10.4 %collective-permute-start.44 = (bf16[320,480]{0,1:T(8,128)(2,1)}, bf16[320,480]{0,1:T(8,128)(2,1)S(1)}, u32[]{:S(2)}, u32[]{:S(2)}) collective-permute-start(bf16[320,480]{0,1:T(8,128)(2,1)} %slice.688), channel_id=1, source_target_pairs={{0,16},{16,0},{1,17},{17,1},{2,18},{18,2},{3,19},{19,3},{4,20},{20... | collective-permute-start | bytes 921608 | tf_op jit(solution)/shard_map/ppermute | solution.py:652
  587.9 9.9 %collective-permute-start.60 = (f32[320,320]{1,0:T(8,128)}, f32[320,320]{1,0:T(8,128)}, u32[]{:S(2)}, u32[]{:S(2)}) collective-permute-start(f32[320,320]{1,0:T(8,128)} %get-tuple-element.184), channel_id=1, source_target_pairs={{0,4},{4,0},{8,12},{12,8},{1,5},{5,1},{9,13},{13,9},{2,6},{6,2},{1... | collective-permute-start | bytes 1228808 | tf_op jit(solution)/shard_map/ppermute | solution.py:642
  597.7 10.4 %collective-permute-start.59 = (f32[320,480]{1,0:T(8,128)}, f32[320,480]{1,0:T(8,128)}, u32[]{:S(2)}, u32[]{:S(2)}) collective-permute-start(f32[320,480]{1,0:T(8,128)} %copy.63), channel_id=1, source_target_pairs={{0,4},{4,0},{8,12},{12,8},{1,5},{5,1},{9,13},{13,9},{2,6},{6,2},{1... | collective-permute-start | bytes 1843208 | tf_op jit(solution)/shard_map/ppermute | solution.py:642
  (100 other events, 1528.7 us)

commit v3 on v2

--- a/solution.py
+++ b/solution.py
@@ -324,6 +324,7 @@
         self.step = width // SPLIT
         self.sibling = (self.x, self.ctx + 1 - 2 * self.core, self.z)
         self.above, self.below = (self.x, self.ctx, self.z + 1), (self.x, self.ctx, self.z - 1)
+        self.neighbours = (self.sibling,)
 
     def enter(self):
         barrier = pltpu.get_barrier_semaphore()
@@ -333,7 +334,8 @@
                 barrier, inc=1, device_id=device, device_id_type=pl.DeviceIdType.MESH
             )
 
-        greet(self.sibling)
+        for device in self.neighbours:
+            greet(device)
 
         @pl.when(self.z < self.last)
         def _():
@@ -344,7 +346,7 @@
             greet(self.below)
 
         ends = jnp.where(self.z == 0, 1, 0) + jnp.where(self.z == self.last, 1, 0)
-        pl.semaphore_wait(barrier, 3 - ends)
+        pl.semaphore_wait(barrier, len(self.neighbours) + 2 - ends)
 
     def place(self, core, block):
         return pl.ds(pl.multiple_of(core * self.rows + block * self.owned, 16), self.owned)
@@ -550,49 +552,471 @@
     return sems + ([pltpu.SemaphoreType.DMA((2, z_count))] if cores else [])
 
 
-def branch_kernel(part, inputs, gain, whole, middle, *scratch):
-    col = Column(inputs.shape[0], inputs.shape[1])
-    total = SumChain(col, part, *scratch[:8])
-    share = ShareChain(col, whole, *scratch[8:])
-    col.enter()
+GROUP = 384
+
+
+class Plane(Column):
+    def __init__(self, owned, width):
+        super().__init__(owned, width)
+        self.over_x = (1 - self.x, self.ctx, self.z)
+        self.over_y = (self.x, lax.rem(self.ctx + 2, 4), self.z)
+        self.part = width // 4
+        self.middle = width // 8
+
+        self.neighbours = (self.sibling, self.over_x, self.over_y)
+
+
+def start_kernel(
+    hidden,
+    gains,
+    keep,
+    give,
+    gate,
+    up,
+    down,
+    output,
+    qkv,
+    h1,
+    w,
+    gains_all,
+    out_own,
+    wide,
+    down_t,
+    out_t,
+    core_sem,
+    gain_sem,
+    x_sem,
+    y_sem,
+    far_sem,
+    local_sem,
+    wide_sem,
+    out_sem,
+    h1_sem,
+):
+    x_at, ctx_at, z_at = (lax.axis_index(name) for name in ("dp", "ctx", "mp"))
+    core = lax.rem(ctx_at, 2)
+    y_at = (ctx_at - core) // 2
+    rows, part = hidden.shape[0], keep.shape[0]
+    chip_part = 2 * part
+    ff = gate.shape[1] // 2
+    groups = ff // 128
+
+    def device(turn, flip):
+        x_to = 1 - x_at if turn >= 2 else x_at
+        y_to = 1 - y_at if turn % 2 else y_at
+        core_to = 1 - core if flip else core
+        return (x_to, 2 * y_to + core_to, z_at)
+
+    def half_rows(which):
+        return pl.ds(pl.multiple_of(which * part, 16), part)
+
+    sibling, over_x, over_y = device(0, 1), device(2, 0), device(1, 0)
+    barrier = pltpu.get_barrier_semaphore()
+    others = [(turn, flip) for turn in range(4) for flip in range(2) if turn or flip]
+    for turn, flip in others:
+        pl.semaphore_signal(
+            barrier, inc=1, device_id=device(turn, flip), device_id_type=pl.DeviceIdType.MESH
+        )
+    w[0, half_rows(core)] = keep[...]
+    gains_all[core] = gains[...]
+    pl.semaphore_wait(barrier, len(others))
+
+    mine = half_rows(core)
+    swap = remote(give, w.at[0, mine], core_sem.at[0], core_sem.at[1], sibling)
+    swap.start()
+
+    def gain_copy(turn, flip):
+        slot = 2 * turn + core
+        index = 2 * turn + flip
+        return remote(
+            gains, gains_all.at[slot], gain_sem.at[0, index], gain_sem.at[1, index], device(turn, flip)
+        )
+
+    for turn, flip in others:
+        gain_copy(turn, flip).start()
+
+    def cross(which, to_x):
+        sem = x_sem if to_x else y_sem
+        rows_of = half_rows(which)
+        return remote(
+            w.at[0, rows_of],
+            w.at[2 if to_x else 1, rows_of],
+            sem.at[0, which],
+            sem.at[1, which],
+            over_x if to_x else over_y,
+        )
+
+    cross(core, True).start()
+    cross(core, False).start()
+
+    def wide_copies(group, kind, source):
+        from_here = pl.ds(pl.multiple_of(core * ff + group * 128, 128), 128)
+        from_there = pl.ds(pl.multiple_of((1 - core) * ff + group * 128, 128), 128)
+        to = pl.ds(pl.multiple_of(group * GROUP + kind * 128, 128), 128)
+        here = pltpu.make_async_copy(
+            source.at[:, from_here], wide.at[mine, to], local_sem.at[kind, group]
+        )
+        there = remote(
+            source.at[:, from_there],
+            wide.at[mine, to],
+            wide_sem.at[0, kind, group],
+            wide_sem.at[1, kind, group],
+            sibling,
+        )
+        return here, there
+
+    def each_wide(kind, source, act):
+        def body(group, carry):
+            for copy in wide_copies(group, kind, source):
+                act(copy)
+            return carry
+
+        lax.fori_loop(0, groups, body, 0)
+
+    each_wide(0, gate, lambda copy: copy.start())
+    each_wide(1, up, lambda copy: copy.start())
+    swap.wait_recv()
+    cross(1 - core, True).start()
+    cross(1 - core, False).start()
+
+    down_t[...] = down[...].T
+    each_wide(2, down_t, lambda copy: copy.start())
+    q_rows = output.shape[0] // 2
+    out_own[mine, q_rows:] = jnp.zeros((part, out_own.shape[1] - q_rows), out_own.dtype)
+    out_t[:, q_rows:] = jnp.zeros((part, out_own.shape[1] - q_rows), out_own.dtype)
+    out_own[mine, :q_rows] = output[pl.ds(pl.multiple_of(core * q_rows, 16), q_rows), :].T
+    out_t[:, :q_rows] = output[pl.ds(pl.multiple_of((1 - core) * q_rows, 16), q_rows), :].T
+    out_copy = remote(out_t, out_own.at[mine], out_sem.at[0], out_sem.at[1], sibling)
+    out_copy.start()
+
+    for turn, flip in others:
+        gain_copy(turn, flip).wait_recv()
+    place = 2 * x_at + y_at
+    squares = hidden[...].astype(jnp.float32)
+    scale = lax.rsqrt(jnp.mean(squares * squares, axis=-1, keepdims=True) + EPS)
+    my_rows = pl.ds(pl.multiple_of(core * rows, 16), rows)
+    for turn in range(4):
+        at = (x_at if turn < 2 else 1 - x_at) * 2 + (1 - y_at if turn % 2 else y_at)
+        block = hidden[:, pl.ds(pl.multiple_of(at * chip_part, 128), chip_part)]
+        gain = gains_all[2 * turn] + gains_all[2 * turn + 1]
+        h1[my_rows, turn * chip_part : (turn + 1) * chip_part] = (
+            block.astype(jnp.float32) * scale * gain[:1]
+        ).astype(h1.dtype)
+    h1_copy = remote(h1.at[my_rows], h1.at[my_rows], h1_sem.at[0], h1_sem.at[1], sibling)
+    h1_copy.start()
+
+    def relay(to_x):
+        which = 1 if to_x else 0
+        rows_of = half_rows(which)
+        return remote(
+            w.at[1 if to_x else 2, rows_of],
+            w.at[3, rows_of],
+            far_sem.at[0, which],
+            far_sem.at[1, which],
+            over_x if to_x else over_y,
+        )
+
+    def block_dot(turn):
+        left = h1[:, turn * chip_part : (turn + 1) * chip_part]
+        return jnp.dot(left, w[turn], preferred_element_type=jnp.float32)
+
+    cross(0, True).wait_recv()
+    relay(False).start()
+    cross(1, False).wait_recv()
+    relay(True).start()
+    h1_copy.wait_recv()
+    qkv[...] = block_dot(0)
+    cross(1, True).wait_recv()
+    qkv[...] += block_dot(2)
+    cross(0, False).wait_recv()
+    qkv[...] += block_dot(1)
+    relay(False).wait_recv()
+    relay(True).wait_recv()
+    qkv[...] += block_dot(3)
+
+    for kind, source in enumerate((gate, up, down_t)):
+        each_wide(kind, source, lambda copy: copy.wait())
+    swap.wait_send()
+    out_copy.wait()
+    h1_copy.wait_send()
+    for turn, flip in others:
+        gain_copy(turn, flip).wait_send()
+    for which in range(2):
+        for to_x in (True, False):
+            cross(which, to_x).wait_send()
+    relay(True).wait_send()
+    relay(False).wait_send()
+
+
+class Gather:
+    def __init__(self, plane, own, w, x_sem, y_sem, far_sem, local_sem):
+        self.plane, self.own, self.w = plane, own, w
+        self.x_sem, self.y_sem, self.far_sem, self.local_sem = x_sem, y_sem, far_sem, local_sem
+        self.groups = own.shape[1] // GROUP
+
+    def columns(self, group):
+        return pl.ds(pl.multiple_of(group * GROUP, 128), GROUP)
+
+    def cross(self, group, to_x):
+        plane, cols = self.plane, self.columns(group)
+        sem = self.x_sem if to_x else self.y_sem
+        return remote(
+            self.own.at[:, cols],
+            self.w.at[2 if to_x else 1, :, cols],
+            sem.at[0, group],
+            sem.at[1, group],
+            plane.over_x if to_x else plane.over_y,
+        )
+
+    def relay(self, group, to_x):
+        plane, cols = self.plane, self.columns(group)
+        rows = pl.ds(plane.middle, plane.middle) if to_x else pl.ds(0, plane.middle)
+        kind = 1 if to_x else 0
+        return remote(
+            self.w.at[1 if to_x else 2, rows, cols],
+            self.w.at[3, rows, cols],
+            self.far_sem.at[0, kind, group],
+            self.far_sem.at[1, kind, group],
+            plane.over_x if to_x else plane.over_y,
+        )
+
+    def load(self):
+        return pltpu.make_async_copy(self.own, self.w.at[0], self.local_sem.at[0])
+
+    def send(self, group):
+        self.cross(group, True).start()
+        self.cross(group, False).start()
+
+    def pump(self, group):
+        self.cross(group, True).wait_recv()
+        self.relay(group, False).start()
+        self.cross(group, False).wait_recv()
+        self.relay(group, True).start()
+
+        @pl.when(group + 2 < self.groups)
+        def _():
+            self.send(group + 2)
+
+    def arrive(self, group):
+        self.relay(group, False).wait_recv()
+        self.relay(group, True).wait_recv()
+
+    def drain(self):
+        def body(group, carry):
+            for to_x in (True, False):
+                self.cross(group, to_x).wait_send()
+                self.relay(group, to_x).wait_send()
+            return carry
+
+        lax.fori_loop(0, self.groups, body, 0)
+
+
+class Scatter:
+    def __init__(self, plane, stage, upper, lower, x_one, y_two, sem):
+        self.plane, self.stage, self.sem = plane, stage, sem
+        first, second = pl.ds(0, plane.middle), pl.ds(plane.middle, plane.middle)
+        self.kinds = (
+            (2, first, upper, plane.over_x),
+            (2, second, lower, plane.over_y),
+            (1, first, x_one, plane.over_x),
+            (0, second, y_two, plane.over_y),
+        )
+
+    def copies(self, group):
+        cols = pl.ds(pl.multiple_of(group * GROUP, 128), GROUP)
+        for kind, (block, rows, into, device) in enumerate(self.kinds):
+            yield remote(
+                self.stage.at[block, rows, cols],
+                into.at[:, cols],
+                self.sem.at[0, kind, group],
+                self.sem.at[1, kind, group],
+                device,
+            )
+
+    def send(self, group):
+        for copy in self.copies(group):
+            copy.start()
+
+    def drain(self, groups):
+        def body(group, carry):
+            for copy in self.copies(group):
+                copy.wait()
+            return carry
+
+        lax.fori_loop(0, groups, body, 0)
+
+
+NT = (((1,), (1,)), ((), ()))
+
+
+def mlp_kernel(
+    branch,
+    inputs,
+    gain,
+    dout,
+    valid,
+    dm,
+    own,
+    da,
+    d_middle,
+    layer,
+    d_gain,
+    own_grad,
+    stage,
+    upper,
+    lower,
+    x_one,
+    y_two,
+    w,
+    h2,
+    h2_t,
+    dm_t,
+    part,
+    mlp_part,
+    dh2,
+    middle,
+    mlp,
+    zd,
+    tile,
+    tile_own,
+    x_sem,
+    y_sem,
+    far_sem,
+    local_sem,
+    scatter_sem,
+    *scratch,
+):
+    f32 = jnp.float32
+    plane = Plane(inputs.shape[0], inputs.shape[1])
+    size = plane.part
+    gather = Gather(plane, own, w, x_sem, y_sem, far_sem, local_sem)
+    groups = gather.groups
+    scatter = Scatter(plane, stage, upper, lower, x_one, y_two, scatter_sem)
+    total = SumChain(plane, part, *scratch[:8])
+    share = ShareChain(plane, h2, *scratch[8:11])
+    total_back = SumChain(plane, part, *scratch[11:19])
+    second = SumChain(plane, mlp_part, *scratch[:5], *scratch[19:22])
+    share_back = ShareChain(plane, da, *scratch[22:25])
+
+    def cut(turn):
+        return slice(turn * size, (turn + 1) * size)
+
+    load_part = pltpu.make_async_copy(branch, part, local_sem.at[1])
+    load_part.start()
+    gather.load().start()
+    load_part.wait()
+    plane.enter()
     total.open()
-    for step in range(col.last):
+    gather.send(0)
+    gather.send(1)
+    for step in range(plane.last):
         total.step(step)
+        if step == 0:
+            for turn in range(4):
+                dm_t[cut(turn)] = dm[:, cut(turn)].T
     total.close(middle)
     middle[...] += inputs[...]
-    whole[col.place(col.core, col.z)] = normed(middle[...], gain[...]).astype(whole.dtype)
-    for step in range(col.last + 1):
+    h2[plane.place(plane.core, plane.z)] = normed(middle[...], gain[...]).astype(h2.dtype)
+    gather.pump(0)
+    for step in range(plane.last + 1):
         share.step(step)
+        if step == 1:
+            gather.pump(1)
+        if step == plane.last:
+            gather.pump(2)
     total.drain()
     share.drain()
-
-
-def middle_kernel(
-    part, mlp_part, middle, gain, dout, valid, whole, d_middle, layer, d_gain, mlp, *scratch
-):
-    col = Column(middle.shape[0], middle.shape[1])
-    total = SumChain(col, part, *scratch[:8])
-    second = SumChain(col, mlp_part, *scratch[8:16])
-    share = ShareChain(col, whole, *scratch[16:])
-    col.enter()
-    total.open()
+    for turn in range(4):
+        h2_t[cut(turn)] = h2[:, cut(turn)].T
+    dh2[...] = jnp.zeros_like(dh2)
+    gather.load().wait()
+
+    def group_body(group, carry):
+        start = pl.multiple_of(group * GROUP, 128)
+        gu_cols, down_cols = pl.ds(start, 256), pl.ds(start + 256, 128)
+        cols = pl.ds(start, GROUP)
+        gather.arrive(group)
+        gu = jnp.zeros((dm.shape[0], 256), f32)
+        d_hidden = jnp.zeros((dm.shape[0], 128), f32)
+        for turn in range(4):
+            gu += jnp.dot(h2[:, cut(turn)], w[turn, :, gu_cols], preferred_element_type=f32)
+            d_hidden += jnp.dot(dm[:, cut(turn)], w[turn, :, down_cols], preferred_element_type=f32)
+        gate, up = gu[:, :128], gu[:, 128:]
+        sigma = jax.nn.sigmoid(gate)
+        silu = gate * sigma
+        zd[:, pl.ds(start, 128)] = (
+            d_hidden * up * sigma * (1.0 + gate * (1.0 - sigma))
+        ).astype(zd.dtype)
+        zd[:, pl.ds(start + 128, 128)] = (d_hidden * silu).astype(zd.dtype)
+        zd[:, down_cols] = (silu * up).astype(zd.dtype)
+        d_gu, hidden = zd[:, gu_cols], zd[:, down_cols]
+        for turn in range(4):
+            dh2[:, cut(turn)] += lax.dot_general(
+                d_gu, w[turn, :, gu_cols], NT, preferred_element_type=f32
+            )
+            grad_gu = jnp.dot(h2_t[cut(turn)], d_gu, preferred_element_type=f32)
+            grad_down = jnp.dot(dm_t[cut(turn)], hidden, preferred_element_type=f32)
+            if turn:
+                tile[turn - 1, :, :256] = grad_gu.astype(tile.dtype)
+                tile[turn - 1, :, 256:] = grad_down.astype(tile.dtype)
+            else:
+                tile_own[:, :256] = grad_gu
+                tile_own[:, 256:] = grad_down
+        keep = pltpu.make_async_copy(tile, stage.at[:, :, cols], local_sem.at[2])
+        keep_own = pltpu.make_async_copy(tile_own, own_grad.at[:, cols], local_sem.at[3])
+        keep.start()
+        keep_own.start()
+
+        @pl.when(group + 3 < groups)
+        def _():
+            gather.pump(group + 3)
+
+        keep.wait()
+        keep_own.wait()
+
+        @pl.when(group == 3)
+        def _():
+            for before in range(3):
+                scatter.send(before)
+
+        @pl.when(group >= 3)
+        def _():
+            scatter.send(group)
+
+        return carry
+
+    lax.fori_loop(0, groups, group_body, 0)
+    for turn in range(4):
+        part[:, cut(turn)] = dh2[:, cut(turn)].astype(part.dtype)
+    total_back.open()
+    for step in range(plane.last):
+        total_back.step(step)
+        for turn in range(4):
+            if turn % plane.last == step:
+                out = jnp.zeros((dm.shape[0], size), f32)
+                for group in range(groups):
+                    cols = slice(group * GROUP + 256, group * GROUP + 384)
+                    out += lax.dot_general(
+                        zd[:, cols], w[turn, :, cols], NT, preferred_element_type=f32
+                    )
+                mlp_part[:, cut(turn)] = out.astype(mlp_part.dtype)
     second.open()
-    for step in range(col.last):
-        total.step(step)
-    total.close(d_middle)
+    total_back.close(d_middle)
     d_norm, d_gain_row = norm_back(middle[...], gain[...], d_middle[...])
     d_gain[...] = d_gain_row[None]
     d_middle[...] = dout[...] + d_norm
-    whole[col.place(col.core, col.z)] = d_middle[...].astype(whole.dtype)
-    for step in range(col.last + 1):
-        share.step(step)
-        if step < col.last:
+    da[plane.place(plane.core, plane.z)] = d_middle[...].astype(da.dtype)
+    for step in range(plane.last + 1):
+        share_back.step(step)
+        if step < plane.last:
             second.step(step)
     second.close(mlp)
     layer[...] = (valid[...] * (middle[...] + mlp[...])).astype(layer.dtype)
-    total.drain()
+    total_back.drain()
     second.drain()
-    share.drain()
+    share_back.drain()
+    gather.drain()
+    scatter.drain(groups)
 
 
 def input_kernel(
@@ -672,7 +1096,7 @@
     f32 = jnp.float32
     _, rows, width = hidden_in.shape
     part = w_query.shape[0]
-    chip_part = 2 * part
+    chip_part, chip_rows = 2 * part, 2 * rows
     x_at, ctx_at, z_at = lax.axis_index("dp"), lax.axis_index("ctx"), lax.axis_index("mp")
     y_at, core = ctx_at // 2, ctx_at % 2
     first = core == 0
@@ -704,10 +1128,8 @@
     def cut(tensor, turn):
         return tensor[..., turn * chip_part : (turn + 1) * chip_part]
 
-    def chip_block(pieces, split_axis, join_axis):
-        keep = jnp.concatenate([half(piece, core, split_axis) for piece in pieces], axis=1)
-        give = jnp.concatenate([half(piece, 1 - core, split_axis) for piece in pieces], axis=1)
-        return both(keep, over_core(give), join_axis)
+    def after(tensor, other):
+        return lax.optimization_barrier((tensor, other))[0]
 
     def gather(block):
         middle = block.shape[0] // 2
@@ -717,15 +1139,28 @@
         lower = x_link.send(from_y[middle:])
         return [block, from_y, from_x, jnp.concatenate([upper, lower], axis=0)]
 
-    def scatter(parts):
-        own, for_y, for_x, for_far = parts
-        middle = own.shape[0] // 2
+    def scatter_first(parts):
+        _, for_y, for_x, for_far = parts
+        middle = for_far.shape[0] // 2
         upper = x_link.send(for_far[:middle].astype(low))
         lower = y_link.send(for_far[middle:].astype(low))
         x_one = x_link.send(for_x[:middle].astype(low))
         y_two = y_link.send(for_y[middle:].astype(low))
-        y_one = y_link.send((for_y[:middle] + upper.astype(f32)).astype(low))
-        x_two = x_link.send((for_x[middle:] + lower.astype(f32)).astype(low))
+        return upper, lower, x_one, y_two
+
+    def scatter_second(parts, came):
+        _, for_y, for_x, _ = parts
+        middle = for_y.shape[0] // 2
+        upper, lower, _, _ = came
+        y_one = y_link.send((for_y[:middle].astype(f32) + upper.astype(f32)).astype(low))
+        x_two = x_link.send((for_x[middle:].astype(f32) + lower.astype(f32)).astype(low))
+        return y_one, x_two
+
+    def scatter_end(parts, came, last):
+        own = parts[0]
+        middle = own.shape[0] // 2
+        _, _, x_one, y_two = came
+        y_one, x_two = last
         return jnp.concatenate(
             [
                 own[:middle] + x_one.astype(f32) + y_one.astype(f32),
@@ -742,41 +1177,83 @@
 
     nn, nt, tn = ((1,), (0,)), ((1,), (1,)), ((0,), (0,))
 
-    gains = both(*(lambda g: (g, over_core(g)))(jnp.stack([norm_attn, norm_mlp])), 1)
-    gains_x = lax.ppermute(gains, "dp", X_SWAP)
-    gains_y = lax.ppermute(gains, "ctx", Y_SWAP)
-    gains_far = lax.ppermute(gains_x, "ctx", Y_SWAP)
-    gains_all = jnp.concatenate([gains, gains_y, gains_x, gains_far], axis=1).astype(f32)
-    gain_one, gain_two = gains_all[0], gains_all[1]
-
-    qkv_w = gather(chip_block((w_query, w_key, w_value), 1, 0))
-    out_w = gather(chip_block((w_output,), 0, 1))
-    gu_w = gather(chip_block((w_gate, w_up), 1, 0))
-    down_w = gather(chip_block((w_down,), 0, 1))
+    heads = w_query.shape[1] // HEAD // 2
+    kv_heads = w_key.shape[1] // HEAD // 2
+    group = heads // kv_heads
+    q_cols, k_cols = heads * HEAD, kv_heads * HEAD
+    qkv_cols = q_cols + 2 * k_cols
+    ff = w_gate.shape[1] // 2
+
+    def lanes(count):
+        return -(-count // 128) * 128
+
+    def qkv_half(which):
+        pieces = [half(weight, which, 1) for weight in (w_query, w_key, w_value)]
+        pad = jnp.zeros((part, lanes(qkv_cols) - qkv_cols), low)
+        return jnp.concatenate(pieces + [pad], axis=1)
+
+    gains = jnp.zeros((8, chip_part), f32)
+    gain_rows = jnp.stack([norm_attn, norm_mlp]).astype(f32)
+    gains = lax.dynamic_update_slice(gains, gain_rows, (0, core * part))
+
+    any_space = pl.BlockSpec(memory_space=pl.ANY)
+    vmem = pl.BlockSpec(memory_space=pltpu.VMEM)
+    wide_cols = 3 * ff
+    groups = wide_cols // GROUP
+    dma = pltpu.SemaphoreType.DMA
+    qkv, h1, qkv_w, gains_all, out_own, wide = pl.pallas_call(
+        start_kernel,
+        out_shape=[
+            jax.ShapeDtypeStruct((chip_rows, lanes(qkv_cols)), f32),
+            jax.ShapeDtypeStruct((chip_rows, width), low),
+            jax.ShapeDtypeStruct((4, chip_part, lanes(qkv_cols)), low),
+            jax.ShapeDtypeStruct((8, 8, chip_part), f32),
+            jax.ShapeDtypeStruct((chip_part, lanes(q_cols)), low),
+            jax.ShapeDtypeStruct((chip_part, wide_cols), low),
+        ],
+        in_specs=[vmem, vmem, vmem, vmem, any_space, any_space, vmem, vmem],
+        out_specs=[vmem, vmem, vmem, vmem, vmem, any_space],
+        scratch_shapes=[
+            pltpu.VMEM((part, 2 * ff), low),
+            pltpu.VMEM((part, lanes(q_cols)), low),
+            dma((2,)),
+            dma((2, 8)),
+            dma((2, 2)),
+            dma((2, 2)),
+            dma((2, 2)),
+            dma((3, groups)),
+            dma((2, 3, groups)),
+            dma((2,)),
+            dma((2,)),
+        ],
+        name="start",
+        cost_estimate=pl.CostEstimate(flops=0, bytes_accessed=100_000_000, transcendentals=0),
+        compiler_params=pltpu.CompilerParams(
+            collective_id=1, has_side_effects=True, vmem_limit_bytes=32 * 2**20
+        ),
+    )(hidden_in[0], gains, qkv_half(core), qkv_half(1 - core), w_gate, w_up, w_down, w_output)
+    gains_rel = (gains_all[0::2] + gains_all[1::2])[:, :2]
+    gain_one, gain_two = (gains_rel[:, row].reshape(1, width) for row in range(2))
+    out_w = gather(out_own)
 
     length = lengths[0]
-    inputs = relative(hidden_in[0]).astype(f32)
-    h1_mine = normed(inputs, gain_one).astype(low)
-    h1 = both(h1_mine, over_core(h1_mine), 0)
-    slots = (y_at * 2) * rows + jnp.arange(2 * rows, dtype=jnp.int32)
+    hidden_own = lax.dynamic_slice_in_dim(hidden_in[0], z_at * owned, owned, axis=0)
+    inputs_own = relative(hidden_own).astype(f32)
+    slots = (y_at * 2) * rows + jnp.arange(chip_rows, dtype=jnp.int32)
     my_slots = ctx_at * rows + jnp.arange(rows, dtype=jnp.int32)
     valid = (my_slots < length).astype(f32)[:, None]
     dout = valid * relative(cotangent[0]).astype(f32)
     dm_mine = dout.astype(low)
     dm = both(dm_mine, over_core(dm_mine), 0)
+    dout_own = lax.dynamic_slice_in_dim(dout, z_at * owned, owned, axis=0)
+    valid_own = lax.dynamic_slice_in_dim(valid, z_at * owned, owned, axis=0)
     cosine, sine = rope_tables(slots.astype(f32), HEAD)
 
-    qkv = sum(matmul(cut(h1, turn), qkv_w[turn], nn) for turn in (0, 2, 1, 3))
-    heads = w_query.shape[1] // HEAD // 2
-    kv_heads = w_key.shape[1] // HEAD // 2
-    group = heads // kv_heads
-    q_cols, k_cols = heads * HEAD, kv_heads * HEAD
-    chip_rows = 2 * rows
     q_low = rotate(qkv[:, :q_cols].reshape(chip_rows, heads, HEAD), cosine, sine).astype(low)
     k_low = rotate(
         qkv[:, q_cols : q_cols + k_cols].reshape(chip_rows, kv_heads, HEAD), cosine, sine
     ).astype(low)
-    v_low = qkv[:, q_cols + k_cols :].astype(low)
+    v_low = qkv[:, q_cols + k_cols : qkv_cols].astype(low)
     kv_mine = jnp.concatenate([k_low.reshape(chip_rows, k_cols), v_low], axis=1)
     kv_other = lax.ppermute(kv_mine, "ctx", Y_SWAP)
     kv_all = jnp.where(
@@ -797,44 +1274,66 @@
     probs_low = probs.astype(low)
     mixed = jnp.einsum("kgbt,tkh->bkgh", probs_low, values, preferred_element_type=f32)
     attn_low = mixed.reshape(chip_rows, q_cols).astype(low)
-    branch = parts(attn_low, out_w, nn)
-    inputs_own = lax.dynamic_slice_in_dim(inputs, z_at * owned, owned, axis=0)
-    whole, half_rows, own = (2 * rows, width), (rows, width), (owned, width)
-    h2, middle = column_call(
-        branch_kernel,
-        [(whole, low), (own, f32)],
-        sum_scratch(owned, z_count, width) + share_scratch(z_count, True),
-        1,
-        "branch_sum",
-    )(branch, inputs_own, gain_two[None])
-
-    ff = gu_w[0].shape[1] // 2
-    gu = sum(matmul(cut(h2, turn), gu_w[turn], nn) for turn in (0, 2, 1, 3))
-    gate, up = gu[:, :ff], gu[:, ff:]
-    sigma = jax.nn.sigmoid(gate)
-    hidden = (gate * sigma * up).astype(low)
-    d_hidden = sum(matmul(cut(dm, turn), down_w[turn], nt) for turn in (0, 2, 1, 3))
-    d_gate = (d_hidden * up * sigma * (1.0 + gate * (1.0 - sigma))).astype(low)
-    d_up = (d_hidden * gate * sigma).astype(low)
-    d_gu = jnp.concatenate([d_gate, d_up], axis=1)
-    dh2 = parts(d_gu, gu_w, nt)
-    grad_gu = scatter([matmul(cut(h2, turn), d_gu, tn) for turn in range(4)])
-    grad_down = scatter([matmul(hidden, cut(dm, turn), tn) for turn in range(4)])
-    mlp = parts(hidden, down_w, nn)
-    dout_own = lax.dynamic_slice_in_dim(dout, z_at * owned, owned, axis=0)
-    valid_own = lax.dynamic_slice_in_dim(valid, z_at * owned, owned, axis=0)
-    da, d_middle, layer_own, gain_two_part = column_call(
-        middle_kernel,
-        [(whole, low), (own, f32), (own, low), ((1, width), f32)],
-        [pltpu.VMEM(own, f32)]
-        + sum_scratch(owned, z_count, width) * 2
-        + share_scratch(z_count, True),
-        2,
-        "middle_sum",
-    )(dh2, mlp, middle, gain_two[None], dout_own, valid_own)
-
-    do = sum(matmul(cut(da, turn), out_w[turn], nt) for turn in range(4)).astype(low)
-    grad_out = scatter([matmul(attn_low, cut(da, turn), tn) for turn in range(4)])
+    out_w = [block[:, :q_cols] for block in out_w]
+    branch = parts(attn_low, out_w, nt)
+
+    whole, half_rows, own = (chip_rows, width), (rows, width), (owned, width)
+    middle_rows = chip_part // 2
+    hops = z_count - 1
+    vm = pltpu.VMEM
+    outs = [
+        (whole, low, vmem),
+        (own, f32, vmem),
+        (own, low, vmem),
+        ((1, width), f32, vmem),
+        ((chip_part, wide_cols), f32, any_space),
+        ((3, chip_part, wide_cols), low, any_space),
+    ] + [((middle_rows, wide_cols), low, any_space)] * 4
+    da, d_middle, layer_own, gain_two_part, own_grad, stage, upper, lower, x_one, y_two = (
+        pl.pallas_call(
+            mlp_kernel,
+            out_shape=[jax.ShapeDtypeStruct(shape, dtype) for shape, dtype, _ in outs],
+            in_specs=[any_space, vmem, vmem, vmem, vmem, vmem, any_space],
+            out_specs=[spec for _, _, spec in outs],
+            scratch_shapes=[
+                vm((4, chip_part, wide_cols), low),
+                vm(whole, low),
+                vm((width, chip_rows), low),
+                vm((width, chip_rows), low),
+                vm(whole, low),
+                vm(whole, low),
+                vm(whole, f32),
+                vm(own, f32),
+                vm(own, f32),
+                vm((chip_rows, wide_cols), low),
+                vm((3, chip_part, GROUP), low),
+                vm((chip_part, GROUP), f32),
+                dma((2, groups)),
+                dma((2, groups)),
+                dma((2, 2, groups)),
+                dma((4,)),
+                dma((2, 4, groups)),
+            ]
+            + sum_scratch(owned, z_count, width)
+            + share_scratch(z_count, True)
+            + sum_scratch(owned, z_count, width)
+            + sum_scratch(owned, z_count, width)[5:]
+            + share_scratch(z_count, True),
+            name="mlp",
+            cost_estimate=pl.CostEstimate(
+                flops=0, bytes_accessed=600_000_000, transcendentals=0
+            ),
+            compiler_params=pltpu.CompilerParams(
+                collective_id=2, has_side_effects=True, vmem_limit_bytes=63 * 2**20
+            ),
+        )(branch, inputs_own, gain_two, dout_own, valid_own, dm, wide)
+    )
+
+    wide_parts = (own_grad, stage[0], stage[1], stage[2])
+    wide_came = (upper, lower, x_one, y_two)
+    wide_last = scatter_second(wide_parts, wide_came)
+    do = sum(matmul(cut(da, turn), out_w[turn], nn) for turn in range(4)).astype(low)
+    out_parts = [matmul(cut(da, turn), attn_low, tn) for turn in range(4)]
     do_grp = do.reshape(chip_rows, kv_heads, group, HEAD)
     d_probs = jnp.einsum("bkgh,tkh->kgbt", do_grp, values, preferred_element_type=f32)
     inner = jnp.sum(probs * d_probs, axis=-1, keepdims=True)
@@ -858,8 +1357,11 @@
         ],
         axis=1,
     )
-    dh1 = parts(d_qkv, qkv_w, nt)
-    grad_qkv = scatter([matmul(cut(h1, turn), d_qkv, tn) for turn in range(4)])
+    qkv_blocks = [qkv_w[turn, :, :qkv_cols] for turn in range(4)]
+    dh1 = parts(d_qkv, qkv_blocks, nt)
+    qkv_parts = [matmul(cut(h1, turn), d_qkv, tn) for turn in range(4)]
+    out_came = scatter_first(out_parts)
+    qkv_came = scatter_first(qkv_parts)
     out_half, grad_half, gain_one_part = column_call(
         input_kernel,
         [(half_rows, low), (half_rows, low), ((1, width), f32)],
@@ -868,8 +1370,15 @@
         + share_scratch(z_count, False) * 2,
         3,
         "input_sum",
-    )(dh1, layer_own, d_middle, inputs_own, gain_one[None])
-
+    )(dh1, layer_own, d_middle, inputs_own, gain_one)
+    out_half, grad_half, gain_one_part = after(
+        (out_half, grad_half, gain_one_part), (wide_last, out_came, qkv_came)
+    )
+    qkv_last = scatter_second(qkv_parts, qkv_came)
+    out_last = scatter_second(out_parts, out_came)
+    grad_wide = scatter_end(wide_parts, wide_came, wide_last)
+    grad_qkv = scatter_end(qkv_parts, qkv_came, qkv_last)
+    grad_out = scatter_end(out_parts, out_came, out_last)
     gain_part = jnp.concatenate([gain_one_part, gain_two_part], axis=0)
     gain_sum = (
         cut(gain_part, 0)
@@ -887,15 +1396,15 @@
         give = half(total, 1 - core, 0)
         return half(total, core, 0), over_core(give)
 
-    def to_cols(total):
-        give = half(total, 1 - core, 1)
-        return both(half(total, core, 1), over_core(give), 0)
-
-    gu_mine, gu_other = to_rows(grad_gu)
+    wide_mine, wide_other = to_rows(grad_wide)
     qkv_mine, qkv_other = to_rows(grad_qkv)
+    out_mine, out_other = to_rows(grad_out)
 
     def joined(start, size, mine, other):
         return both(mine[:, start : start + size], other[:, start : start + size], 1)
+
+    def kind(total, which):
+        return total.reshape(part, groups, 3, 128)[:, :, which].reshape(part, ff)
 
     return (
         relative(out_half)[None],
@@ -904,11 +1413,11 @@
         joined(0, q_cols, qkv_mine, qkv_other),
         joined(q_cols, k_cols, qkv_mine, qkv_other),
         joined(q_cols + k_cols, k_cols, qkv_mine, qkv_other),
-        to_cols(grad_out),
+        both(out_mine.T, out_other.T, 0),
         gain_mine[1],
-        joined(0, ff, gu_mine, gu_other),
-        joined(ff, ff, gu_mine, gu_other),
-        to_cols(grad_down),
+        both(kind(wide_mine, 0), kind(wide_other, 0), 1),
+        both(kind(wide_mine, 1), kind(wide_other, 1), 1),
+        both(kind(wide_mine, 2).T, kind(wide_other, 2).T, 0),
     )
 
 

time: 625 us -> 563 us (0.901)
  Pallas kernels: 179 us -> 299 us
  waiting for transfers between devices: 180 us -> 61.2 us
  matrix products: 76.9 us -> 35.6 us
  starting transfers between devices: 57.2 us -> 24.5 us
  local copies, waits for them, and re-layouts: 61 us -> 74.5 us
    ppermute x40 -> x18, waiting for transfers between devices: 173 us -> 9.55 us  [send(): got = lax.ppermute(tensor, self.axis, self.pairs)]
    pallas_call x2, Pallas kernels: 115 us -> 235 us  [the longest x1 203 us: on_plane(): pl.pallas_call(mlp_kernel, out_shape=[jax.ShapeDtypeStruct(shape, dtype)...]
    ppermute x1, waiting for transfers between devices: 0.01 us -> 43.4 us  [on_plane(): lax.ppermute(half(dkv, 1 - y_at, 0), 'ctx', Y_SWAP)]
    dot_general x48 -> x20, matrix products: 62.5 us -> 21 us  [matmul(): lax.dot_general(left, right, (dims, ((), ())), preferred_element_type=f32)]
    ppermute x40 -> x18, starting transfers between devices: 44.3 us -> 17.5 us  [send(): got = lax.ppermute(tensor, self.axis, self.pairs)]
    another operation x2 -> x9, local copies, waits for them, and re-layouts: 0.01 us -> 15.4 us  [the longest x6 14 us: kind(): return total.reshape(part, groups, 3, 128)[:, :, which].reshape(part, ff)]
    select_n x14 -> x8, other arithmetic: 25.1 us -> 12.1 us  [both(): jnp.where(first, jnp.concatenate([mine, other], axis=axis), jnp.concatena...]
    unnamed x180 -> x135, local copies, waits for them, and re-layouts: 16.4 us -> 17.2 us
  transfers between devices with their start and end apart: 63 -> 31, of which waited for: 19 -> 8; matrix products, arithmetic and copies ran while one was open for 22% -> 18% of each run, Pallas kernels for 19% -> 12%
where the time goes in v3:
time: 563 us; the launch traced here: 553 us
  Pallas kernels  299 us (53%)
  local copies, waits for them, and re-layouts  74.5 us (13%)
  waiting for transfers between devices  61.2 us (11%)
  other arithmetic  54.9 us (10%)
  matrix products  35.6 us (6%)
  starting transfers between devices  24.5 us (4%)
    pallas_call x1, Pallas kernels, on_plane(): pl.pallas_call(mlp_kernel, out_shape=[jax.ShapeDtypeStruct(shape, dtype)...  203 us
    pallas_call x1, Pallas kernels, on_plane(): column_call(input_kernel, [(half_rows, low), (half_rows, low), ((1, width...  64 us
    ppermute x1, waiting for transfers between devices, on_plane(): lax.ppermute(half(dkv, 1 - y_at, 0), 'ctx', Y_SWAP)  43.4 us
    pallas_call x1, Pallas kernels, on_plane(): pl.pallas_call(start_kernel, out_shape=[jax.ShapeDtypeStruct((chip_rows,...  31.9 us
    dot_general x20, matrix products, matmul(): lax.dot_general(left, right, (dims, ((), ())), preferred_element_type=f32)  21 us
    ppermute x18, starting transfers between devices, send(): got = lax.ppermute(tensor, self.axis, self.pairs)  17.5 us
    unnamed x135, local copies, waits for them, and re-layouts  17.2 us
    another operation x6, local copies, waits for them, and re-layouts, kind(): return total.reshape(part, groups, 3, 128)[:, :, which].reshape(part, ff)  14 us
  transfers between devices with their start and end apart: 31, of which 8 were waited for; matrix products, arithmetic and copies ran while one was open for 18% of the time, Pallas kernels for 12%

profile of v3, /device:TPU:0, one launch (start us, length us, event | category | flops | bytes accessed | tf_op | source)
XLA Modules:
  0.0 552.7 jit_solution(1866428567732862992)
XLA Ops:
  3.5 2.0 copy.114.output
  5.5 1.9 copy.113.down
  11.0 31.9 %start.1 = (f32[512,512]{1,0:T(8,128)S(1)}, bf16[512,2560]{1,0:T(8,128)(2,1)S(1)}, bf16[4,640,512]{2,1,0:T(8,128)(2,1)S(1)}, f32[8,8,640]{2,1,0:T(8,128)S(1)}, b...) custom-call(bf16[256,2560]{1,0:T(8,128)(2,1)S(1)} %bitcast.176, f32[8,640]{1,0:T(8,128)S(1)} %dynamic_update_slice.3.gains, ...), custom_call_target="tpu_custom_call" | custom-call | bytes 100000000 | tf_op jit(solution)/shard_map/start/pallas_call | solution.py:1204
  42.9 1.8 copy-done.1
  45.7 1.5 copy-done.10
  51.8 2.2 fusion.113
  57.2 1.5 collective-permute-start
  60.8 2.0 constant_dynamic-slice_fusion.10.dout
  69.0 1.6 fusion.5
  70.6 1.8 fusion.4
  72.5 2.9 fusion.25
  78.3 1.8 collective-permute-start.4
  80.1 1.6 convolution_convert_fusion.5
  81.8 1.6 convolution_convert_fusion.6
  84.2 1.6 collective-permute-done.4
  87.1 1.7 pad_maximum_fusion.branch
  88.8 3.9 maximum_select_fusion.dm
  92.7 203.1 %mlp.1 = (bf16[512,2560]{1,0:T(8,128)(2,1)}, f32[64,2560]{1,0:T(8,128)}, bf16[64,2560]{1,0:T(8,128)(2,1)}, f32[1,2560]{1,0:T(1,128)}, f32[640,2688]{1,0:T(8,128)...) custom-call(bf16[512,2560]{1,0:T(8,128)(2,1)} %pad_maximum_fusion.br, ...), custom_call_target="tpu_custom_call" | custom-call | bytes 600000000 | tf_op jit(solution)/shard_map/mlp/pallas_call | solution.py:1293
  295.8 1.7 fusion.61
  297.6 2.3 convolution_convert_fusion.9
  301.2 1.6 fusion.57
  302.8 1.7 fusion.24
  304.5 4.8 fusion.19
  309.4 3.2 fusion
  312.6 2.9 fusion.6
  321.5 4.7 fusion.13
  333.3 43.4 %collective-permute-done.6 = f32[512,160]{1,0:T(8,128)S(1)} collective-permute-done((f32[512,160]{1,0:T(8,128)S(1)}, f32[512,160]{1,0:T(8,128)S(1)}, u32[]{:S(2)}, u32[]{:S(2)}) %collective-permute-start.6) | collective-permute-done | bytes 327712 | tf_op jit(solution)/shard_map/ppermute | solution.py:1347
  379.2 1.5 convolution_convert_fusion.2
  387.4 1.6 fusion.38
  390.7 64.0 %input_sum.1 = (bf16[256,2560]{1,0:T(8,128)(2,1)S(1)}, bf16[256,2560]{1,0:T(8,128)(2,1)S(1)}, f32[1,2560]{1,0:T(1,128)S(1)}) custom-call(bf16[512,2560]{1,0:T(8,128)(2,1)S(1)} %pad_maximum_fusion.1.part, bf16[64,2560]{1,0:T(8,128)(2,1)S(1)} %copy-done.9, f32[64,2560]{1,0:T(8,128)S(1)} %copy-done.8, f32[64,2560]{1,0:T(8,128)S(1)} %copy-done, ...), custom_call_target="tpu_custom_call" | custom-call | bytes 150000000 | tf_op jit(solution)/shard_map/input_sum/pallas_call | solution.py:1365
  460.7 4.9 convert_add_fusion.2
  465.6 5.2 fusion.12
  470.7 5.4 copy.134
  478.1 4.2 fusion.114
  482.4 2.8 copy.164
  485.2 2.8 copy.162
  487.9 2.9 copy.160
  497.7 1.9 collective-permute-done.19
  500.6 1.7 fusion.29
  504.4 2.2 copy.130
  508.0 7.1 %collective-permute-done.28 = bf16[320,320]{0,1:T(8,128)(2,1)S(1)} collective-permute-done((bf16[320,320]{0,1:T(8,128)(2,1)S(1)}, bf16[320,320]{0,1:T(8,128)(2,1)S(1)}, u32[]{:S(2)}, u32[]{:S(2)}) %collective-permute-start.28) | collective-permute-done | bytes 204832 | tf_op jit(solution)/shard_map/ppermute | solution.py:1076
  518.5 4.4 collective-permute-done.23
  530.3 5.4 copy.136
  535.6 3.6 fusion.115
  539.2 2.8 copy.141
  544.8 3.4 maximum_select_fusion.3
  548.2 1.6 maximum_select_fusion.2
  550.6 1.6 maximum_select_fusion.1
  (280 shorter events, 86.2 us)
Async XLA Ops:
  48.6 27.4 %collective-permute-start.2 = (bf16[640,384]{1,0:T(8,128)(2,1)S(1)}, bf16[640,384]{1,0:T(8,128)(2,1)}, u32[]{:S(2)}, u32[]{:S(2)}) collective-permute-start(bf16[640,384]{1,0:T(8,128)(2,1)S(1)} %get-tuple-element.48), channel_id=1, source_target_pairs={{0,16},{16,0},{1,17},{17,1},{2,18},{18,2},{3,19},{19,3},{4,20},{20... | collective-permute-start | bytes 1474568 | tf_op jit(solution)/shard_map/ppermute | solution.py:1076
  49.2 28.2 %collective-permute-start.1 = (bf16[640,384]{1,0:T(8,128)(2,1)S(1)}, bf16[640,384]{1,0:T(8,128)(2,1)}, u32[]{:S(2)}, u32[]{:S(2)}) collective-permute-start(bf16[640,384]{1,0:T(8,128)(2,1)S(1)} %get-tuple-element.48), channel_id=1, source_target_pairs={{0,8},{4,12},{8,0},{12,4},{1,9},{5,13},{9,1},{13,5},{2,10},{6,14},... | collective-permute-start | bytes 1474568 | tf_op jit(solution)/shard_map/ppermute | solution.py:1076
  54.1 34.7 %collective-permute-start.5 = (bf16[256,2560]{1,0:T(8,128)(2,1)}, bf16[256,2560]{1,0:T(8,128)(2,1)}, u32[]{:S(2)}, u32[]{:S(2)}) collective-permute-start(bf16[256,2560]{1,0:T(8,128)(2,1)} %get-tuple-element.143), channel_id=1, source_target_pairs={{0,4},{4,0},{8,12},{12,8},{1,5},{5,1},{9,13},{13,9},{2,6},{6,2},{1... | collective-permute-start | bytes 3932168 | tf_op jit(solution)/shard_map/ppermute | solution.py:1066
  54.1 8.7 %copy-start.54 = (f32[40]{0:T(128)}, f32[40]{0:T(128)S(1)}, u32[]{:S(2)}) copy-start(f32[40]{0:T(128)S(1)} %negate_power_fusion) | copy-start | bytes 484
  54.4 9.9 %copy-start.52 = (f32[512]{0:T(512)}, f32[512]{0:T(512)S(1)}, u32[]{:S(2)}) copy-start(f32[512]{0:T(512)S(1)} %fusion.106) | copy-start | bytes 6148
  57.2 10.3 %collective-permute-start = (bf16[512,160]{1,0:T(8,128)(2,1)}, bf16[512,160]{1,0:T(8,128)(2,1)}, u32[]{:S(2)}, u32[]{:S(2)}) collective-permute-start(bf16[512,160]{1,0:T(8,128)(2,1)} %pad_maximum_fusion.8), channel_id=1, source_target_pairs={{0,8},{4,12},{8,0},{12,4},{1,9},{5,13},{9,1},{13,5},{2,10},{6,14},... | collective-permute-start | bytes 491528 | tf_op jit(solution)/shard_map/ppermute | solution.py:1258
  64.6 7.8 %copy-start.16 = (pred[512,1024]{0,1:T(8,128)(4,1)}, pred[512,1024]{0,1:T(8,128)(4,1)S(1)}, u32[]{:S(2)}) copy-start(pred[512,1024]{0,1:T(8,128)(4,1)S(1)} %fusion.16) | copy-start | bytes 1572868
  77.0 7.2 %collective-permute-start.3 = (bf16[320,384]{1,0:T(8,128)(2,1)S(1)}, bf16[320,384]{1,0:T(8,128)(2,1)S(1)}, u32[]{:S(2)}, u32[]{:S(2)}) collective-permute-start(bf16[320,384]{1,0:T(8,128)(2,1)S(1)} %slice.332), channel_id=1, source_target_pairs={{0,8},{4,12},{8,0},{12,4},{1,9},{5,13},{9,1},{13,5},{2,10},{6,14},... | collective-permute-start | bytes 737288 | tf_op jit(solution)/shard_map/ppermute | solution.py:1076
  78.3 7.5 %collective-permute-start.4 = (bf16[320,384]{1,0:T(8,128)(2,1)S(1)}, bf16[320,384]{1,0:T(8,128)(2,1)S(1)}, u32[]{:S(2)}, u32[]{:S(2)}) collective-permute-start(bf16[320,384]{1,0:T(8,128)(2,1)S(1)} %slice.333), channel_id=1, source_target_pairs={{0,16},{16,0},{1,17},{17,1},{2,18},{18,2},{3,19},{19,3},{4,20},{20... | collective-permute-start | bytes 737288 | tf_op jit(solution)/shard_map/ppermute | solution.py:1076
  302.8 6.5 %slice-start = ((s8[8388608]{0:T(1024)(128)(4,1)}), s8[4194304]{0:T(1024)(128)(4,1)S(1)}, s32[]{:S(2)}) async-start(s8[8388608]{0:T(1024)(128)(4,1)} %bitcast.178), calls=%async_computation | async-start | bytes 8388608
  317.9 13.8 %collective-permute-start.9 = (bf16[320,320]{0,1:T(8,128)(2,1)S(1)}, bf16[320,320]{0,1:T(8,128)(2,1)S(1)}, u32[]{:S(2)}, u32[]{:S(2)}) collective-permute-start(bf16[320,320]{0,1:T(8,128)(2,1)S(1)} %get-tuple-element.63), channel_id=1, source_target_pairs={{0,16},{16,0},{1,17},{17,1},{2,18},{18,2},{3,19},{19,3},{4,20},{20... | collective-permute-start | bytes 614408 | tf_op jit(solution)/shard_map/ppermute | solution.py:1076
  318.9 13.5 %collective-permute-start.10 = (bf16[320,320]{0,1:T(8,128)(2,1)S(1)}, bf16[320,320]{0,1:T(8,128)(2,1)S(1)}, u32[]{:S(2)}, u32[]{:S(2)}) collective-permute-start(bf16[320,320]{0,1:T(8,128)(2,1)S(1)} %get-tuple-element.64), channel_id=1, source_target_pairs={{0,8},{4,12},{8,0},{12,4},{1,9},{5,13},{9,1},{13,5},{2,10},{6,14},... | collective-permute-start | bytes 614408 | tf_op jit(solution)/shard_map/ppermute | solution.py:1076
  321.5 6.7 %copy-start.40 = (f32[512,40]{0,1:T(8,128)S(1)}, f32[512,40]{0,1:T(8,128)}, u32[]{:S(2)}) copy-start(f32[512,40]{0,1:T(8,128)} %copy-done.39) | copy-start | bytes 245764
  321.5 6.7 %copy-start.42 = (f32[512,40]{0,1:T(8,128)S(1)}, f32[512,40]{0,1:T(8,128)}, u32[]{:S(2)}) copy-start(f32[512,40]{0,1:T(8,128)} %copy-done.41) | copy-start | bytes 245764
  326.2 132.5 %collective-permute-start.7 = (bf16[320,2688]{1,0:T(8,128)(2,1)}, bf16[320,2688]{1,0:T(8,128)(2,1)}, u32[]{:S(2)}, u32[]{:S(2)}) collective-permute-start(bf16[320,2688]{1,0:T(8,128)(2,1)} %get-tuple-element.60), channel_id=1, source_target_pairs={{0,8},{4,12},{8,0},{12,4},{1,9},{5,13},{9,1},{13,5},{2,10},{6,14},... | collective-permute-start | bytes 5160968 | tf_op jit(solution)/shard_map/ppermute | solution.py:1076
  327.1 132.5 %collective-permute-start.8 = (bf16[320,2688]{1,0:T(8,128)(2,1)}, bf16[320,2688]{1,0:T(8,128)(2,1)}, u32[]{:S(2)}, u32[]{:S(2)}) collective-permute-start(bf16[320,2688]{1,0:T(8,128)(2,1)} %get-tuple-element.62), channel_id=1, source_target_pairs={{0,16},{16,0},{1,17},{17,1},{2,18},{18,2},{3,19},{19,3},{4,20},{20... | collective-permute-start | bytes 5160968 | tf_op jit(solution)/shard_map/ppermute | solution.py:1076
  328.6 48.1 %collective-permute-start.6 = (f32[512,160]{1,0:T(8,128)S(1)}, f32[512,160]{1,0:T(8,128)S(1)}, u32[]{:S(2)}, u32[]{:S(2)}) collective-permute-start(f32[512,160]{1,0:T(8,128)S(1)} %fusion.63), channel_id=1, source_target_pairs={{0,8},{4,12},{8,0},{12,4},{1,9},{5,13},{9,1},{13,5},{2,10},{6,14},... | collective-permute-start | bytes 983048 | tf_op jit(solution)/shard_map/ppermute | solution.py:1347
  331.6 46.1 %copy-start.53 = (f32[512]{0:T(512)S(1)}, f32[512]{0:T(512)}, u32[]{:S(2)}) copy-start(f32[512]{0:T(512)} %copy-done.52) | copy-start | bytes 6148
  331.6 46.1 %copy-start.55 = (f32[40]{0:T(128)S(1)}, f32[40]{0:T(128)}, u32[]{:S(2)}) copy-start(f32[40]{0:T(128)} %copy-done.54) | copy-start | bytes 484
  332.4 46.8 %copy-start.13 = (bf16[4,640,512]{2,1,0:T(8,128)(2,1)S(1)}, bf16[4,640,512]{2,1,0:T(8,128)(2,1)}, u32[]{:S(2)}) copy-start(bf16[4,640,512]{2,1,0:T(8,128)(2,1)} %copy-done.12) | copy-start | bytes 7864324
  332.4 46.8 %copy-start.48 = (bf16[512,4,80]{0,2,1:T(8,128)(2,1)S(1)}, bf16[512,4,80]{0,2,1:T(8,128)(2,1)}, u32[]{:S(2)}) copy-start(bf16[512,4,80]{0,2,1:T(8,128)(2,1)} %pad_maximum_fusion.5) | copy-start | bytes 983044
  383.8 71.0 %collective-permute-start.13 = (bf16[320,480]{0,1:T(8,128)(2,1)S(1)}, bf16[320,480]{0,1:T(8,128)(2,1)S(1)}, u32[]{:S(2)}, u32[]{:S(2)}) collective-permute-start(bf16[320,480]{0,1:T(8,128)(2,1)S(1)} %get-tuple-element.68), channel_id=1, source_target_pairs={{0,16},{16,0},{1,17},{17,1},{2,18},{18,2},{3,19},{19,3},{4,20},{20... | collective-permute-start | bytes 921608 | tf_op jit(solution)/shard_map/ppermute | solution.py:1076
  386.3 69.3 %collective-permute-start.14 = (bf16[320,480]{0,1:T(8,128)(2,1)S(1)}, bf16[320,480]{0,1:T(8,128)(2,1)S(1)}, u32[]{:S(2)}, u32[]{:S(2)}) collective-permute-start(bf16[320,480]{0,1:T(8,128)(2,1)S(1)} %get-tuple-element.69), channel_id=1, source_target_pairs={{0,8},{4,12},{8,0},{12,4},{1,9},{5,13},{9,1},{13,5},{2,10},{6,14},... | collective-permute-start | bytes 921608 | tf_op jit(solution)/shard_map/ppermute | solution.py:1076
  390.7 70.0 %copy-start.25 = (bf16[320,2688]{1,0:T(8,128)(2,1)S(1)}, bf16[320,2688]{1,0:T(8,128)(2,1)}, u32[]{:S(2)}) copy-start(bf16[320,2688]{1,0:T(8,128)(2,1)} %get-tuple-element.81) | copy-start | bytes 5160964
  390.7 70.0 %copy-start.26 = (bf16[320,2688]{1,0:T(8,128)(2,1)S(1)}, bf16[320,2688]{1,0:T(8,128)(2,1)}, u32[]{:S(2)}) copy-start(bf16[320,2688]{1,0:T(8,128)(2,1)} %get-tuple-element.82) | copy-start | bytes 5160964
  455.6 38.6 %collective-permute-start.24 = (bf16[320,480]{0,1:T(8,128)(2,1)}, bf16[320,480]{0,1:T(8,128)(2,1)S(1)}, u32[]{:S(2)}, u32[]{:S(2)}) collective-permute-start(bf16[320,480]{0,1:T(8,128)(2,1)} %fusion.32), channel_id=1, source_target_pairs={{0,8},{4,12},{8,0},{12,4},{1,9},{5,13},{9,1},{13,5},{2,10},{6,14},... | collective-permute-start | bytes 921608 | tf_op jit(solution)/shard_map/ppermute | solution.py:1076
  457.6 37.6 %collective-permute-start.25 = (bf16[320,480]{0,1:T(8,128)(2,1)}, bf16[320,480]{0,1:T(8,128)(2,1)S(1)}, u32[]{:S(2)}, u32[]{:S(2)}) collective-permute-start(bf16[320,480]{0,1:T(8,128)(2,1)} %fusion.30), channel_id=1, source_target_pairs={{0,16},{16,0},{1,17},{17,1},{2,18},{18,2},{3,19},{19,3},{4,20},{20... | collective-permute-start | bytes 921608 | tf_op jit(solution)/shard_map/ppermute | solution.py:1076
  458.7 17.4 %collective-permute-start.12 = (bf16[320,320]{0,1:T(8,128)(2,1)}, bf16[320,320]{0,1:T(8,128)(2,1)}, u32[]{:S(2)}, u32[]{:S(2)}) collective-permute-start(bf16[320,320]{0,1:T(8,128)(2,1)} %slice.536), channel_id=1, source_target_pairs={{0,8},{4,12},{8,0},{12,4},{1,9},{5,13},{9,1},{13,5},{2,10},{6,14},... | collective-permute-start | bytes 614408 | tf_op jit(solution)/shard_map/ppermute | solution.py:1076
  459.6 17.5 %collective-permute-start.11 = (bf16[320,320]{0,1:T(8,128)(2,1)}, bf16[320,320]{0,1:T(8,128)(2,1)}, u32[]{:S(2)}, u32[]{:S(2)}) collective-permute-start(bf16[320,320]{0,1:T(8,128)(2,1)} %slice.537), channel_id=1, source_target_pairs={{0,16},{16,0},{1,17},{17,1},{2,18},{18,2},{3,19},{19,3},{4,20},{20... | collective-permute-start | bytes 614408 | tf_op jit(solution)/shard_map/ppermute | solution.py:1076
  476.1 14.7 %collective-permute-start.16 = (bf16[320,480]{0,1:T(8,128)(2,1)}, bf16[320,480]{0,1:T(8,128)(2,1)}, u32[]{:S(2)}, u32[]{:S(2)}) collective-permute-start(bf16[320,480]{0,1:T(8,128)(2,1)} %slice.534), channel_id=1, source_target_pairs={{0,8},{4,12},{8,0},{12,4},{1,9},{5,13},{9,1},{13,5},{2,10},{6,14},... | collective-permute-start | bytes 921608 | tf_op jit(solution)/shard_map/ppermute | solution.py:1076
  477.0 14.7 %collective-permute-start.15 = (bf16[320,480]{0,1:T(8,128)(2,1)}, bf16[320,480]{0,1:T(8,128)(2,1)}, u32[]{:S(2)}, u32[]{:S(2)}) collective-permute-start(bf16[320,480]{0,1:T(8,128)(2,1)} %slice.535), channel_id=1, source_target_pairs={{0,16},{16,0},{1,17},{17,1},{2,18},{18,2},{3,19},{19,3},{4,20},{20... | collective-permute-start | bytes 921608 | tf_op jit(solution)/shard_map/ppermute | solution.py:1076
  490.8 39.5 %collective-permute-start.30 = (f32[320,2688]{1,0:T(8,128)}, f32[320,2688]{1,0:T(8,128)}, u32[]{:S(2)}, u32[]{:S(2)}) collective-permute-start(f32[320,2688]{1,0:T(8,128)} %get-tuple-element.132), channel_id=1, source_target_pairs={{0,4},{4,0},{8,12},{12,8},{1,5},{5,1},{9,13},{13,9},{2,6},{6,2},{1... | collective-permute-start | bytes 10321928 | tf_op jit(solution)/shard_map/ppermute | solution.py:1066
  490.8 17.2 %collective-permute-start.27 = (bf16[320,320]{0,1:T(8,128)(2,1)}, bf16[320,320]{0,1:T(8,128)(2,1)}, u32[]{:S(2)}, u32[]{:S(2)}) collective-permute-start(bf16[320,320]{0,1:T(8,128)(2,1)} %fusion.71), channel_id=1, source_target_pairs={{0,8},{4,12},{8,0},{12,4},{1,9},{5,13},{9,1},{13,5},{2,10},{6,14},... | collective-permute-start | bytes 614408 | tf_op jit(solution)/shard_map/ppermute | solution.py:1076
  491.9 10.4 %collective-permute-start.17 = (f32[2,640]{1,0:T(2,128)S(1)}, f32[2,640]{1,0:T(2,128)S(1)}, u32[]{:S(2)}, u32[]{:S(2)}) collective-permute-start(f32[2,640]{1,0:T(2,128)S(1)} %get-tuple-element.191), channel_id=1, source_target_pairs={{0,8},{4,12},{8,0},{12,4},{1,9},{5,13},{9,1},{13,5},{2,10},{6,14},... | collective-permute-start | bytes 15368 | tf_op jit(solution)/shard_map/ppermute | solution.py:1385
  494.2 5.4 collective-permute-start.19
  495.2 7.1 %collective-permute-start.18 = (f32[2,640]{1,0:T(2,128)S(1)}, f32[2,640]{1,0:T(2,128)S(1)}, u32[]{:S(2)}, u32[]{:S(2)}) collective-permute-start(f32[2,640]{1,0:T(2,128)S(1)} %get-tuple-element.193), channel_id=1, source_target_pairs={{0,16},{16,0},{1,17},{17,1},{2,18},{18,2},{3,19},{19,3},{4,20},{20... | collective-permute-start | bytes 15368 | tf_op jit(solution)/shard_map/ppermute | solution.py:1386
  499.6 3.6 collective-permute-start.20
  502.3 12.8 %copy-start.23 = (f32[640,320]{0,1:T(8,128)S(1)}, f32[640,320]{0,1:T(8,128)}, u32[]{:S(2)}) copy-start(f32[640,320]{0,1:T(8,128)} %fusion.59) | copy-start | bytes 2457604
  503.3 4.6 collective-permute-start.21
  506.7 10.5 %copy-start.29 = (bf16[256,640]{1,0:T(8,128)(2,1)S(1)}, bf16[256,640]{1,0:T(8,128)(2,1)}, u32[]{:S(2)}) copy-start(bf16[256,640]{1,0:T(8,128)(2,1)} %get-tuple-element.149) | copy-start | bytes 983044
  506.7 10.6 %copy-start.30 = (bf16[256,640]{1,0:T(8,128)(2,1)S(1)}, bf16[256,640]{1,0:T(8,128)(2,1)}, u32[]{:S(2)}) copy-start(bf16[256,640]{1,0:T(8,128)(2,1)} %get-tuple-element.150) | copy-start | bytes 983044
  506.7 10.6 %copy-start.31 = (bf16[256,640]{1,0:T(8,128)(2,1)S(1)}, bf16[256,640]{1,0:T(8,128)(2,1)}, u32[]{:S(2)}) copy-start(bf16[256,640]{1,0:T(8,128)(2,1)} %get-tuple-element.151) | copy-start | bytes 983044
  506.7 10.6 %copy-start.32 = (bf16[256,640]{1,0:T(8,128)(2,1)S(1)}, bf16[256,640]{1,0:T(8,128)(2,1)}, u32[]{:S(2)}) copy-start(bf16[256,640]{1,0:T(8,128)(2,1)} %get-tuple-element.152) | copy-start | bytes 983044
  506.7 8.4 %collective-permute-start.28 = (bf16[320,320]{0,1:T(8,128)(2,1)S(1)}, bf16[320,320]{0,1:T(8,128)(2,1)S(1)}, u32[]{:S(2)}, u32[]{:S(2)}) collective-permute-start(bf16[320,320]{0,1:T(8,128)(2,1)S(1)} %copy-done.49), channel_id=1, source_target_pairs={{0,16},{16,0},{1,17},{17,1},{2,18},{18,2},{3,19},{19,3},{4,20},{20... | collective-permute-start | bytes 614408 | tf_op jit(solution)/shard_map/ppermute | solution.py:1076
  507.7 17.1 %collective-permute-start.26 = (f32[320,480]{1,0:T(8,128)}, f32[320,480]{1,0:T(8,128)}, u32[]{:S(2)}, u32[]{:S(2)}) collective-permute-start(f32[320,480]{1,0:T(8,128)} %copy.130), channel_id=1, source_target_pairs={{0,4},{4,0},{8,12},{12,8},{1,5},{5,1},{9,13},{13,9},{2,6},{6,2},{1... | collective-permute-start | bytes 1843208 | tf_op jit(solution)/shard_map/ppermute | solution.py:1066
  508.0 10.4 %collective-permute-start.22 = (f32[2,320]{1,0:T(2,128)S(1)}, f32[2,320]{1,0:T(2,128)S(1)}, u32[]{:S(2)}, u32[]{:S(2)}) collective-permute-start(f32[2,320]{1,0:T(2,128)S(1)} %fusion.105), channel_id=1, source_target_pairs={{0,1},{1,0},{2,3},{3,2},{4,5},{5,4},{6,7},{7,6},{8,9},{9,8},{10,11... | collective-permute-start | bytes 7688 | tf_op jit(solution)/shard_map/ppermute | solution.py:1391
  517.1 6.4 %collective-permute-start.29 = (f32[320,320]{0,1:T(8,128)S(1)}, f32[320,320]{0,1:T(8,128)S(1)}, u32[]{:S(2)}, u32[]{:S(2)}) collective-permute-start(f32[320,320]{0,1:T(8,128)S(1)} %get-tuple-element.164), channel_id=1, source_target_pairs={{0,4},{4,0},{8,12},{12,8},{1,5},{5,1},{9,13},{13,9},{2,6},{6,2},{1... | collective-permute-start | bytes 1228808 | tf_op jit(solution)/shard_map/ppermute | solution.py:1066
  518.4 4.5 collective-permute-start.23
  (45 other events, 139.7 us)
